TPU v7x, 32 devices: a whole 2x2x4 slice. The times are simulated.
32 devices in a mesh: fsdp: 4 (over y, x), ctx: 2 (over core), tp: 4 (over z).
Axes of the slice: x: 2, y: 2, z: 4, core: 2. Of those that a mesh axis runs over, the one named last changes fastest.
Arguments:
- tokens: bfloat16 [12, 640, 1024], P('fsdp', 'ctx')
- lengths: int32 [12, 2], P('fsdp'), may hold values from 257 to 320, as said below
- image_count: int32 [4], P('fsdp'), may hold values from 1 to 3, as said below
- qkv_weight: bfloat16 [2, 1024, 3, 1024], P(None, 'fsdp', None, 'tp')
- qv_bias: bfloat16 [2, 2, 4, 256], P(None, None, 'tp', 'fsdp'), may hold values from -0.59765625 to 0.59765625
- out_weight: bfloat16 [2, 1024, 1024], P(None, 'tp', 'fsdp')
- out_bias: bfloat16 [2, 1024], P(None, 'fsdp'), may hold values from -1.796875 to 1.796875
- up_weight: bfloat16 [2, 1024, 4096], P(None, 'fsdp', 'tp')
- up_bias: bfloat16 [2, 4, 1024], P(None, 'tp', 'fsdp'), may hold values from -1.796875 to 1.796875
- down_weight: bfloat16 [2, 4096, 1024], P(None, 'tp', 'fsdp')
- down_bias: bfloat16 [2, 1024], P(None, 'fsdp'), may hold values from -1.796875 to 1.796875
- gain_one: bfloat16 [2, 1024], P(None, 'fsdp'), may hold values from 0.5 to 1.5
- gain_two: bfloat16 [2, 1024], P(None, 'fsdp'), may hold values from 0.5 to 1.5
- cotangent: bfloat16 [12, 640, 1024], P('fsdp', 'ctx')
Outputs:
- output: bfloat16 [12, 640, 1024], P('fsdp', 'ctx')
- input_grad: bfloat16 [12, 640, 1024], P('fsdp', 'ctx')
- qkv_weight_grad: float32 [2, 1024, 3, 1024], P(None, 'fsdp', None, 'tp')
- qv_bias_grad: float32 [2, 2, 4, 256], P(None, None, 'tp', 'fsdp')
- out_weight_grad: float32 [2, 1024, 1024], P(None, 'tp', 'fsdp')
- out_bias_grad: float32 [2, 1024], P(None, 'fsdp')
- up_weight_grad: float32 [2, 1024, 4096], P(None, 'fsdp', 'tp')
- up_bias_grad: float32 [2, 4, 1024], P(None, 'tp', 'fsdp')
- down_weight_grad: float32 [2, 4096, 1024], P(None, 'tp', 'fsdp')
- down_bias_grad: float32 [2, 1024], P(None, 'fsdp')
- gain_one_grad: float32 [2, 1024], P(None, 'fsdp')
- gain_two_grad: float32 [2, 1024], P(None, 'fsdp')
Inputs may be any that keep to these rules, and one draw needn't show every extreme that they name: `lengths`: in each image one index of ctx, drawn from the seed, holds exactly 320 tokens; the other indices share the remaining 577 - 320 tokens as evenly as possible; each image's counts sum to 577. Slots 0 to image_count - 1 of an fsdp index hold images; some index holds 3.
All inputs are finite; a program needn't handle non-finite values.
Results may differ from a plain program's by a relative error of at most 0.02.
Values may be sent and summed in bfloat16 or wider, within the bound.
No kernel may reach another device: no remote copies, remote signals or barrier semaphores. Data moves between devices by JAX's collectives and lax.ppermute only.
A program may use at most 192 MiB of HBM per device.

v0:
```python
import jax
import jax.numpy as jnp
from jax import lax
from jax.sharding import PartitionSpec as P

HD = 64


def layer_norm(vectors, scaling):
    centre = vectors - jnp.mean(vectors, axis=-1, keepdims=True)
    spread = jnp.mean(centre * centre, axis=-1, keepdims=True)
    return centre * lax.rsqrt(spread + 1e-06) * scaling


def gelu_exact(values):
    return 0.5 * values * (1.0 + lax.erf(values * 0.7071067811865476))


def layer_pieces(layer_index, arrays):
    return tuple((array[layer_index] for array in arrays))


def fetch_weights(pieces):
    return (
        lax.all_gather(pieces[0], "fsdp", axis=0, tiled=True),
        lax.all_gather(pieces[1], "fsdp", axis=2, tiled=True),
        lax.all_gather(pieces[2], "fsdp", axis=1, tiled=True),
        lax.all_gather(pieces[3], "fsdp", axis=0, tiled=True),
        lax.all_gather(pieces[4], "fsdp", axis=0, tiled=True),
        lax.all_gather(pieces[5], "fsdp", axis=1, tiled=True),
        lax.all_gather(pieces[6], "fsdp", axis=1, tiled=True),
        lax.all_gather(pieces[7], "fsdp", axis=0, tiled=True),
        lax.all_gather(pieces[8], "fsdp", axis=0, tiled=True),
        lax.all_gather(pieces[9], "fsdp", axis=0, tiled=True),
    )


def fetch_again(pieces):
    return (
        lax.all_gather(pieces[0], "fsdp", axis=0, tiled=True),
        lax.all_gather(pieces[1], "fsdp", axis=2, tiled=True),
        lax.all_gather(pieces[2], "fsdp", axis=1, tiled=True),
        lax.all_gather(pieces[3], "fsdp", axis=0, tiled=True),
        lax.all_gather(pieces[4], "fsdp", axis=0, tiled=True),
        lax.all_gather(pieces[5], "fsdp", axis=1, tiled=True),
        lax.all_gather(pieces[6], "fsdp", axis=1, tiled=True),
        lax.all_gather(pieces[7], "fsdp", axis=0, tiled=True),
        lax.all_gather(pieces[8], "fsdp", axis=0, tiled=True),
        lax.all_gather(pieces[9], "fsdp", axis=0, tiled=True),
    )


def branch_sum(partial_sum):
    return lax.psum(partial_sum.astype(jnp.bfloat16), "tp").astype(jnp.float32)


def normed_sum(partial_sum):
    return lax.psum(partial_sum.astype(jnp.bfloat16), "tp").astype(jnp.float32)


def reduce_grads(grads):
    scattered = (
        lax.psum_scatter(
            grads[0].astype(jnp.bfloat16), "fsdp", scatter_dimension=1, tiled=True
        ).astype(jnp.float32),
        lax.psum_scatter(
            grads[1].astype(jnp.bfloat16), "fsdp", scatter_dimension=3, tiled=True
        ).astype(jnp.float32),
        lax.psum_scatter(
            grads[2].astype(jnp.bfloat16), "fsdp", scatter_dimension=2, tiled=True
        ).astype(jnp.float32),
        lax.psum_scatter(
            grads[3].astype(jnp.bfloat16), "fsdp", scatter_dimension=1, tiled=True
        ).astype(jnp.float32),
        lax.psum_scatter(
            grads[4].astype(jnp.bfloat16), "fsdp", scatter_dimension=1, tiled=True
        ).astype(jnp.float32),
        lax.psum_scatter(
            grads[5].astype(jnp.bfloat16), "fsdp", scatter_dimension=2, tiled=True
        ).astype(jnp.float32),
        lax.psum_scatter(
            grads[6].astype(jnp.bfloat16), "fsdp", scatter_dimension=2, tiled=True
        ).astype(jnp.float32),
        lax.psum_scatter(
            grads[7].astype(jnp.bfloat16), "fsdp", scatter_dimension=1, tiled=True
        ).astype(jnp.float32),
        lax.psum_scatter(grads[8], "fsdp", scatter_dimension=1, tiled=True).astype(jnp.float32),
        lax.psum_scatter(grads[9], "fsdp", scatter_dimension=1, tiled=True).astype(jnp.float32),
    )
    return (
        lax.psum(scattered[0].astype(jnp.bfloat16), "ctx").astype(jnp.float32),
        lax.psum(scattered[1].astype(jnp.bfloat16), "ctx").astype(jnp.float32),
        lax.psum(scattered[2].astype(jnp.bfloat16), "ctx").astype(jnp.float32),
        lax.psum(scattered[3].astype(jnp.bfloat16), "ctx").astype(jnp.float32),
        lax.psum(scattered[4].astype(jnp.bfloat16), "ctx").astype(jnp.float32),
        lax.psum(scattered[5].astype(jnp.bfloat16), "ctx").astype(jnp.float32),
        lax.psum(scattered[6].astype(jnp.bfloat16), "ctx").astype(jnp.float32),
        lax.psum(scattered[7].astype(jnp.bfloat16), "ctx").astype(jnp.float32),
        lax.psum(scattered[8].astype(jnp.bfloat16), "ctx").astype(jnp.float32),
        lax.psum(scattered[9].astype(jnp.bfloat16), "ctx").astype(jnp.float32),
    )


def masked_scores(queries, all_keys, key_valid):
    scores = jnp.einsum(
        "sqhd,skhd->shqk", queries, all_keys, preferred_element_type=jnp.float32
    ) * HD ** (-0.5)
    return jnp.where(key_valid[:, None, None, :], scores, -1000000000.0)


def forward_layer(stream, weights, key_valid):
    (
        qkv_matrix,
        qv_shift,
        out_matrix,
        out_shift,
        up_matrix,
        up_shift,
        down_matrix,
        down_shift,
        gain_first,
        gain_second,
    ) = weights
    normed = layer_norm(stream, gain_first).astype(jnp.bfloat16)
    slot_count, capacity, features = normed.shape
    project = jnp.einsum("scd,dke->scke", normed, qkv_matrix, preferred_element_type=jnp.float32)
    queries = (project[:, :, 0] + qv_shift[0, 0]).astype(jnp.bfloat16)
    key_local = project[:, :, 1].astype(jnp.bfloat16)
    value_local = (project[:, :, 2] + qv_shift[1, 0]).astype(jnp.bfloat16)
    all_keys, all_values = (
        lax.all_gather(key_local, "ctx", axis=1, tiled=True),
        lax.all_gather(value_local, "ctx", axis=1, tiled=True),
    )
    head_count = queries.shape[-1] // HD
    queries4 = queries.reshape(slot_count, capacity, head_count, HD)
    keys4 = all_keys.reshape(slot_count, -1, head_count, HD)
    values4 = all_values.reshape(slot_count, -1, head_count, HD)
    scores = masked_scores(queries4, keys4, key_valid)
    highest_score = jnp.max(scores, axis=-1, keepdims=True)
    exponent = jnp.exp(scores - highest_score)
    denominator = jnp.sum(exponent, axis=-1, keepdims=True)
    probs = (exponent / denominator).astype(jnp.bfloat16)
    log_total = highest_score + jnp.log(denominator)
    mixed = jnp.einsum(
        "shqk,skhd->sqhd", probs, values4, preferred_element_type=jnp.float32
    ).astype(jnp.bfloat16)
    mixed = mixed.reshape(slot_count, capacity, head_count * HD)
    out_partial = jnp.einsum("sce,ed->scd", mixed, out_matrix, preferred_element_type=jnp.float32)
    branch = branch_sum(out_partial) + out_shift
    middle = stream + branch
    normed_b = layer_norm(middle, gain_second).astype(jnp.bfloat16)
    hidden = (
        jnp.einsum("scd,df->scf", normed_b, up_matrix, preferred_element_type=jnp.float32)
        + up_shift[0]
    )
    active = gelu_exact(hidden).astype(jnp.bfloat16)
    down_partial = jnp.einsum(
        "scf,fd->scd", active, down_matrix, preferred_element_type=jnp.float32
    )
    branch_b = branch_sum(down_partial) + down_shift
    saved_items = (
        stream,
        normed,
        queries4,
        keys4,
        values4,
        log_total,
        mixed,
        middle,
        normed_b,
        hidden,
        active,
    )
    return (middle + branch_b, saved_items)


def backward_layer(gradient, saved_items, weights, key_valid):
    (
        qkv_matrix,
        qv_shift,
        out_matrix,
        out_shift,
        up_matrix,
        up_shift,
        down_matrix,
        down_shift,
        gain_first,
        gain_second,
    ) = weights
    stream, normed, queries4, keys4, values4, log_total, mixed, middle, normed_b, hidden, active = (
        saved_items
    )
    slot_count, capacity, head_count, head_size = queries4.shape
    head_width = head_count * head_size
    grad_low = gradient.astype(jnp.bfloat16)
    delta_down = jnp.einsum("scf,scd->fd", active, grad_low, preferred_element_type=jnp.float32)
    delta_down_shift = jnp.sum(grad_low.astype(jnp.float32), axis=(0, 1))
    delta_active = jnp.einsum(
        "scd,fd->scf", grad_low, down_matrix, preferred_element_type=jnp.float32
    )
    delta_hidden = jax.vjp(gelu_exact, hidden)[1](delta_active)[0].astype(jnp.bfloat16)
    delta_up = jnp.einsum("scd,scf->df", normed_b, delta_hidden, preferred_element_type=jnp.float32)
    delta_up_shift = jnp.sum(delta_hidden.astype(jnp.float32), axis=(0, 1))[None]
    normed_b_partial = jnp.einsum(
        "scf,df->scd", delta_hidden, up_matrix, preferred_element_type=jnp.float32
    )
    delta_normed_b = normed_sum(normed_b_partial)
    back_middle, delta_gain_second = jax.vjp(layer_norm, middle, gain_second)[1](delta_normed_b)
    grad_middle = gradient + back_middle
    grad_attend = grad_middle.astype(jnp.bfloat16)
    delta_out = jnp.einsum("sce,scd->ed", mixed, grad_attend, preferred_element_type=jnp.float32)
    delta_out_shift = jnp.sum(grad_attend.astype(jnp.float32), axis=(0, 1))
    delta_mixed = jnp.einsum(
        "scd,ed->sce", grad_attend, out_matrix, preferred_element_type=jnp.float32
    ).astype(jnp.bfloat16)
    delta_mixed4 = delta_mixed.reshape(slot_count, capacity, head_count, head_size)
    scores = masked_scores(queries4, keys4, key_valid)
    probs = jnp.exp(scores - log_total)
    probs_low = probs.astype(jnp.bfloat16)
    delta_values_all = jnp.einsum(
        "shqk,sqhd->skhd", probs_low, delta_mixed4, preferred_element_type=jnp.float32
    )
    delta_probs = jnp.einsum(
        "sqhd,skhd->shqk", delta_mixed4, values4, preferred_element_type=jnp.float32
    )
    inner_sum = jnp.sum(probs * delta_probs, axis=-1, keepdims=True)
    delta_scores = (probs * (delta_probs - inner_sum)).astype(jnp.bfloat16)
    score_scale = HD ** (-0.5)
    delta_queries = (
        jnp.einsum("shqk,skhd->sqhd", delta_scores, keys4, preferred_element_type=jnp.float32)
        * score_scale
    ).astype(jnp.bfloat16)
    delta_keys_all = (
        jnp.einsum("shqk,sqhd->skhd", delta_scores, queries4, preferred_element_type=jnp.float32)
        * score_scale
    )
    delta_keys, delta_values = (
        lax.psum_scatter(
            delta_keys_all.reshape(slot_count, -1, head_width).astype(jnp.bfloat16),
            "ctx",
            scatter_dimension=1,
            tiled=True,
        ).astype(jnp.float32),
        lax.psum_scatter(
            delta_values_all.reshape(slot_count, -1, head_width).astype(jnp.bfloat16),
            "ctx",
            scatter_dimension=1,
            tiled=True,
        ).astype(jnp.float32),
    )
    delta_queries = delta_queries.reshape(slot_count, capacity, head_width)
    delta_values = delta_values.astype(jnp.bfloat16)
    delta_project = jnp.stack(
        [delta_queries, delta_keys.astype(jnp.bfloat16), delta_values], axis=2
    )
    delta_qkv = jnp.einsum(
        "scd,scke->dke", normed, delta_project, preferred_element_type=jnp.float32
    )
    delta_qv_shift = jnp.stack(
        [
            jnp.sum(delta_queries.astype(jnp.float32), axis=(0, 1)),
            jnp.sum(delta_values.astype(jnp.float32), axis=(0, 1)),
        ]
    )[:, None, :]
    normed_partial = jnp.einsum(
        "scke,dke->scd", delta_project, qkv_matrix, preferred_element_type=jnp.float32
    )
    delta_normed = normed_sum(normed_partial)
    back_stream, delta_gain_first = jax.vjp(layer_norm, stream, gain_first)[1](delta_normed)
    pieces = (
        delta_qkv,
        delta_qv_shift,
        delta_out,
        delta_out_shift,
        delta_up,
        delta_up_shift,
        delta_down,
        delta_down_shift,
        delta_gain_first,
        delta_gain_second,
    )
    return (grad_middle + back_stream, pieces)


def shards(
    tokens,
    lengths,
    image_count,
    qkv_weight,
    qv_bias,
    out_weight,
    out_bias,
    up_weight,
    up_bias,
    down_weight,
    down_bias,
    gain_one,
    gain_two,
    cotangent,
):
    slot_count, capacity, features = tokens.shape
    context_count = lax.axis_size("ctx")
    context_place = lax.axis_index("ctx")
    positions = jnp.arange(capacity)
    own_lengths = lax.dynamic_slice_in_dim(lengths, context_place, 1, 1)[:, 0]
    occupied = jnp.arange(slot_count) < image_count[0]
    row_mask = ((positions[None, :] < own_lengths[:, None]) & occupied[:, None]).astype(
        jnp.float32
    )[:, :, None]
    key_valid = (positions[None, None, :] < lengths[:, :, None]).reshape(
        slot_count, context_count * capacity
    )
    arrays = (
        qkv_weight,
        qv_bias,
        out_weight,
        out_bias,
        up_weight,
        up_bias,
        down_weight,
        down_bias,
        gain_one,
        gain_two,
    )
    layer_total = qkv_weight.shape[0]
    stream = tokens.astype(jnp.float32)
    saved_list = []
    weight_list = []
    for layer_index in range(layer_total):
        weights = fetch_weights(layer_pieces(layer_index, arrays))
        stream, saved_items = forward_layer(stream, weights, key_valid)
        saved_list.append(saved_items)
        weight_list.append(weights)
    gradient = cotangent.astype(jnp.float32) * row_mask
    collected = [None] * layer_total
    for layer_index in reversed(range(layer_total)):
        weights = fetch_again(layer_pieces(layer_index, arrays))
        gradient, pieces = backward_layer(gradient, saved_list[layer_index], weights, key_valid)
        collected[layer_index] = reduce_grads(tuple((element[None] for element in pieces)))
    summed = tuple(
        (
            jnp.concatenate(
                [collected[layer_index][member] for layer_index in range(layer_total)], axis=0
            )
            for member in range(10)
        )
    )
    output = (stream * row_mask).astype(jnp.bfloat16)
    input_grad = gradient.astype(jnp.bfloat16)
    return (output, input_grad) + tuple(summed)


def solution(mesh):
    in_specs = (
        P("fsdp", "ctx", None),
        P("fsdp", None),
        P("fsdp"),
        P(None, "fsdp", None, "tp"),
        P(None, None, "tp", "fsdp"),
        P(None, "tp", "fsdp"),
        P(None, "fsdp"),
        P(None, "fsdp", "tp"),
        P(None, "tp", "fsdp"),
        P(None, "tp", "fsdp"),
        P(None, "fsdp"),
        P(None, "fsdp"),
        P(None, "fsdp"),
        P("fsdp", "ctx", None),
    )
    out_specs = (
        P("fsdp", "ctx", None),
        P("fsdp", "ctx", None),
        P(None, "fsdp", None, "tp"),
        P(None, None, "tp", "fsdp"),
        P(None, "tp", "fsdp"),
        P(None, "fsdp"),
        P(None, "fsdp", "tp"),
        P(None, "tp", "fsdp"),
        P(None, "tp", "fsdp"),
        P(None, "fsdp"),
        P(None, "fsdp"),
        P(None, "fsdp"),
    )
    return jax.shard_map(shards, mesh=mesh, in_specs=in_specs, out_specs=out_specs, check_vma=False)
```

profile of v0, /device:TPU:0, one launch (start us, length us, event | category | flops | bytes accessed | tf_op | source)
XLA Modules:
  0.0 1731.2 jit_solution(4498654425942981708)
XLA Ops:
  113.4 52.4 %all-reduce.12.cloned.1.call-done = bf16[3,320,1024]{2,1,0:T(8,128)(2,1)} async-done(((bf16[3,320,1024]{2,1,0:T(8,128)(2,1)}), bf16[3,320,1024]{2,1,0:T(8,128)(2,1)}) %all-reduce.12.cloned.1.call-update) | async-done | bytes 1966096 | tf_op jit(solution)/shard_map/psum | solution.py:54
  169.3 33.3 %all-gather.31.cloned.1.call-done = bf16[1,1024,1024]{2,1,0:T(8,128)(2,1)} async-done(((bf16[1,256,1024]{2,1,0:T(8,128)(2,1)}), bf16[1,1024,1024]{2,1,0:T(8,128)(2,1)}) %all-gather.31.cloned.1.call-update) | async-done | bytes 2097168 | tf_op jit(solution)/shard_map/all_gather | solution.py:29
  209.1 31.0 %all-gather.33.cloned.1.call-done = bf16[1,1024,1024]{2,1,0:T(8,128)(2,1)} async-done(((bf16[1,1024,256]{2,1,0:T(8,128)(2,1)}), bf16[1,1024,1024]{2,1,0:T(8,128)(2,1)}) %all-gather.33.cloned.1.call-update) | async-done | bytes 2097168 | tf_op jit(solution)/shard_map/all_gather | solution.py:31
  283.8 44.1 %all-reduce.14.cloned.1.call-done = bf16[3,320,1024]{2,1,0:T(8,128)(2,1)} async-done(((bf16[3,320,1024]{2,1,0:T(8,128)(2,1)}), bf16[3,320,1024]{2,1,0:T(8,128)(2,1)}) %all-reduce.14.cloned.1.call-update) | async-done | bytes 1966096 | tf_op jit(solution)/shard_map/psum | solution.py:54
  333.7 25.9 %all-gather.35.cloned.1.call-done = bf16[1,1024,3,256]{3,1,2,0:T(8,128)(2,1)} async-done(((bf16[1,256,3,256]{3,1,2,0:T(8,128)(2,1)}), bf16[1,1024,3,256]{3,1,2,0:T(8,128)(2,1)}) %all-gather.35.cloned.1.call-update) | async-done | bytes 1572880 | tf_op jit(solution)/shard_map/all_gather | solution.py:25
  418.6 56.1 %all-reduce.16.cloned.1.call-done = bf16[3,320,1024]{2,1,0:T(8,128)(2,1)} async-done(((bf16[3,320,1024]{2,1,0:T(8,128)(2,1)}), bf16[3,320,1024]{2,1,0:T(8,128)(2,1)}) %all-reduce.16.cloned.1.call-update) | async-done | bytes 1966096 | tf_op jit(solution)/shard_map/psum | solution.py:54
  481.1 30.4 %all-gather.37.cloned.1.call-done = bf16[1,1024,1024]{2,1,0:T(8,128)(2,1)} async-done(((bf16[1,256,1024]{2,1,0:T(8,128)(2,1)}), bf16[1,1024,1024]{2,1,0:T(8,128)(2,1)}) %all-gather.37.cloned.1.call-update) | async-done | bytes 2097168 | tf_op jit(solution)/shard_map/all_gather | solution.py:29
  518.2 30.9 %all-gather.39.cloned.1.call-done = bf16[1,1024,1024]{2,1,0:T(8,128)(2,1)} async-done(((bf16[1,1024,256]{2,1,0:T(8,128)(2,1)}), bf16[1,1024,1024]{2,1,0:T(8,128)(2,1)}) %all-gather.39.cloned.1.call-update) | async-done | bytes 2097168 | tf_op jit(solution)/shard_map/all_gather | solution.py:31
  562.2 81.1 %all-reduce.18.cloned.1.call-done = bf16[3,320,1024]{2,1,0:T(8,128)(2,1)} async-done(((bf16[3,320,1024]{2,1,0:T(8,128)(2,1)}), bf16[3,320,1024]{2,1,0:T(8,128)(2,1)}) %all-reduce.18.cloned.1.call-update) | async-done | bytes 1966096 | tf_op jit(solution)/shard_map/psum | solution.py:58
  701.9 82.9 %all-reduce.20.cloned.1.call-done = bf16[3,320,1024]{2,1,0:T(8,128)(2,1)} async-done(((bf16[3,320,1024]{2,1,0:T(8,128)(2,1)}), bf16[3,320,1024]{2,1,0:T(8,128)(2,1)}) %all-reduce.20.cloned.1.call-update) | async-done | bytes 1966096 | tf_op jit(solution)/shard_map/psum | solution.py:58
  808.5 80.0 %all-reduce.22.cloned.1.call-done = bf16[3,320,1024]{2,1,0:T(8,128)(2,1)} async-done(((bf16[3,320,1024]{2,1,0:T(8,128)(2,1)}), bf16[3,320,1024]{2,1,0:T(8,128)(2,1)}) %all-reduce.22.cloned.1.call-update) | async-done | bytes 1966096 | tf_op jit(solution)/shard_map/psum | solution.py:58
  1005.6 82.8 %all-reduce.24.cloned.1.call-done = (bf16[3,320,1024]{2,1,0:T(8,128)(2,1)}, bf16[3,320,1024]{2,1,0:T(8,128)(2,1)}) async-done(((bf16[3,320,1024]{2,1,0:T(8,128)(2,1)}, bf16[3,320,1024]{2,1,0:T(8,128)(2,1)}), (bf16[3,320,1024]{2,1,0:T(8,128)(2,1)}, bf16[3,320,1024]{2,1,0:T(8,128)(2,1)})) %all-reduce.24.cloned.1.call-update) | async-done | bytes 3932176 | tf_op jit(solution)/shard_map/psum | solution.py:54
  1094.5 21.0 %reduce-scatter.63.cloned.1.call-done = bf16[1,256,256]{2,1,0:T(8,128)(2,1)} async-done(((bf16[1,256,1024]{2,1,0:T(8,128)(2,1)}), bf16[1,256,256]{2,1,0:T(8,128)(2,1)}) %reduce-scatter.63.cloned.1.call-update) | async-done | bytes 131088 | tf_op jit(solution)/shard_map/reduce_scatter | solution.py:69
  1115.5 38.4 %reduce-scatter.71.cloned.1.call-done = bf16[1,1024,256]{2,1,0:T(8,128)(2,1)} async-done(((bf16[1,1024,1024]{2,1,0:T(8,128)(2,1)}), bf16[1,1024,256]{2,1,0:T(8,128)(2,1)}) %reduce-scatter.71.cloned.1.call-update) | async-done | bytes 524304 | tf_op jit(solution)/shard_map/reduce_scatter | solution.py:81
  1154.0 38.6 %reduce-scatter.67.cloned.1.call-done = bf16[1,256,1024]{2,1,0:T(8,128)(2,1)} async-done(((bf16[1,1024,1024]{2,1,0:T(8,128)(2,1)}), bf16[1,256,1024]{2,1,0:T(8,128)(2,1)}) %reduce-scatter.67.cloned.1.call-update) | async-done | bytes 524304 | tf_op jit(solution)/shard_map/reduce_scatter | solution.py:75
  1192.6 34.8 %reduce-scatter.59.cloned.1.call-done = bf16[1,256,3,256]{3,1,2,0:T(8,128)(2,1)} async-done(((bf16[1,1024,3,256]{3,1,2,0:T(8,128)(2,1)}), bf16[1,256,3,256]{3,1,2,0:T(8,128)(2,1)}) %reduce-scatter.59.cloned.1.call-update) | async-done | bytes 393232 | tf_op jit(solution)/shard_map/reduce_scatter | solution.py:63
  1227.4 28.4 %reduce-scatter.61.cloned.1.call-done = bf16[1,256,256]{2,1,0:T(8,128)(2,1)} async-done(((bf16[1,256,1024]{2,1,0:T(8,128)(2,1)}), bf16[1,256,256]{2,1,0:T(8,128)(2,1)}) %reduce-scatter.61.cloned.1.call-update) | async-done | bytes 131088 | tf_op jit(solution)/shard_map/reduce_scatter | solution.py:69
  1255.8 38.2 %reduce-scatter.69.cloned.1.call-done = bf16[1,1024,256]{2,1,0:T(8,128)(2,1)} async-done(((bf16[1,1024,1024]{2,1,0:T(8,128)(2,1)}), bf16[1,1024,256]{2,1,0:T(8,128)(2,1)}) %reduce-scatter.69.cloned.1.call-update) | async-done | bytes 524304 | tf_op jit(solution)/shard_map/reduce_scatter | solution.py:81
  1294.0 38.9 %reduce-scatter.65.cloned.1.call-done = bf16[1,256,1024]{2,1,0:T(8,128)(2,1)} async-done(((bf16[1,1024,1024]{2,1,0:T(8,128)(2,1)}), bf16[1,256,1024]{2,1,0:T(8,128)(2,1)}) %reduce-scatter.65.cloned.1.call-update) | async-done | bytes 524304 | tf_op jit(solution)/shard_map/reduce_scatter | solution.py:75
  1332.9 34.5 %reduce-scatter.57.cloned.1.call-done = bf16[1,256,3,256]{3,1,2,0:T(8,128)(2,1)} async-done(((bf16[1,1024,3,256]{3,1,2,0:T(8,128)(2,1)}), bf16[1,256,3,256]{3,1,2,0:T(8,128)(2,1)}) %reduce-scatter.57.cloned.1.call-update) | async-done | bytes 393232 | tf_op jit(solution)/shard_map/reduce_scatter | solution.py:63
  1375.4 18.7 %reduce-scatter.83.cloned.1.call-done = bf16[256,1]{1,0:T(8,128)(2,1)} async-done(((bf16[1024,1]{1,0:T(8,128)(2,1)}), bf16[256,1]{1,0:T(8,128)(2,1)}) %reduce-scatter.83.cloned.1.call-update) | async-done | bytes 528
  1395.5 25.6 %reduce-scatter.95.cloned.1.call-done = bf16[256,1]{1,0:T(8,128)(2,1)} async-done(((bf16[1024,1]{1,0:T(8,128)(2,1)}), bf16[256,1]{1,0:T(8,128)(2,1)}) %reduce-scatter.95.cloned.1.call-update) | async-done | bytes 528
  1422.0 25.9 %reduce-scatter.79.cloned.1.call-done = bf16[256,1]{1,0:T(8,128)(2,1)} async-done(((bf16[1024,1]{1,0:T(8,128)(2,1)}), bf16[256,1]{1,0:T(8,128)(2,1)}) %reduce-scatter.79.cloned.1.call-update) | async-done | bytes 528
  1448.9 26.2 %reduce-scatter.87.cloned.1.call-done = bf16[256,1]{1,0:T(8,128)(2,1)} async-done(((bf16[1024,1]{1,0:T(8,128)(2,1)}), bf16[256,1]{1,0:T(8,128)(2,1)}) %reduce-scatter.87.cloned.1.call-update) | async-done | bytes 528
  1476.0 25.3 %reduce-scatter.75.cloned.1.call-done = bf16[64,2]{1,0:T(8,128)(2,1)} async-done(((bf16[256,2]{1,0:T(8,128)(2,1)}), bf16[64,2]{1,0:T(8,128)(2,1)}) %reduce-scatter.75.cloned.1.call-update) | async-done | bytes 272
  1502.3 26.2 %reduce-scatter.85.cloned.1.call-done = bf16[256,1]{1,0:T(8,128)(2,1)} async-done(((bf16[1024,1]{1,0:T(8,128)(2,1)}), bf16[256,1]{1,0:T(8,128)(2,1)}) %reduce-scatter.85.cloned.1.call-update) | async-done | bytes 528
  1529.4 25.9 %reduce-scatter.91.cloned.1.call-done = bf16[256,1]{1,0:T(8,128)(2,1)} async-done(((bf16[1024,1]{1,0:T(8,128)(2,1)}), bf16[256,1]{1,0:T(8,128)(2,1)}) %reduce-scatter.91.cloned.1.call-update) | async-done | bytes 528
  1556.2 26.0 %reduce-scatter.81.cloned.1.call-done = bf16[256,1]{1,0:T(8,128)(2,1)} async-done(((bf16[1024,1]{1,0:T(8,128)(2,1)}), bf16[256,1]{1,0:T(8,128)(2,1)}) %reduce-scatter.81.cloned.1.call-update) | async-done | bytes 528
  1583.6 25.5 %reduce-scatter.77.cloned.1.call-done = bf16[256,1]{1,0:T(8,128)(2,1)} async-done(((bf16[1024,1]{1,0:T(8,128)(2,1)}), bf16[256,1]{1,0:T(8,128)(2,1)}) %reduce-scatter.77.cloned.1.call-update) | async-done | bytes 528
  1610.1 26.2 %reduce-scatter.93.cloned.1.call-done = bf16[256,1]{1,0:T(8,128)(2,1)} async-done(((bf16[1024,1]{1,0:T(8,128)(2,1)}), bf16[256,1]{1,0:T(8,128)(2,1)}) %reduce-scatter.93.cloned.1.call-update) | async-done | bytes 528
  1637.1 25.4 %reduce-scatter.73.cloned.1.call-done = bf16[64,2]{1,0:T(8,128)(2,1)} async-done(((bf16[256,2]{1,0:T(8,128)(2,1)}), bf16[64,2]{1,0:T(8,128)(2,1)}) %reduce-scatter.73.cloned.1.call-update) | async-done | bytes 272
  1696.1 19.8 %all-reduce.26.cloned.1.call-done = (bf16[1,256,3,256]{3,1,2,0:T(8,128)(2,1)}, bf16[1,256,3,256]{3,1,2,0:T(8,128)(2,1)}, bf16[1,256,256]{2,1,0:T(8,128)(2,1)}, b...) async-done(((bf16[1,256,3,256]{3,1,2,0:T(8,128)(2,1)}, ...) | async-done | bytes 3145744 | tf_op jit(solution)/shard_map/psum | solution.py:91
  (544 shorter events, 513.9 us)
Async XLA Ops:
  9.4 156.4 %all-reduce.12.cloned.1.call-start = ((), (), s32[]{:S(2)}) async-start(), calls=%async_computation.24 | async-start | bytes 3932160 | tf_op jit(solution)/shard_map/psum | solution.py:54
  83.6 119.0 %all-gather.31.cloned.1.call-start = ((), (), s32[]{:S(2)}) async-start(), calls=%async_computation.43 | async-start | bytes 2621440 | tf_op jit(solution)/shard_map/all_gather | solution.py:29
  86.0 154.1 %all-gather.33.cloned.1.call-start = ((), (), s32[]{:S(2)}) async-start(), calls=%async_computation.44 | async-start | bytes 2621440 | tf_op jit(solution)/shard_map/all_gather | solution.py:31
  88.3 239.6 %all-reduce.14.cloned.1.call-start = ((), (), s32[]{:S(2)}) async-start(), calls=%async_computation.25 | async-start | bytes 3932160 | tf_op jit(solution)/shard_map/psum | solution.py:54
  246.4 228.3 %all-reduce.16.cloned.1.call-start = ((), (), s32[]{:S(2)}) async-start(), calls=%async_computation.26 | async-start | bytes 3932160 | tf_op jit(solution)/shard_map/psum | solution.py:54
  393.3 155.8 %all-gather.39.cloned.1.call-start = ((), (), s32[]{:S(2)}) async-start(), calls=%async_computation.47 | async-start | bytes 2621440 | tf_op jit(solution)/shard_map/all_gather | solution.py:31
  394.0 249.3 %all-reduce.18.cloned.1.call-start = ((), (), s32[]{:S(2)}) async-start(), calls=%async_computation.27 | async-start | bytes 3932160 | tf_op jit(solution)/shard_map/psum | solution.py:58
  561.2 134.5 %reduce-scatter.51.cloned.1.call-start = ((), (), s32[]{:S(2)}) async-start(), calls=%async_computation.29 | async-start | bytes 1474560 | tf_op jit(solution)/shard_map/reduce_scatter | solution.py:244
  701.6 186.9 %all-reduce.22.cloned.1.call-start = ((), (), s32[]{:S(2)}) async-start(), calls=%async_computation.31 | async-start | bytes 3932160 | tf_op jit(solution)/shard_map/psum | solution.py:58
  807.4 128.7 %reduce-scatter.55.cloned.1.call-start = ((), (), s32[]{:S(2)}) async-start(), calls=%async_computation.33 | async-start | bytes 1474560 | tf_op jit(solution)/shard_map/reduce_scatter | solution.py:244
  927.6 160.8 %all-reduce.24.cloned.1.call-start = ((), (), s32[]{:S(2)}) async-start(), calls=%async_computation.60 | async-start | bytes 7864320 | tf_op jit(solution)/shard_map/psum | solution.py:54
  941.7 173.8 %reduce-scatter.63.cloned.1.call-start = ((), (), s32[]{:S(2)}) async-start(), calls=%async_computation.37 | async-start | bytes 655360 | tf_op jit(solution)/shard_map/reduce_scatter | solution.py:69
  945.8 208.2 %reduce-scatter.71.cloned.1.call-start = ((), (), s32[]{:S(2)}) async-start(), calls=%async_computation.41 | async-start | bytes 2621440 | tf_op jit(solution)/shard_map/reduce_scatter | solution.py:81
  952.6 240.0 %reduce-scatter.67.cloned.1.call-start = ((), (), s32[]{:S(2)}) async-start(), calls=%async_computation.39 | async-start | bytes 2621440 | tf_op jit(solution)/shard_map/reduce_scatter | solution.py:75
  959.5 267.9 %reduce-scatter.59.cloned.1.call-start = ((), (), s32[]{:S(2)}) async-start(), calls=%async_computation.35 | async-start | bytes 1966080 | tf_op jit(solution)/shard_map/reduce_scatter | solution.py:63
  965.2 290.6 %reduce-scatter.61.cloned.1.call-start = ((), (), s32[]{:S(2)}) async-start(), calls=%async_computation.36 | async-start | bytes 655360 | tf_op jit(solution)/shard_map/reduce_scatter | solution.py:69
  969.2 324.8 %reduce-scatter.69.cloned.1.call-start = ((), (), s32[]{:S(2)}) async-start(), calls=%async_computation.40 | async-start | bytes 2621440 | tf_op jit(solution)/shard_map/reduce_scatter | solution.py:81
  975.8 357.2 %reduce-scatter.65.cloned.1.call-start = ((), (), s32[]{:S(2)}) async-start(), calls=%async_computation.38 | async-start | bytes 2621440 | tf_op jit(solution)/shard_map/reduce_scatter | solution.py:75
  982.1 385.2 %reduce-scatter.57.cloned.1.call-start = ((), (), s32[]{:S(2)}) async-start(), calls=%async_computation.34 | async-start | bytes 1966080 | tf_op jit(solution)/shard_map/reduce_scatter | solution.py:63
  986.7 407.5 %reduce-scatter.83.cloned.1.call-start = ((), (), s32[]{:S(2)}) async-start(), calls=%async_computation.53 | async-start | bytes 327680
  990.9 430.1 %reduce-scatter.95.cloned.1.call-start = ((), (), s32[]{:S(2)}) async-start(), calls=%async_computation.59 | async-start | bytes 327680
  991.9 456.0 %reduce-scatter.79.cloned.1.call-start = ((), (), s32[]{:S(2)}) async-start(), calls=%async_computation.51 | async-start | bytes 327680
  992.9 482.1 %reduce-scatter.87.cloned.1.call-start = ((), (), s32[]{:S(2)}) async-start(), calls=%async_computation.55 | async-start | bytes 327680
  994.0 507.3 %reduce-scatter.75.cloned.1.call-start = ((), (), s32[]{:S(2)}) async-start(), calls=%async_computation.49 | async-start | bytes 81920
  995.5 533.0 %reduce-scatter.85.cloned.1.call-start = ((), (), s32[]{:S(2)}) async-start(), calls=%async_computation.54 | async-start | bytes 327680
  996.5 558.9 %reduce-scatter.91.cloned.1.call-start = ((), (), s32[]{:S(2)}) async-start(), calls=%async_computation.57 | async-start | bytes 327680
  997.5 584.8 %reduce-scatter.81.cloned.1.call-start = ((), (), s32[]{:S(2)}) async-start(), calls=%async_computation.52 | async-start | bytes 327680
  1001.8 607.3 %reduce-scatter.77.cloned.1.call-start = ((), (), s32[]{:S(2)}) async-start(), calls=%async_computation.50 | async-start | bytes 327680
  1003.0 633.2 %reduce-scatter.93.cloned.1.call-start = ((), (), s32[]{:S(2)}) async-start(), calls=%async_computation.58 | async-start | bytes 327680
  1004.1 658.4 %reduce-scatter.73.cloned.1.call-start = ((), (), s32[]{:S(2)}) async-start(), calls=%async_computation.48 | async-start | bytes 81920
  1005.6 683.9 %reduce-scatter.89.cloned.1.call-start = ((), (), s32[]{:S(2)}) async-start(), calls=%async_computation.56 | async-start | bytes 327680
  1094.5 621.4 %all-reduce.26.cloned.1.call-start = ((), (), s32[]{:S(2)}) async-start(), calls=%async_computation.61 | async-start | bytes 6291456 | tf_op jit(solution)/shard_map/psum | solution.py:91
  (136 other events, 4033.5 us)
Sparse Core Ops, SparseCore 0:
  10.4 38.7 all-gather.28
  83.8 81.9 all-reduce.11
  168.2 34.3 all-gather.30
  204.9 35.1 all-gather.32
  245.9 81.9 all-reduce.13
  329.6 30.0 all-gather.34
  392.7 81.9 all-reduce.15
  477.1 34.3 all-gather.36
  513.9 35.1 all-gather.38
  561.3 81.9 all-reduce.17
  701.7 83.0 all-reduce.19
  807.5 80.9 all-reduce.21
  941.8 146.5 all-reduce.23
  1091.7 23.8 reduce-scatter.62
  1118.8 35.1 reduce-scatter.70
  1157.4 35.1 reduce-scatter.66
  1196.4 30.9 reduce-scatter.58
  1231.0 24.7 reduce-scatter.60
  1258.8 35.1 reduce-scatter.68
  1297.7 35.2 reduce-scatter.64
  1336.5 30.8 reduce-scatter.56
  1370.0 24.0 reduce-scatter.82
  1397.0 24.0 reduce-scatter.94
  1423.8 24.0 reduce-scatter.78
  1450.9 24.0 reduce-scatter.86
  1504.3 24.1 reduce-scatter.84
  1531.2 24.0 reduce-scatter.90
  1558.1 24.0 reduce-scatter.80
  1585.0 24.0 reduce-scatter.76
  1612.1 24.0 reduce-scatter.92
  1638.8 23.6 reduce-scatter.72
  1665.3 24.0 reduce-scatter.88
  (6 shorter events, 77.2 us)
where the time goes:
time: 1740 us; the launch traced here: 1730 us
  waiting for transfers between devices  1220 us (70%)
  matrix products  162 us (9%)
  blocking collectives  145 us (8%)
  other arithmetic  91.1 us (5%)
  local copies, waits for them, and re-layouts  90 us (5%)
    unnamed x50, waiting for transfers between devices  298 us
    psum x3, waiting for transfers between devices, normed_sum(): return lax.psum(partial_sum.astype(jnp.bfloat16), 'tp').astype(jnp.float32)  244 us
    psum x4, waiting for transfers between devices, branch_sum(): return lax.psum(partial_sum.astype(jnp.bfloat16), 'tp').astype(jnp.float32)  235 us
    reduce_scatter x2, waiting for transfers between devices, reduce_grads(): lax.psum_scatter(grads[4].astype(jnp.bfloat16), 'fsdp', scatter_dimension...  77.5 us
    reduce_scatter x2, waiting for transfers between devices, reduce_grads(): lax.psum_scatter(grads[6].astype(jnp.bfloat16), 'fsdp', scatter_dimension...  76.6 us
    reduce_scatter x2, waiting for transfers between devices, reduce_grads(): lax.psum_scatter(grads[0].astype(jnp.bfloat16), 'fsdp', scatter_dimension...  69.3 us
    all_gather x2, waiting for transfers between devices, fetch_weights(): lax.all_gather(pieces[4], 'fsdp', axis=0, tiled=True)  63.7 us
    all_gather x2, waiting for transfers between devices, fetch_weights(): lax.all_gather(pieces[6], 'fsdp', axis=1, tiled=True)  61.9 us
  transfers between devices with their start and end apart: 38, of which 34 were waited for; matrix products, arithmetic and copies ran while one was open for 10% of the time, Pallas kernels for 0%

commit v1 on v0

v1 whole, which is shorter than its diff:
```python
import jax
import jax.numpy as jnp
from jax import lax
from jax.sharding import PartitionSpec as P

HD = 64
SEQ = 577
BF = jnp.bfloat16
F32 = jnp.float32


def layer_norm(vectors, scaling):
    centre = vectors - jnp.mean(vectors, axis=-1, keepdims=True)
    spread = jnp.mean(centre * centre, axis=-1, keepdims=True)
    return centre * lax.rsqrt(spread + 1e-06) * scaling


def gelu_exact(values):
    return 0.5 * values * (1.0 + lax.erf(values * 0.7071067811865476))


X_PAIRS = [(0, 1), (1, 0), (2, 3), (3, 2)]
Y_PAIRS = [(0, 2), (2, 0), (1, 3), (3, 1)]


def square():
    return lax.axis_size("fsdp") == 4


def reorder(values):
    if not square():
        return values
    place = lax.axis_index("fsdp")
    lead = values.shape[:-1]
    blocks = values.reshape(lead + (2, 2, values.shape[-1] // 4))
    blocks = jnp.where(place % 2 == 1, blocks[..., :, ::-1, :], blocks)
    blocks = jnp.where(place >= 2, blocks[..., ::-1, :, :], blocks)
    return blocks.reshape(values.shape)


def send_x(values):
    return lax.ppermute(values, "fsdp", X_PAIRS)


def send_y(values):
    return lax.ppermute(values, "fsdp", Y_PAIRS)


def swap(values):
    return lax.ppermute(values, "ctx", [(0, 1), (1, 0)])


def both_cores(partial_sum):
    low = partial_sum.astype(BF)
    return low.astype(F32) + swap(low).astype(F32)


def gather_rows(shard):
    if not square():
        return lax.all_gather(shard, "fsdp", axis=0, tiled=True)
    half = shard.shape[0] // 2
    from_x, from_y = send_x(shard), send_y(shard)
    far_a, far_b = send_y(from_x[:half]), send_x(from_y[half:])
    return jnp.concatenate([shard, from_x, from_y, far_a, far_b], axis=0)


def scatter_rows(full):
    if not square():
        return lax.psum_scatter(full.astype(BF), "fsdp", scatter_dimension=0, tiled=True).astype(F32)
    rows = full.shape[0] // 4
    half = rows // 2
    own, to_x, to_y, far = [full[k * rows : (k + 1) * rows] for k in range(4)]
    first = send_x(jnp.concatenate([to_x[:half], far[:half]]).astype(BF)).astype(F32)
    second = send_y(jnp.concatenate([to_y[half:], far[half:]]).astype(BF)).astype(F32)
    own_a = own[:half] + first[:half]
    own_b = own[half:] + second[:half]
    pass_y = (to_y[:half] + first[half:]).astype(BF)
    pass_x = (to_x[half:] + second[half:]).astype(BF)
    own_a = own_a + send_y(pass_y).astype(F32)
    own_b = own_b + send_x(pass_x).astype(F32)
    return jnp.concatenate([own_a, own_b])


def gather_matrix(shard, place):
    rows, groups, columns = shard.shape
    half = lax.dynamic_index_in_dim(shard.reshape(rows, groups, 2, columns // 2), place, 2, keepdims=False)
    along = lax.all_gather(half, "tp", axis=0)
    along = jnp.transpose(along, (1, 2, 0, 3)).reshape(rows, -1)
    return gather_rows(along)


def scatter_matrix(grad, groups, place):
    count = lax.axis_size("tp")
    kept = scatter_rows(grad).astype(BF)
    rows = kept.shape[0]
    kept = jnp.transpose(kept.reshape(rows, groups, count, -1), (2, 0, 1, 3))
    own = lax.psum_scatter(kept, "tp", scatter_dimension=0, tiled=False)
    other = swap(own)
    low = jnp.where(place == 0, own, other)
    high = jnp.where(place == 0, other, own)
    return jnp.concatenate([low, high], axis=-1).astype(F32)


def heads_of(values):
    return values.reshape(values.shape[0], -1, HD)


def masked_scores(queries, keys, key_valid):
    scores = jnp.einsum("qhd,khd->hqk", queries, keys, preferred_element_type=F32) * HD ** (-0.5)
    return jnp.where(key_valid, scores, -1000000000.0)


def mm(left, right):
    return jnp.dot(left, right, preferred_element_type=F32)


def mm_nt(left, right):
    return lax.dot_general(left, right, (((1,), (1,)), ((), ())), preferred_element_type=F32)


def mm_tn(left, right):
    return lax.dot_general(left, right, (((0,), (0,)), ((), ())), preferred_element_type=F32)


def forward_layer(stream, weights, vectors, key_valid):
    qkv, out, up, down = weights
    shift_q, shift_v, out_shift, up_shift, down_shift, gain_first, gain_second = vectors
    normed = layer_norm(stream, gain_first).astype(BF)
    project = mm(normed, qkv)
    width = project.shape[1] // 3
    queries = heads_of((project[:, :width] + shift_q).astype(BF))
    keys = heads_of(project[:, width : 2 * width].astype(BF))
    values = heads_of((project[:, 2 * width :] + shift_v).astype(BF))
    scores = masked_scores(queries, keys, key_valid)
    highest = jnp.max(scores, axis=-1, keepdims=True)
    exponent = jnp.exp(scores - highest)
    denominator = jnp.sum(exponent, axis=-1, keepdims=True)
    probs = (exponent / denominator).astype(BF)
    log_total = highest + jnp.log(denominator)
    mixed = jnp.einsum("hqk,khd->qhd", probs, values, preferred_element_type=F32).astype(BF)
    mixed = mixed.reshape(stream.shape[0], width)
    middle = stream + both_cores(mm_nt(mixed, out)) + out_shift
    normed_b = layer_norm(middle, gain_second).astype(BF)
    hidden = mm(normed_b, up) + up_shift
    active = gelu_exact(hidden).astype(BF)
    following = middle + both_cores(mm_nt(active, down)) + down_shift
    return following, (stream, normed, queries, keys, values, log_total, mixed, middle, normed_b, hidden, active)


def backward_layer(gradient, saved, weights, vectors, key_valid, emit):
    qkv, out, up, down = weights
    gain_first, gain_second = vectors[5:]
    stream, normed, queries, keys, values, log_total, mixed, middle, normed_b, hidden, active = saved
    total = lambda array: jnp.sum(array.astype(F32), axis=0)
    grad_low = gradient.astype(BF)
    emit("down", mm_tn(grad_low, active))
    delta_hidden = jax.vjp(gelu_exact, hidden)[1](mm(grad_low, down))[0].astype(BF)
    emit("up", mm_tn(normed_b, delta_hidden))
    delta_normed_b = both_cores(mm_nt(delta_hidden, up))
    back_middle, delta_gain_second = jax.vjp(layer_norm, middle, gain_second)[1](delta_normed_b)
    grad_middle = gradient + back_middle
    grad_attend = grad_middle.astype(BF)
    emit("out", mm_tn(grad_attend, mixed))
    delta_mixed = heads_of(mm(grad_attend, out).astype(BF))
    probs = jnp.exp(masked_scores(queries, keys, key_valid) - log_total)
    delta_values = jnp.einsum("hqk,qhd->khd", probs.astype(BF), delta_mixed, preferred_element_type=F32).astype(BF)
    delta_probs = jnp.einsum("qhd,khd->hqk", delta_mixed, values, preferred_element_type=F32)
    inner = jnp.sum(probs * delta_probs, axis=-1, keepdims=True)
    delta_scores = (probs * (delta_probs - inner)).astype(BF)
    scale = HD ** (-0.5)
    delta_queries = (jnp.einsum("hqk,khd->qhd", delta_scores, keys, preferred_element_type=F32) * scale).astype(BF)
    delta_keys = (jnp.einsum("hqk,qhd->khd", delta_scores, queries, preferred_element_type=F32) * scale).astype(BF)
    flat = [piece.reshape(stream.shape[0], -1) for piece in (delta_queries, delta_keys, delta_values)]
    delta_project = jnp.concatenate(flat, axis=1)
    emit("qkv", mm_tn(normed, delta_project))
    delta_normed = both_cores(mm_nt(delta_project, qkv))
    back_stream, delta_gain_first = jax.vjp(layer_norm, stream, gain_first)[1](delta_normed)
    sums = (
        total(flat[0]),
        total(flat[2]),
        total(grad_attend),
        total(delta_hidden),
        total(grad_low),
        delta_gain_first,
        delta_gain_second,
    )
    return grad_middle + back_stream, sums


def shards(
    tokens,
    lengths,
    image_count,
    qkv_weight,
    qv_bias,
    out_weight,
    out_bias,
    up_weight,
    up_bias,
    down_weight,
    down_bias,
    gain_one,
    gain_two,
    cotangent,
):
    slots, capacity, features = tokens.shape
    layers = qkv_weight.shape[0]
    n_fsdp, n_tp = lax.axis_size("fsdp"), lax.axis_size("tp")
    assert lax.axis_size("ctx") == 2 and slots <= n_tp
    group, core, lane = lax.axis_index("fsdp"), lax.axis_index("ctx"), lax.axis_index("tp")
    rows = -(-SEQ // 16) * 16
    slot = jnp.minimum(lane, slots - 1)
    own_lengths = lax.dynamic_index_in_dim(lengths, slot, 0, keepdims=False)
    live = lane < jnp.minimum(image_count[0], slots)
    key_valid = (jnp.arange(rows) < SEQ)[None, None, :]
    row_mask = ((jnp.arange(rows) < SEQ) & live).astype(F32)[:, None]

    pieces = (qv_bias, up_bias, out_bias, down_bias, gain_one, gain_two)
    packed = jnp.concatenate([piece.reshape(-1) for piece in pieces])
    spread = lax.all_gather(packed, ("fsdp", "tp"), axis=0).reshape(n_fsdp, n_tp, -1)
    found, start = [], 0
    for piece in pieces:
        found.append(spread[:, :, start : start + piece.size])
        start += piece.size

    def by_core(array, count):
        array = array.reshape(n_fsdp, n_tp, layers, count, -1)
        array = jnp.transpose(array, (2, 3, 1, 0, 4)).reshape(layers, count, n_tp, 2, -1)
        return lax.dynamic_index_in_dim(array, core, 3, keepdims=False).reshape(layers, count, -1)

    def by_feature(array):
        array = array[:, 0].reshape(n_fsdp, layers, -1)
        return reorder(jnp.transpose(array, (1, 0, 2)).reshape(layers, features))

    qv_all, up_all = by_core(found[0], 2), by_core(found[1], 1)
    out_all, down_all, one_all, two_all = [by_feature(array) for array in found[2:]]
    vectors = [
        (qv_all[l, 0], qv_all[l, 1], out_all[l], up_all[l, 0], down_all[l], one_all[l], two_all[l])
        for l in range(layers)
    ]

    weights = []
    for l in range(layers):
        raw = (qkv_weight[l], out_weight[l].T[:, None], up_weight[l][:, None], down_weight[l].T[:, None])
        weights.append(tuple(gather_matrix(piece, core) for piece in raw))

    own_pair = jnp.stack([lax.dynamic_index_in_dim(a, slot, 0, keepdims=False) for a in (tokens, cotangent)])
    other_pair = swap(own_pair)
    low = jnp.where(core == 0, own_pair, other_pair)
    high = jnp.where(core == 0, other_pair, own_pair)
    image = jnp.concatenate([low, jnp.zeros_like(low)], axis=1)
    image = lax.dynamic_update_slice_in_dim(image, high, own_lengths[0], 1)[:, :rows]
    image = reorder(image).astype(F32)

    stream = image[0]
    saved = []
    for l in range(layers):
        stream, items = forward_layer(stream, weights[l], vectors[l], key_valid)
        saved.append(items)

    own_length = own_lengths[core]
    own_rows = ((jnp.arange(capacity) < own_length) & live)[:, None]

    def give_back(values):
        values = jnp.pad(reorder(values.astype(BF)), ((0, 2 * capacity - rows), (0, 0)))
        mine = lax.dynamic_slice_in_dim(values, jnp.where(core == 0, 0, own_lengths[0]), capacity, 0)
        mine = jnp.where(own_rows, mine, jnp.zeros_like(mine))
        return lax.all_gather(mine, "tp", axis=0)[:slots]

    output = give_back(stream)
    gradient = image[1] * row_mask
    grads = {}
    sums = [None] * layers
    for l in reversed(range(layers)):

        def emit(name, grad, l=l):
            grads[name, l] = scatter_matrix(grad, 3 if name == "qkv" else 1, core)

        gradient, sums[l] = backward_layer(gradient, saved[l], weights[l], vectors[l], key_valid, emit)
    input_grad = give_back(gradient)

    def from_core(array, count):
        array = array.reshape(layers, count, n_tp, 1, -1)
        mask = (jnp.arange(2) == core)[:, None]
        return jnp.where(mask, array, 0.0).reshape(layers * count, -1)

    first = (core == 0).astype(F32)
    member = lambda k: jnp.stack([sums[l][k] for l in range(layers)])
    joined = [
        from_core(jnp.stack([member(0), member(1)], axis=1), 2),
        from_core(member(3)[:, None], 1),
    ] + [reorder(member(k)) * first for k in (2, 4, 5, 6)]
    summed = lax.psum(jnp.concatenate([a.reshape(-1) for a in joined]), ("fsdp", "ctx", "tp"))
    whole, start = [], 0
    for a in joined:
        whole.append(summed[start : start + a.size])
        start += a.size
    pick = lambda a, i, axis: lax.dynamic_index_in_dim(a, i, axis, keepdims=True)
    qv_grad = pick(pick(whole[0].reshape(layers, 2, n_tp, n_fsdp, -1), lane, 2), group, 3)[:, :, :, 0]
    up_grad = pick(pick(whole[1].reshape(layers, n_tp, n_fsdp, -1), lane, 1), group, 2)[:, :, 0]
    out_shift, down_shift, one, two = [pick(a.reshape(layers, n_fsdp, -1), group, 1)[:, 0] for a in whole[2:]]

    stacked = lambda name: jnp.stack([grads[name, l] for l in range(layers)])
    qkv_grad = stacked("qkv")
    out_grad = jnp.swapaxes(stacked("out")[:, :, 0], 1, 2)
    up_w_grad = stacked("up")[:, :, 0]
    down_grad = jnp.swapaxes(stacked("down")[:, :, 0], 1, 2)
    return (
        output,
        input_grad,
        qkv_grad,
        qv_grad,
        out_grad,
        out_shift,
        up_w_grad,
        up_grad,
        down_grad,
        down_shift,
        one,
        two,
    )


def solution(mesh):
    in_specs = (
        P("fsdp", "ctx", None),
        P("fsdp", None),
        P("fsdp"),
        P(None, "fsdp", None, "tp"),
        P(None, None, "tp", "fsdp"),
        P(None, "tp", "fsdp"),
        P(None, "fsdp"),
        P(None, "fsdp", "tp"),
        P(None, "tp", "fsdp"),
        P(None, "tp", "fsdp"),
        P(None, "fsdp"),
        P(None, "fsdp"),
        P(None, "fsdp"),
        P("fsdp", "ctx", None),
    )
    out_specs = (
        P("fsdp", "ctx", None),
        P("fsdp", "ctx", None),
        P(None, "fsdp", None, "tp"),
        P(None, None, "tp", "fsdp"),
        P(None, "tp", "fsdp"),
        P(None, "fsdp"),
        P(None, "fsdp", "tp"),
        P(None, "tp", "fsdp"),
        P(None, "tp", "fsdp"),
        P(None, "fsdp"),
        P(None, "fsdp"),
        P(None, "fsdp"),
    )
    return jax.shard_map(shards, mesh=mesh, in_specs=in_specs, out_specs=out_specs, check_vma=False)
```

time: 1740 us -> 1230 us (0.71)
  waiting for transfers between devices: 1220 us -> 425 us
  local copies, waits for them, and re-layouts: 90 us -> 235 us
  other arithmetic: 91.1 us -> 202 us
  starting transfers between devices: 3.31 us -> 77.2 us
  blocking collectives: 145 us -> 117 us
  matrix products: 162 us -> 144 us
    psum x8 -> x1, waiting for transfers between devices: 499 us -> 40.2 us  [shards(): lax.psum(jnp.concatenate([a.reshape(-1) for a in joined]), ('fsdp', 'ctx'...]
    unnamed x50 -> x15, waiting for transfers between devices: 298 us -> 0.76 us
    ppermute x0 -> x81, waiting for transfers between devices: none -> 205 us  [the longest x32 133 us: send_x(): return lax.ppermute(values, 'fsdp', X_PAIRS)]
    reduce_scatter x12 -> x8, waiting for transfers between devices: 274 us -> 79.1 us  [scatter_matrix(): own = lax.psum_scatter(kept, 'tp', scatter_dimension=0, tiled=False)]
    ppermute x0 -> x81, starting transfers between devices: none -> 75.7 us  [the longest x32 37.6 us: send_x(): return lax.ppermute(values, 'fsdp', X_PAIRS)]
    all_gather x6, waiting for transfers between devices: 151 us -> 100 us  [the longest x2 100 us: give_back(): return lax.all_gather(mine, 'tp', axis=0)[:slots]]
    convert_element_type x17 -> x33, other arithmetic: 20.1 us -> 64.6 us  [the longest x8 17.6 us: scatter_rows(): pass_y = (to_y[:half] + first[half:]).astype(BF)]
    rev x0 -> x11, local copies, waits for them, and re-layouts: none -> 41.1 us  [reorder(): blocks = jnp.where(place % 2 == 1, blocks[..., :, ::-1, :], blocks)]
  transfers between devices with their start and end apart: 38 -> 96, of which waited for: 34 -> 30; matrix products, arithmetic and copies ran while one was open for 10% -> 44% of each run, Pallas kernels for 0% -> 0%
where the time goes in v1:
time: 1230 us; the launch traced here: 1220 us
  waiting for transfers between devices  425 us (35%)
  local copies, waits for them, and re-layouts  235 us (19%)
  other arithmetic  202 us (16%)
  matrix products  144 us (12%)
  blocking collectives  117 us (10%)
  starting transfers between devices  77.2 us (6%)
  between operations  20.5 us (2%)
    ppermute x32, waiting for transfers between devices, send_x(): return lax.ppermute(values, 'fsdp', X_PAIRS)  133 us
    all_gather x2, waiting for transfers between devices, give_back(): return lax.all_gather(mine, 'tp', axis=0)[:slots]  100 us
    reduce_scatter x8, waiting for transfers between devices, scatter_matrix(): own = lax.psum_scatter(kept, 'tp', scatter_dimension=0, tiled=False)  79.1 us
    all_gather x4, blocking collectives, gather_matrix(): along = lax.all_gather(half, 'tp', axis=0)  77.4 us
    ppermute x32, waiting for transfers between devices, send_y(): return lax.ppermute(values, 'fsdp', Y_PAIRS)  70.7 us
    unnamed x340, local copies, waits for them, and re-layouts  62.1 us
    dot_general x8, matrix products, mm_tn(): lax.dot_general(left, right, (((0,), (0,)), ((), ())), preferred_element_...  41.4 us
    rev x11, local copies, waits for them, and re-layouts, reorder(): blocks = jnp.where(place % 2 == 1, blocks[..., :, ::-1, :], blocks)  41.1 us
  transfers between devices with their start and end apart: 96, of which 30 were waited for; matrix products, arithmetic and copies ran while one was open for 44% of the time, Pallas kernels for 0%

profile of v1, /device:TPU:0, one launch (start us, length us, event | category | flops | bytes accessed | tf_op | source)
XLA Modules:
  0.0 1220.9 jit_solution(7200938606107575798)
XLA Ops:
  11.6 16.6 %all-gather.6 = bf16[1024,1,1,128]{0,3,2,1:T(8,128)(2,1)S(1)} all-gather(bf16[256,1,1,128]{0,3,2,1:T(8,128)(2,1)S(1)} %constant_dynamic-slice_fusion.8), channel_id=8, replica_groups=mesh['fsdp'=4,'ctx'=2,'tp'=4] {'tp'}, dimensions={0}, use_global_device_ids=true | all-gather | bytes 327680 | tf_op jit(solution)/shard_map/all_gather | solution.py:87
  31.9 16.8 %all-gather.2 = bf16[1024,1,1,128]{0,3,2,1:T(8,128)(2,1)S(1)} all-gather(bf16[256,1,1,128]{0,3,2,1:T(8,128)(2,1)S(1)} %constant_dynamic-slice_fusion.12), channel_id=4, replica_groups=mesh['fsdp'=4,'ctx'=2,'tp'=4] {'tp'}, dimensions={0}, use_global_device_ids=true | all-gather | bytes 327680 | tf_op jit(solution)/shard_map/all_gather | solution.py:87
  50.7 24.3 %all-gather.5 = bf16[1024,3,1,128]{0,3,2,1:T(8,128)(2,1)S(1)} all-gather(bf16[256,3,1,128]{0,3,2,1:T(8,128)(2,1)S(1)} %constant_dynamic-slice_fusion.9), channel_id=7, replica_groups=mesh['fsdp'=4,'ctx'=2,'tp'=4] {'tp'}, dimensions={0}, use_global_device_ids=true | all-gather | bytes 983040 | tf_op jit(solution)/shard_map/all_gather | solution.py:87
  80.7 39.9 %all-gather.11 = bf16[16,1,2816]{2,1,0:T(2,128)(2,1)S(1)} all-gather(bf16[1,1,2816]{2,1,0:T(2,128)(2,1)S(1)} %reshape.1168), channel_id=2, replica_groups=mesh['fsdp'=4,'ctx'=2,'tp'=4] {'fsdp','tp'}, dimensions={0}, use_global_device_ids=true | all-gather | bytes 95744 | tf_op jit(solution)/shard_map/all_gather | solution.py:220
  126.1 19.7 %all-gather.1 = bf16[1024,3,1,128]{0,3,2,1:T(8,128)(2,1)S(1)} all-gather(bf16[256,3,1,128]{0,3,2,1:T(8,128)(2,1)S(1)} %constant_dynamic-slice_fusion.13), channel_id=3, replica_groups=mesh['fsdp'=4,'ctx'=2,'tp'=4] {'tp'}, dimensions={0}, use_global_device_ids=true | all-gather | bytes 983040 | tf_op jit(solution)/shard_map/all_gather | solution.py:87
  206.0 6.9 collective-permute-done.3
  216.1 9.2 dynamic_update_slice.3
  232.7 19.4 %rev.66 = bf16[2,592,2,2,256]{4,3,2,1,0:T(2,128)(2,1)} reverse(bf16[2,592,2,2,256]{4,3,2,1,0:T(2,128)(2,1)S(1)} %reshape.1095), dimensions={3} | reverse | bytes 4849664 | tf_op jit(solution)/shard_map/rev | solution.py:36
  325.9 27.4 %collective-permute-done.10 = bf16[256,2048]{0,1:T(8,128)(2,1)} collective-permute-done((bf16[256,2048]{0,1:T(8,128)(2,1)}, bf16[256,2048]{0,1:T(8,128)(2,1)}, u32[]{:S(2)}, u32[]{:S(2)}) %collective-permute-start.10) | collective-permute-done | bytes 1048608 | tf_op jit(solution)/shard_map/ppermute | solution.py:42
  367.4 17.2 %collective-permute-done.12 = bf16[128,2048]{0,1:T(8,128)(2,1)S(1)} collective-permute-done((bf16[128,2048]{0,1:T(8,128)(2,1)S(1)}, bf16[128,2048]{0,1:T(8,128)(2,1)S(1)}, u32[]{:S(2)}, u32[]{:S(2)}) %collective-permute-start.12) | collective-permute-done | bytes 524320 | tf_op jit(solution)/shard_map/ppermute | solution.py:46
  396.0 21.9 %collective-permute-done.16 = bf16[128,2048]{0,1:T(8,128)(2,1)S(1)} collective-permute-done((bf16[128,2048]{0,1:T(8,128)(2,1)S(1)}, bf16[128,2048]{0,1:T(8,128)(2,1)S(1)}, u32[]{:S(2)}, u32[]{:S(2)}) %collective-permute-start.16) | collective-permute-done | bytes 524320 | tf_op jit(solution)/shard_map/ppermute | solution.py:46
  430.7 14.6 %collective-permute-done.28 = bf16[256,2048]{0,1:T(8,128)(2,1)S(1)} collective-permute-done((bf16[256,2048]{0,1:T(8,128)(2,1)S(1)}, bf16[256,2048]{0,1:T(8,128)(2,1)S(1)}, u32[]{:S(2)}, u32[]{:S(2)}) %collective-permute-start.28) | collective-permute-done | bytes 1048608 | tf_op jit(solution)/shard_map/ppermute | solution.py:42
  519.2 10.9 collective-permute-done.66
  534.4 17.7 %collective-permute-done.76 = bf16[256,2048]{1,0:T(8,128)(2,1)} collective-permute-done((bf16[256,2048]{1,0:T(8,128)(2,1)}, bf16[256,2048]{1,0:T(8,128)(2,1)}, u32[]{:S(2)}, u32[]{:S(2)}) %collective-permute-start.76) | collective-permute-done | bytes 1048608 | tf_op jit(solution)/shard_map/ppermute | solution.py:42
  579.0 6.8 convert_reduce_fusion.6
  585.8 8.7 multiply_reduce_fusion.1
  623.7 12.7 %rev.76 = bf16[592,2,2,256]{3,2,1,0:T(2,128)(2,1)} reverse(bf16[592,2,2,256]{3,2,1,0:T(2,128)(2,1)} %reshape.1124), dimensions={2} | reverse | bytes 2424832 | tf_op jit(solution)/shard_map/rev | solution.py:36
  645.3 11.9 collective-permute-done.57
  713.4 6.8 convert_reduce_fusion.1
  724.0 6.7 fusion.141
  751.3 11.4 collective-permute-done.61
  768.2 16.3 %collective-permute-done.71 = bf16[256,2048]{1,0:T(8,128)(2,1)} collective-permute-done((bf16[256,2048]{1,0:T(8,128)(2,1)}, bf16[256,2048]{1,0:T(8,128)(2,1)}, u32[]{:S(2)}, u32[]{:S(2)}) %collective-permute-start.71) | collective-permute-done | bytes 1048608 | tf_op jit(solution)/shard_map/ppermute | solution.py:42
  812.1 8.8 multiply_reduce_fusion
  862.9 8.2 collective-permute-done.54
  891.9 13.0 %collective-permute-done.41 = bf16[256,1536]{1,0:T(8,128)(2,1)} collective-permute-done((bf16[256,1536]{1,0:T(8,128)(2,1)}, bf16[256,1536]{1,0:T(8,128)(2,1)}, u32[]{:S(2)}, u32[]{:S(2)}) %collective-permute-start.41) | collective-permute-done | bytes 786464 | tf_op jit(solution)/shard_map/ppermute | solution.py:42
  949.8 8.2 rev.78
  975.0 40.2 %all-reduce.5.cloned.1.call-done = f32[20480]{0:T(1024)} async-done(((f32[20480]{0:T(1024)}), f32[20480]{0:T(1024)}) %all-reduce.5.cloned.1.call-update) | async-done | bytes 81936 | tf_op jit(solution)/shard_map/psum | solution.py:293
  1016.0 30.6 %reduce-scatter.21.cloned.1.call-done = bf16[1,256,1,512]{3,1,2,0:T(8,128)(2,1)} async-done(((bf16[4,256,1,512]{3,1,2,0:T(8,128)(2,1)}), bf16[1,256,1,512]{3,1,2,0:T(8,128)(2,1)}) %reduce-scatter.21.cloned.1.call-update) | async-done | bytes 262160 | tf_op jit(solution)/shard_map/reduce_scatter | solution.py:97
  1051.6 23.6 %reduce-scatter.17.cloned.1.call-done = bf16[1,256,1,512]{3,1,2,0:T(8,128)(2,1)} async-done(((bf16[4,256,1,512]{3,1,2,0:T(8,128)(2,1)}), bf16[1,256,1,512]{3,1,2,0:T(8,128)(2,1)}) %reduce-scatter.17.cloned.1.call-update) | async-done | bytes 262160 | tf_op jit(solution)/shard_map/reduce_scatter | solution.py:97
  1075.2 24.9 %reduce-scatter.9.cloned.1.call-done = bf16[1,256,3,128]{3,1,2,0:T(8,128)(2,1)} async-done(((bf16[4,256,3,128]{3,1,2,0:T(8,128)(2,1)}), bf16[1,256,3,128]{3,1,2,0:T(8,128)(2,1)}) %reduce-scatter.9.cloned.1.call-update) | async-done | bytes 196624 | tf_op jit(solution)/shard_map/reduce_scatter | solution.py:97
  1108.1 48.1 %all-gather.29.cloned.1.call-done = bf16[1280,1024]{1,0:T(8,128)(2,1)} async-done(((bf16[320,1024]{1,0:T(8,128)(2,1)}), bf16[1280,1024]{1,0:T(8,128)(2,1)}) %all-gather.29.cloned.1.call-update) | async-done | bytes 2621456 | tf_op jit(solution)/shard_map/all_gather | solution.py:268
  1159.1 52.1 %all-gather.27.cloned.1.call-done = bf16[1280,1024]{1,0:T(8,128)(2,1)} async-done(((bf16[320,1024]{1,0:T(8,128)(2,1)}), bf16[1280,1024]{1,0:T(8,128)(2,1)}) %all-gather.27.cloned.1.call-update) | async-done | bytes 2621456 | tf_op jit(solution)/shard_map/all_gather | solution.py:268
  (897 shorter events, 599.2 us)
Async XLA Ops:
  7.2 292.2 %all-gather.21.cloned.1.call-start = ((), (), s32[]{:S(2)}) async-start(), calls=%async_computation.18 | async-start | bytes 1310720 | tf_op jit(solution)/shard_map/all_gather | solution.py:87
  9.4 297.6 %all-gather.19.cloned.1.call-start = ((), (), s32[]{:S(2)}) async-start(), calls=%async_computation.17 | async-start | bytes 1310720 | tf_op jit(solution)/shard_map/all_gather | solution.py:87
  10.5 300.2 %all-gather.23.cloned.1.call-start = ((), (), s32[]{:S(2)}) async-start(), calls=%async_computation.19 | async-start | bytes 1310720 | tf_op jit(solution)/shard_map/all_gather | solution.py:87
  11.5 302.9 %all-gather.25.cloned.1.call-start = ((), (), s32[]{:S(2)}) async-start(), calls=%async_computation.20 | async-start | bytes 1310720 | tf_op jit(solution)/shard_map/all_gather | solution.py:87
  28.6 124.0 %collective-permute-start.24 = (bf16[256,512]{0,1:T(8,128)(2,1)S(1)}, bf16[256,512]{0,1:T(8,128)(2,1)}, u32[]{:S(2)}, u32[]{:S(2)}) collective-permute-start(bf16[256,512]{0,1:T(8,128)(2,1)S(1)} %bitcast.413), channel_id=1, source_target_pairs={{0,16},{16,0},{8,24},{24,8},{1,17},{17,1},{9,25},{25,9},{2,18},{18... | collective-permute-start | bytes 786440 | tf_op jit(solution)/shard_map/ppermute | solution.py:46
  30.3 132.3 %collective-permute-start.23 = (bf16[256,512]{0,1:T(8,128)(2,1)S(1)}, bf16[256,512]{0,1:T(8,128)(2,1)}, u32[]{:S(2)}, u32[]{:S(2)}) collective-permute-start(bf16[256,512]{0,1:T(8,128)(2,1)S(1)} %bitcast.414), channel_id=1, source_target_pairs={{0,8},{8,0},{16,24},{24,16},{1,9},{9,1},{17,25},{25,17},{2,10},{10... | collective-permute-start | bytes 786440 | tf_op jit(solution)/shard_map/ppermute | solution.py:42
  49.0 116.7 %collective-permute-start.6 = (bf16[256,512]{0,1:T(8,128)(2,1)S(1)}, bf16[256,512]{0,1:T(8,128)(2,1)}, u32[]{:S(2)}, u32[]{:S(2)}) collective-permute-start(bf16[256,512]{0,1:T(8,128)(2,1)S(1)} %bitcast.410), channel_id=1, source_target_pairs={{0,16},{16,0},{8,24},{24,8},{1,17},{17,1},{9,25},{25,9},{2,18},{18... | collective-permute-start | bytes 786440 | tf_op jit(solution)/shard_map/ppermute | solution.py:46
  49.6 119.0 %collective-permute-start.5 = (bf16[256,512]{0,1:T(8,128)(2,1)S(1)}, bf16[256,512]{0,1:T(8,128)(2,1)}, u32[]{:S(2)}, u32[]{:S(2)}) collective-permute-start(bf16[256,512]{0,1:T(8,128)(2,1)S(1)} %bitcast.411), channel_id=1, source_target_pairs={{0,8},{8,0},{16,24},{24,16},{1,9},{9,1},{17,25},{25,17},{2,10},{10... | collective-permute-start | bytes 786440 | tf_op jit(solution)/shard_map/ppermute | solution.py:42
  75.6 115.4 %collective-permute-start.20 = (bf16[256,1536]{0,1:T(8,128)(2,1)S(1)}, bf16[256,1536]{0,1:T(8,128)(2,1)}, u32[]{:S(2)}, u32[]{:S(2)}) collective-permute-start(bf16[256,1536]{0,1:T(8,128)(2,1)S(1)} %bitcast.384), channel_id=1, source_target_pairs={{0,16},{16,0},{8,24},{24,8},{1,17},{17,1},{9,25},{25,9},{2,18},{18... | collective-permute-start | bytes 2359304 | tf_op jit(solution)/shard_map/ppermute | solution.py:46
  77.8 889.2 %reduce-scatter.15.cloned.1.call-start = ((), (), s32[]{:S(2)}) async-start(), calls=%async_computation.12 | async-start | bytes 327680 | tf_op jit(solution)/shard_map/reduce_scatter | solution.py:97
  192.8 97.3 %collective-permute-start.22 = (bf16[128,1536]{0,1:T(8,128)(2,1)}, bf16[128,1536]{0,1:T(8,128)(2,1)S(1)}, u32[]{:S(2)}, u32[]{:S(2)}) collective-permute-start(bf16[128,1536]{0,1:T(8,128)(2,1)} %slice.877), channel_id=1, source_target_pairs={{0,8},{8,0},{16,24},{24,16},{1,9},{9,1},{17,25},{25,17},{2,10},{10... | collective-permute-start | bytes 1179656 | tf_op jit(solution)/shard_map/ppermute | solution.py:42
  302.2 59.9 %collective-permute-start.15 = (bf16[256,2048]{0,1:T(8,128)(2,1)}, bf16[256,2048]{0,1:T(8,128)(2,1)}, u32[]{:S(2)}, u32[]{:S(2)}) collective-permute-start(bf16[256,2048]{0,1:T(8,128)(2,1)} %bitcast.41), channel_id=1, source_target_pairs={{0,16},{16,0},{8,24},{24,8},{1,17},{17,1},{9,25},{25,9},{2,18},{18... | collective-permute-start | bytes 3145736 | tf_op jit(solution)/shard_map/ppermute | solution.py:46
  321.8 102.9 %collective-permute-start.33 = (bf16[256,2048]{0,1:T(8,128)(2,1)S(1)}, bf16[256,2048]{0,1:T(8,128)(2,1)S(1)}, u32[]{:S(2)}, u32[]{:S(2)}) collective-permute-start(bf16[256,2048]{0,1:T(8,128)(2,1)S(1)} %bitcast.377), channel_id=1, source_target_pairs={{0,16},{16,0},{8,24},{24,8},{1,17},{17,1},{9,25},{25,9},{2,18},{18... | collective-permute-start | bytes 3145736 | tf_op jit(solution)/shard_map/ppermute | solution.py:46
  353.3 72.3 %collective-permute-start.32 = (bf16[256,2048]{0,1:T(8,128)(2,1)S(1)}, bf16[256,2048]{0,1:T(8,128)(2,1)S(1)}, u32[]{:S(2)}, u32[]{:S(2)}) collective-permute-start(bf16[256,2048]{0,1:T(8,128)(2,1)S(1)} %bitcast.378), channel_id=1, source_target_pairs={{0,8},{8,0},{16,24},{24,16},{1,9},{9,1},{17,25},{25,17},{2,10},{10... | collective-permute-start | bytes 3145736 | tf_op jit(solution)/shard_map/ppermute | solution.py:42
  359.6 68.2 %collective-permute-start.29 = (bf16[256,2048]{0,1:T(8,128)(2,1)S(1)}, bf16[256,2048]{0,1:T(8,128)(2,1)S(1)}, u32[]{:S(2)}, u32[]{:S(2)}) collective-permute-start(bf16[256,2048]{0,1:T(8,128)(2,1)S(1)} %bitcast.374), channel_id=1, source_target_pairs={{0,16},{16,0},{8,24},{24,8},{1,17},{17,1},{9,25},{25,9},{2,18},{18... | collective-permute-start | bytes 3145736 | tf_op jit(solution)/shard_map/ppermute | solution.py:46
  500.8 63.4 %collective-permute-start.37 = (bf16[592,1024]{1,0:T(8,128)(2,1)}, bf16[592,1024]{1,0:T(8,128)(2,1)}, u32[]{:S(2)}, u32[]{:S(2)}) collective-permute-start(bf16[592,1024]{1,0:T(8,128)(2,1)} %convolution_convert_fusion.1), channel_id=1, source_target_pairs={{0,4},{4,0},{1,5},{5,1},{2,6},{6,2},{3,7},{7,3},{8,12},{12,8},{9,1... | collective-permute-start | bytes 3637256 | tf_op jit(solution)/shard_map/ppermute | solution.py:50
  502.0 55.8 %collective-permute-start.68 = (bf16[256,2048]{1,0:T(8,128)(2,1)}, bf16[256,2048]{1,0:T(8,128)(2,1)}, u32[]{:S(2)}, u32[]{:S(2)}) collective-permute-start(bf16[256,2048]{1,0:T(8,128)(2,1)} %pad_maximum_fusion.6), channel_id=1, source_target_pairs={{0,16},{16,0},{8,24},{24,8},{1,17},{17,1},{9,25},{25,9},{2,18},{18... | collective-permute-start | bytes 3145736 | tf_op jit(solution)/shard_map/ppermute | solution.py:46
  552.1 89.4 %collective-permute-start.67 = (bf16[128,2048]{1,0:T(8,128)(2,1)}, bf16[128,2048]{1,0:T(8,128)(2,1)}, u32[]{:S(2)}, u32[]{:S(2)}) collective-permute-start(bf16[128,2048]{1,0:T(8,128)(2,1)} %fusion.48), channel_id=1, source_target_pairs={{0,16},{16,0},{8,24},{24,8},{1,17},{17,1},{9,25},{25,9},{2,18},{18... | collective-permute-start | bytes 1572872 | tf_op jit(solution)/shard_map/ppermute | solution.py:46
  557.9 116.2 %collective-permute-start.77 = (bf16[128,2048]{1,0:T(8,128)(2,1)}, bf16[128,2048]{1,0:T(8,128)(2,1)}, u32[]{:S(2)}, u32[]{:S(2)}) collective-permute-start(bf16[128,2048]{1,0:T(8,128)(2,1)} %fusion.36), channel_id=1, source_target_pairs={{0,16},{16,0},{8,24},{24,8},{1,17},{17,1},{9,25},{25,9},{2,18},{18... | collective-permute-start | bytes 1572872 | tf_op jit(solution)/shard_map/ppermute | solution.py:46
  668.6 298.6 %reduce-scatter.19.cloned.1.call-start = ((), (), s32[]{:S(2)}) async-start(), calls=%async_computation.14 | async-start | bytes 1310720 | tf_op jit(solution)/shard_map/reduce_scatter | solution.py:97
  674.0 293.7 %reduce-scatter.23.cloned.1.call-start = ((), (), s32[]{:S(2)}) async-start(), calls=%async_computation.16 | async-start | bytes 1310720 | tf_op jit(solution)/shard_map/reduce_scatter | solution.py:97
  695.8 273.6 %reduce-scatter.11.cloned.1.call-start = ((), (), s32[]{:S(2)}) async-start(), calls=%async_computation.9 | async-start | bytes 983040 | tf_op jit(solution)/shard_map/reduce_scatter | solution.py:97
  731.6 64.0 %collective-permute-start.39 = (bf16[592,1024]{1,0:T(8,128)(2,1)}, bf16[592,1024]{1,0:T(8,128)(2,1)}, u32[]{:S(2)}, u32[]{:S(2)}) collective-permute-start(bf16[592,1024]{1,0:T(8,128)(2,1)} %convolution_convert_fusion), channel_id=1, source_target_pairs={{0,4},{4,0},{1,5},{5,1},{2,6},{6,2},{3,7},{7,3},{8,12},{12,8},{9,1... | collective-permute-start | bytes 3637256 | tf_op jit(solution)/shard_map/ppermute | solution.py:50
  751.0 220.7 %reduce-scatter.13.cloned.1.call-start = ((), (), s32[]{:S(2)}) async-start(), calls=%async_computation.11 | async-start | bytes 327680 | tf_op jit(solution)/shard_map/reduce_scatter | solution.py:97
  767.1 118.3 %collective-permute-start.62 = (bf16[128,2048]{1,0:T(8,128)(2,1)}, bf16[128,2048]{1,0:T(8,128)(2,1)}, u32[]{:S(2)}, u32[]{:S(2)}) collective-permute-start(bf16[128,2048]{1,0:T(8,128)(2,1)} %fusion.54), channel_id=1, source_target_pairs={{0,16},{16,0},{8,24},{24,8},{1,17},{17,1},{9,25},{25,9},{2,18},{18... | collective-permute-start | bytes 1572872 | tf_op jit(solution)/shard_map/ppermute | solution.py:46
  788.8 64.1 %collective-permute-start.72 = (bf16[128,2048]{1,0:T(8,128)(2,1)}, bf16[128,2048]{1,0:T(8,128)(2,1)}, u32[]{:S(2)}, u32[]{:S(2)}) collective-permute-start(bf16[128,2048]{1,0:T(8,128)(2,1)} %fusion.42), channel_id=1, source_target_pairs={{0,16},{16,0},{8,24},{24,8},{1,17},{17,1},{9,25},{25,9},{2,18},{18... | collective-permute-start | bytes 1572872 | tf_op jit(solution)/shard_map/ppermute | solution.py:46
  873.7 141.4 %all-reduce.5.cloned.1.call-start = ((), (), s32[]{:S(2)}) async-start(), calls=%async_computation.10 | async-start | bytes 163840 | tf_op jit(solution)/shard_map/psum | solution.py:293
  880.7 165.8 %reduce-scatter.21.cloned.1.call-start = ((), (), s32[]{:S(2)}) async-start(), calls=%async_computation.15 | async-start | bytes 1310720 | tf_op jit(solution)/shard_map/reduce_scatter | solution.py:97
  881.9 193.3 %reduce-scatter.17.cloned.1.call-start = ((), (), s32[]{:S(2)}) async-start(), calls=%async_computation.13 | async-start | bytes 1310720 | tf_op jit(solution)/shard_map/reduce_scatter | solution.py:97
  917.8 182.3 %reduce-scatter.9.cloned.1.call-start = ((), (), s32[]{:S(2)}) async-start(), calls=%async_computation.8 | async-start | bytes 983040 | tf_op jit(solution)/shard_map/reduce_scatter | solution.py:97
  943.2 213.0 %all-gather.29.cloned.1.call-start = ((), (), s32[]{:S(2)}) async-start(), calls=%async_computation.22 | async-start | bytes 3276800 | tf_op jit(solution)/shard_map/all_gather | solution.py:268
  966.4 244.8 %all-gather.27.cloned.1.call-start = ((), (), s32[]{:S(2)}) async-start(), calls=%async_computation.21 | async-start | bytes 3276800 | tf_op jit(solution)/shard_map/all_gather | solution.py:268
  (197 other events, 3125.2 us)
Sparse Core Ops, SparseCore 0:
  10.2 36.8 all-gather.20
  49.2 35.7 all-gather.18
  87.1 36.1 all-gather.22
  124.8 30.8 all-gather.24
  668.7 17.1 reduce-scatter.14
  688.1 25.3 reduce-scatter.18
  715.8 25.7 reduce-scatter.22
  751.1 20.8 reduce-scatter.10
  873.8 17.9 reduce-scatter.12
  897.3 117.8 all-reduce.4
  1017.4 29.0 reduce-scatter.20
  1049.4 25.7 reduce-scatter.16
  1078.1 21.9 reduce-scatter.8
  1102.1 54.0 all-gather.28
  1157.6 53.5 all-gather.26

commit v2 on v1

v2 whole, which is shorter than its diff:
```python
import jax
import jax.numpy as jnp
from jax import lax
from jax.sharding import PartitionSpec as P

HD = 64
SEQ = 577
BF = jnp.bfloat16
F32 = jnp.float32


def layer_norm(vectors, scaling):
    centre = vectors - jnp.mean(vectors, axis=-1, keepdims=True)
    spread = jnp.mean(centre * centre, axis=-1, keepdims=True)
    return centre * lax.rsqrt(spread + 1e-06) * scaling


def gelu_exact(values):
    return 0.5 * values * (1.0 + lax.erf(values * 0.7071067811865476))


X_PAIRS = [(0, 1), (1, 0), (2, 3), (3, 2)]
Y_PAIRS = [(0, 2), (2, 0), (1, 3), (3, 1)]
BLOCKS = ((0, 0), (0, 1), (1, 1), (2, 0), (1, 0), (3, 0), (3, 1), (2, 1))


def square():
    return lax.axis_size("fsdp") == 4


def order_matrix(features):
    if not square():
        return None
    half = features // 8
    group = lax.axis_index("fsdp")
    starts = jnp.stack([((group ^ other) * 2 + part) * half for other, part in BLOCKS])
    natural = (starts[:, None] + jnp.arange(half)[None]).reshape(-1)
    return (jnp.arange(features)[:, None] == natural[None]).astype(BF)


def send_x(values):
    return lax.ppermute(values, "fsdp", X_PAIRS)


def send_y(values):
    return lax.ppermute(values, "fsdp", Y_PAIRS)


def swap(values):
    return lax.ppermute(values, "ctx", [(0, 1), (1, 0)])


def both_cores(partial_sum):
    low = partial_sum.astype(BF)
    return low.astype(F32) + swap(low).astype(F32)


def gather_line(shard):
    count, lane = lax.axis_size("tp"), lax.axis_index("tp")
    up_pairs = [(j, j + 1) for j in range(count - 1)]
    down_pairs = [(j + 1, j) for j in range(count - 1)]
    lower, upper = [shard], [shard]
    for step in range(count - 1):
        lower.append(lax.ppermute(lower[-1], "tp", up_pairs[step:]))
        upper.append(lax.ppermute(upper[-1], "tp", down_pairs[: count - 1 - step]))
    placed = []
    for owner in range(count):
        piece = shard
        for away in range(1, count):
            piece = jnp.where(lane == owner + away, lower[away], piece)
            piece = jnp.where(lane == owner - away, upper[away], piece)
        placed.append(piece)
    return jnp.stack(placed)


def scatter_line(full):
    count, lane = lax.axis_size("tp"), lax.axis_index("tp")
    take = lambda k: lax.dynamic_index_in_dim(full, jnp.clip(k, 0, count - 1), 0, keepdims=False)
    rising = falling = None
    for step in range(count - 1):
        to_up, to_down = take(lane + count - 1 - step), take(lane - (count - 1 - step))
        if step:
            to_up, to_down = to_up + rising, to_down + falling
        rising = lax.ppermute(to_up, "tp", [(j, j + 1) for j in range(step + 1)])
        falling = lax.ppermute(to_down, "tp", [(j + 1, j) for j in range(count - 2 - step, count - 1)])
    return (take(lane).astype(F32) + rising.astype(F32) + falling.astype(F32)).astype(BF)


def gather_features(shard):
    if not square():
        return [lax.all_gather(shard, "fsdp", axis=1, tiled=True)]
    half = shard.shape[1] // 2
    from_x, from_y = send_x(shard), send_y(shard)
    far_a, far_b = send_y(from_x[:, :half]), send_x(from_y[:, half:])
    return [shard, from_x[:, half:], from_y[:, :half], from_x[:, :half], far_a, far_b, from_y[:, half:]]


def gradient_rows(delta, values):
    if not square():
        return lax.psum_scatter(mm_tn(delta, values).astype(BF), "fsdp", scatter_dimension=1, tiled=True)
    half = values.shape[1] // 8
    to_x = mm_tn(delta, values[:, 4 * half : 6 * half]).astype(BF)
    from_x = send_x(to_x)
    to_y = mm_tn(delta, values[:, 6 * half :]).astype(BF)
    from_y = send_y(to_y)
    own_a, own_b, x_b, y_a = jnp.split(mm_tn(delta, values[:, : 4 * half]).astype(BF), 4, axis=1)
    last_a = send_y(y_a + from_x[:, half:])
    last_b = send_x(x_b + from_y[:, :half])
    add = lambda *terms: sum(term.astype(F32) for term in terms).astype(BF)
    return jnp.concatenate([add(own_a, from_x[:, :half], last_a), add(own_b, from_y[:, half:], last_b)], axis=1)


def gather_group(shards):
    count = lax.axis_size("tp")
    heights = [shard.shape[0] for shard in shards]
    along = gather_line(jnp.concatenate(shards, axis=0))
    pieces = gather_features(along.reshape(-1, along.shape[-1]))
    pieces = [piece.reshape(count, -1, piece.shape[-1]) for piece in pieces]
    result, start = [], 0
    for height in heights:
        cut = [piece[:, start : start + height].reshape(count * height, -1) for piece in pieces]
        result.append(jnp.concatenate(cut, axis=1))
        start += height
    return result


def heads_of(values):
    return values.reshape(values.shape[0], -1, HD)


def masked_scores(queries, keys, key_valid):
    scores = jnp.einsum("qhd,khd->hqk", queries, keys, preferred_element_type=F32) * HD ** (-0.5)
    return jnp.where(key_valid, scores, -1000000000.0)


def mm(left, right):
    return jnp.dot(left, right, preferred_element_type=F32)


def mm_nt(left, right):
    return lax.dot_general(left, right, (((1,), (1,)), ((), ())), preferred_element_type=F32)


def mm_tn(left, right):
    return lax.dot_general(left, right, (((0,), (0,)), ((), ())), preferred_element_type=F32)


def forward_layer(stream, weights, vectors, key_valid):
    qkv, out, up, down = weights
    shift_q, shift_v, out_shift, up_shift, down_shift, gain_first, gain_second = vectors
    normed = layer_norm(stream, gain_first).astype(BF)
    project = mm_nt(normed, qkv)
    width = project.shape[1] // 3
    tile = width // lax.axis_size("tp")
    member = lambda k: jnp.concatenate(
        [project[:, c : c + tile] for c in range(k * tile, 3 * width, 3 * tile)], axis=1
    )
    queries = heads_of((member(0) + shift_q).astype(BF))
    keys = heads_of(member(1).astype(BF))
    values = heads_of((member(2) + shift_v).astype(BF))
    scores = masked_scores(queries, keys, key_valid)
    highest = jnp.max(scores, axis=-1, keepdims=True)
    exponent = jnp.exp(scores - highest)
    denominator = jnp.sum(exponent, axis=-1, keepdims=True)
    probs = (exponent / denominator).astype(BF)
    log_total = highest + jnp.log(denominator)
    mixed = jnp.einsum("hqk,khd->qhd", probs, values, preferred_element_type=F32).astype(BF)
    mixed = mixed.reshape(stream.shape[0], width)
    middle = stream + both_cores(mm(mixed, out)) + out_shift
    normed_b = layer_norm(middle, gain_second).astype(BF)
    hidden = mm_nt(normed_b, up) + up_shift
    active = gelu_exact(hidden).astype(BF)
    following = middle + both_cores(mm(active, down)) + down_shift
    return following, (stream, normed, queries, keys, values, log_total, mixed, middle, normed_b, hidden, active)


def backward_layer(gradient, saved, weights, vectors, key_valid, emit):
    qkv, out, up, down = weights
    gain_first, gain_second = vectors[5:]
    stream, normed, queries, keys, values, log_total, mixed, middle, normed_b, hidden, active = saved
    total = lambda array: jnp.sum(array.astype(F32), axis=0)
    grad_low = gradient.astype(BF)
    emit("down", active, grad_low)
    delta_hidden = jax.vjp(gelu_exact, hidden)[1](mm_nt(grad_low, down))[0].astype(BF)
    emit("up", delta_hidden, normed_b)
    delta_normed_b = both_cores(mm(delta_hidden, up))
    back_middle, delta_gain_second = jax.vjp(layer_norm, middle, gain_second)[1](delta_normed_b)
    grad_middle = gradient + back_middle
    grad_attend = grad_middle.astype(BF)
    emit("out", mixed, grad_attend)
    delta_mixed = heads_of(mm_nt(grad_attend, out).astype(BF))
    probs = jnp.exp(masked_scores(queries, keys, key_valid) - log_total)
    delta_values = jnp.einsum("hqk,qhd->khd", probs.astype(BF), delta_mixed, preferred_element_type=F32).astype(BF)
    delta_probs = jnp.einsum("qhd,khd->hqk", delta_mixed, values, preferred_element_type=F32)
    inner = jnp.sum(probs * delta_probs, axis=-1, keepdims=True)
    delta_scores = (probs * (delta_probs - inner)).astype(BF)
    scale = HD ** (-0.5)
    delta_queries = (jnp.einsum("hqk,khd->qhd", delta_scores, keys, preferred_element_type=F32) * scale).astype(BF)
    delta_keys = (jnp.einsum("hqk,qhd->khd", delta_scores, queries, preferred_element_type=F32) * scale).astype(BF)
    flat = [piece.reshape(stream.shape[0], -1) for piece in (delta_queries, delta_keys, delta_values)]
    width = flat[0].shape[1]
    tile = width // lax.axis_size("tp")
    delta_project = jnp.concatenate([piece[:, c : c + tile] for c in range(0, width, tile) for piece in flat], axis=1)
    emit("qkv", delta_project, normed)
    delta_normed = both_cores(mm(delta_project, qkv))
    back_stream, delta_gain_first = jax.vjp(layer_norm, stream, gain_first)[1](delta_normed)
    sums = (
        total(flat[0]),
        total(flat[2]),
        total(grad_attend),
        total(delta_hidden),
        total(grad_low),
        delta_gain_first,
        delta_gain_second,
    )
    return grad_middle + back_stream, sums


def shards(
    tokens,
    lengths,
    image_count,
    qkv_weight,
    qv_bias,
    out_weight,
    out_bias,
    up_weight,
    up_bias,
    down_weight,
    down_bias,
    gain_one,
    gain_two,
    cotangent,
):
    slots, capacity, features = tokens.shape
    layers = qkv_weight.shape[0]
    n_fsdp, n_tp = lax.axis_size("fsdp"), lax.axis_size("tp")
    assert lax.axis_size("ctx") == 2 and slots <= n_tp
    group, core, lane = lax.axis_index("fsdp"), lax.axis_index("ctx"), lax.axis_index("tp")
    rows = -(-SEQ // 16) * 16
    slot = jnp.minimum(lane, slots - 1)
    own_lengths = lax.dynamic_index_in_dim(lengths, slot, 0, keepdims=False)
    live = lane < jnp.minimum(image_count[0], slots)
    key_valid = (jnp.arange(rows) < SEQ)[None, None, :]
    row_mask = ((jnp.arange(rows) < SEQ) & live).astype(F32)[:, None]
    halves = lambda array, axis: lax.dynamic_index_in_dim(
        array.reshape(array.shape[:axis] + (2, -1) + array.shape[axis + 1 :]), core, axis, keepdims=False
    )

    cut = []
    for l in range(layers):
        qkv = jnp.transpose(halves(qkv_weight[l], 2), (1, 2, 0)).reshape(-1, qkv_weight.shape[1])
        cut.append((qkv, halves(out_weight[l], 0), halves(up_weight[l], 1).T, halves(down_weight[l], 0)))
    first_qkv = gather_group([cut[0][0]])

    pieces = (qv_bias, up_bias, out_bias, down_bias, gain_one, gain_two)
    packed = jnp.concatenate([piece.reshape(1, -1) for piece in pieces], axis=1)
    if square():
        near_x, near_y = send_x(packed), send_y(packed)
        found = jnp.concatenate([packed, near_x, near_y, send_y(near_x)])
        natural = [lax.dynamic_index_in_dim(found, group ^ k, 0, keepdims=False) for k in range(4)]
        spread = jnp.stack(natural)
    else:
        spread = lax.all_gather(packed[0], "fsdp", axis=0)
    order = order_matrix(features)
    split = qv_bias.size + up_bias.size
    across = gather_line(spread[:, :split])

    def by_core(array, count):
        array = array.reshape(n_tp, n_fsdp, layers, count, -1)
        array = jnp.transpose(array, (2, 3, 0, 1, 4)).reshape(layers, count, n_tp, 2, -1)
        return lax.dynamic_index_in_dim(array, core, 3, keepdims=False).reshape(layers, count, -1)

    qv_all = by_core(across[:, :, : qv_bias.size], 2)
    up_all = by_core(across[:, :, qv_bias.size :], 1)
    by_feature = jnp.transpose(spread[:, split:].reshape(n_fsdp, 4, layers, -1), (1, 2, 0, 3)).reshape(4 * layers, features)
    if order is not None:
        by_feature = mm(by_feature, order)
    by_feature = by_feature.astype(F32).reshape(4, layers, features)
    out_all, down_all, one_all, two_all = by_feature[0], by_feature[1], by_feature[2], by_feature[3]
    vectors = [
        (qv_all[l, 0], qv_all[l, 1], out_all[l], up_all[l, 0], down_all[l], one_all[l], two_all[l])
        for l in range(layers)
    ]

    own_pair = [lax.dynamic_index_in_dim(a, slot, 0, keepdims=False) for a in (tokens, cotangent)]
    own_pair = jnp.concatenate(own_pair, axis=1)
    pair = jnp.concatenate([own_pair, swap(own_pair)], axis=0)
    row = jnp.arange(rows)
    in_first = row < own_lengths[0]
    position = jnp.where(in_first, row, row - own_lengths[0])
    source = position + capacity * (jnp.where(in_first, 0, 1) != core)
    pick_rows = ((jnp.arange(2 * capacity)[None] == source[:, None]) & (row < SEQ)[:, None]).astype(BF)
    packed_pair = mm(pick_rows, pair).astype(BF)
    image = [packed_pair[:, :features], packed_pair[:, features:]]
    if order is not None:
        image = [mm(half, order) for half in image]
    stream = image[0].astype(F32)
    gradient = image[1].astype(F32) * row_mask

    weights = [tuple(first_qkv + gather_group(cut[0][1:3]) + gather_group(cut[0][3:]))]
    for l in range(1, layers):
        weights.append(tuple(gather_group(cut[l][:2]) + gather_group(cut[l][2:])))

    saved = []
    for l in range(layers):
        stream, items = forward_layer(stream, weights[l], vectors[l], key_valid)
        saved.append(items)

    place = jnp.arange(capacity)
    target = place + jnp.where(core == 0, 0, own_lengths[0])
    pick_back = (row[None] == target[:, None]) & ((place < own_lengths[core]) & live)[:, None]
    pick_back = pick_back.astype(BF)

    def give_back(values):
        values = values.astype(BF)
        if order is not None:
            values = mm_nt(values, order).astype(BF)
        return lax.all_gather(mm(pick_back, values).astype(BF), "tp", axis=0)[:slots]

    output = give_back(stream)
    names = ("down", "up", "out", "qkv")
    found = {}
    sums = [None] * layers
    mine = [None] * layers
    for l in reversed(range(layers)):

        def emit(name, delta, values):
            found[name] = gradient_rows(delta, values).reshape(n_tp, -1, features // n_fsdp)

        if l == layers - 2:
            gradient, output = lax.optimization_barrier((gradient, output))
        gradient, sums[l] = backward_layer(gradient, saved[l], weights[l], vectors[l], key_valid, emit)
        together = lambda some: jnp.concatenate([found[name] for name in some], axis=1)
        if l > 0:
            mine[l] = lax.psum_scatter(together(names), "tp", scatter_dimension=0, tiled=False)
        else:
            early = lax.psum_scatter(together(names[:2]), "tp", scatter_dimension=0, tiled=False)
            mine[l] = jnp.concatenate([early, scatter_line(together(names[2:]))], axis=0)
    input_grad = give_back(gradient)

    grads = {name: [] for name in names}
    heights = [2 * found[name].shape[1] // 2 for name in names]
    for l in range(layers):
        other = swap(mine[l])
        low = jnp.where(core == 0, mine[l], other)
        high = jnp.where(core == 0, other, mine[l])
        start = 0
        for name, height in zip(names, heights):
            grads[name].append((low[start : start + height], high[start : start + height]))
            start += height
    rows_joined = lambda name: jnp.stack([jnp.concatenate(p, axis=0) for p in grads[name]]).astype(F32)
    turned = lambda name: jnp.stack([jnp.concatenate([h.T for h in p], axis=1) for p in grads[name]]).astype(F32)
    depth = features // n_fsdp
    qkv_grad = jnp.stack(
        [
            jnp.concatenate([jnp.transpose(h.reshape(3, -1, depth), (2, 0, 1)) for h in p], axis=2)
            for p in grads["qkv"]
        ]
    ).astype(F32)

    def from_core(array, count):
        array = array.reshape(layers, count, n_tp, 1, -1)
        mask = (jnp.arange(2) == core)[:, None]
        return jnp.where(mask, array, 0.0).reshape(-1)

    first = (core == 0).astype(F32)
    member = lambda k: jnp.stack([sums[l][k] for l in range(layers)])
    by_feature = jnp.stack([member(k) for k in (2, 4, 5, 6)]).reshape(4 * layers, features) * first
    if order is not None:
        by_feature = lax.dot_general(
            by_feature, order.astype(F32), (((1,), (1,)), ((), ())), precision=lax.Precision.HIGHEST
        )
    joined = [
        from_core(jnp.stack([member(0), member(1)], axis=1), 2),
        from_core(member(3)[:, None], 1),
        by_feature.reshape(-1),
    ]
    summed = jnp.concatenate(joined).reshape(-1, 128)
    if square() and n_tp == 4:
        summed = summed + swap(summed)
        summed = summed + send_x(summed)
        summed = summed + send_y(summed)
        summed = summed + lax.ppermute(summed, "tp", [(0, 1), (1, 0), (2, 3), (3, 2)])
        summed = summed + lax.ppermute(summed, "tp", [(0, 2), (2, 0), (1, 3), (3, 1)])
    else:
        summed = lax.psum(summed, ("fsdp", "ctx", "tp"))
    summed = summed.reshape(-1)
    pick = lambda a, i, axis: lax.dynamic_index_in_dim(a, i, axis, keepdims=True)
    ends = (joined[0].size, joined[0].size + joined[1].size)
    qv_grad = pick(pick(summed[: ends[0]].reshape(layers, 2, n_tp, n_fsdp, -1), lane, 2), group, 3)[:, :, :, 0]
    up_grad = pick(pick(summed[ends[0] : ends[1]].reshape(layers, n_tp, n_fsdp, -1), lane, 1), group, 2)[:, :, 0]
    out_shift, down_shift, one, two = pick(summed[ends[1] :].reshape(4, layers, n_fsdp, -1), group, 2)[:, :, 0]
    return (
        output,
        input_grad,
        qkv_grad,
        qv_grad,
        rows_joined("out"),
        out_shift,
        turned("up"),
        up_grad,
        rows_joined("down"),
        down_shift,
        one,
        two,
    )


def solution(mesh):
    in_specs = (
        P("fsdp", "ctx", None),
        P("fsdp", None),
        P("fsdp"),
        P(None, "fsdp", None, "tp"),
        P(None, None, "tp", "fsdp"),
        P(None, "tp", "fsdp"),
        P(None, "fsdp"),
        P(None, "fsdp", "tp"),
        P(None, "tp", "fsdp"),
        P(None, "tp", "fsdp"),
        P(None, "fsdp"),
        P(None, "fsdp"),
        P(None, "fsdp"),
        P("fsdp", "ctx", None),
    )
    out_specs = (
        P("fsdp", "ctx", None),
        P("fsdp", "ctx", None),
        P(None, "fsdp", None, "tp"),
        P(None, None, "tp", "fsdp"),
        P(None, "tp", "fsdp"),
        P(None, "fsdp"),
        P(None, "fsdp", "tp"),
        P(None, "tp", "fsdp"),
        P(None, "tp", "fsdp"),
        P(None, "fsdp"),
        P(None, "fsdp"),
        P(None, "fsdp"),
    )
    return jax.shard_map(shards, mesh=mesh, in_specs=in_specs, out_specs=out_specs, check_vma=False)
```

time: 1230 us -> 929 us (0.76)
  waiting for transfers between devices: 425 us -> 285 us
  blocking collectives: 117 us -> 0 us
  other arithmetic: 202 us -> 125 us
  local copies, waits for them, and re-layouts: 235 us -> 162 us
  starting transfers between devices: 77.2 us -> 144 us
  matrix products: 144 us -> 178 us
    all_gather x5 -> x0, blocking collectives: 117 us -> none  [the longest x4 77.4 us: gather_matrix(): along = lax.all_gather(half, 'tp', axis=0)]
    all_gather x6 -> x2, waiting for transfers between devices: 100 us -> 0.04 us  [give_back(): lax.all_gather(mm(pick_back, values).astype(BF), 'tp', axis=0)[:slots]]
    ppermute x0 -> x44, waiting for transfers between devices: none -> 89.6 us  [the longest x18 63.7 us: gather_line(): upper.append(lax.ppermute(upper[-1], 'tp', down_pairs[:count - 1 - step]))]
    ppermute x0 -> x44, starting transfers between devices: none -> 82.1 us  [the longest x18 31.4 us: gather_line(): lower.append(lax.ppermute(lower[-1], 'tp', up_pairs[step:]))]
    reduce_scatter x8 -> x2, waiting for transfers between devices: 79.1 us -> 0.04 us  [the longest x1 0.02 us: shards(): lax.psum_scatter(together(names[:2]), 'tp', scatter_dimension=0, tiled=Fa...]
    rev x11 -> x0, local copies, waits for them, and re-layouts: 41.1 us -> none  [reorder(): blocks = jnp.where(place % 2 == 1, blocks[..., :, ::-1, :], blocks)]
    psum x1 -> x0, waiting for transfers between devices: 40.2 us -> none  [shards(): lax.psum(jnp.concatenate([a.reshape(-1) for a in joined]), ('fsdp', 'ctx'...]
    slice x46 -> x99, local copies, waits for them, and re-layouts: 36.4 us -> 72.1 us  [the longest x28 32.5 us: forward_layer(): project[:, c:c + tile]]
  transfers between devices with their start and end apart: 96 -> 117, of which waited for: 30 -> 37; matrix products, arithmetic and copies ran while one was open for 44% -> 42% of each run, Pallas kernels for 0% -> 0%
where the time goes in v2:
time: 929 us; the launch traced here: 914 us
  waiting for transfers between devices  285 us (31%)
  matrix products  178 us (19%)
  local copies, waits for them, and re-layouts  162 us (17%)
  starting transfers between devices  144 us (16%)
  other arithmetic  125 us (13%)
  between operations  19.3 us (2%)
    ppermute x28, waiting for transfers between devices, send_x(): return lax.ppermute(values, 'fsdp', X_PAIRS)  156 us
    ppermute x18, waiting for transfers between devices, gather_line(): upper.append(lax.ppermute(upper[-1], 'tp', down_pairs[:count - 1 - step]))  63.7 us
    unnamed x421, local copies, waits for them, and re-layouts  58.6 us
    dot_general x24, matrix products, mm_tn(): lax.dot_general(left, right, (((0,), (0,)), ((), ())), preferred_element_...  50 us
    dot_general x14, matrix products, mm(): return jnp.dot(left, right, preferred_element_type=F32)  43.1 us
    ppermute x29, waiting for transfers between devices, send_y(): return lax.ppermute(values, 'fsdp', Y_PAIRS)  39.3 us
    ppermute x29, starting transfers between devices, send_y(): return lax.ppermute(values, 'fsdp', Y_PAIRS)  34 us
    slice x28, local copies, waits for them, and re-layouts, forward_layer(): project[:, c:c + tile]  32.5 us
  transfers between devices with their start and end apart: 117, of which 37 were waited for; matrix products, arithmetic and copies ran while one was open for 42% of the time, Pallas kernels for 0%

profile of v2, /device:TPU:0, one launch (start us, length us, event | category | flops | bytes accessed | tf_op | source)
XLA Modules:
  0.0 913.6 jit_solution(9060548783301266955)
XLA Ops:
  25.6 5.2 collective-permute-start.7
  77.1 5.0 collective-permute-done.5
  85.3 5.3 collective-permute-done.43
  118.5 13.3 %collective-permute-done.32 = bf16[512,256]{1,0:T(8,128)(2,1)S(1)} collective-permute-done((bf16[512,256]{1,0:T(8,128)(2,1)S(1)}, bf16[512,256]{1,0:T(8,128)(2,1)S(1)}, u32[]{:S(2)}, u32[]{:S(2)}) %collective-permute-start.32) | collective-permute-done | bytes 262176 | tf_op jit(solution)/shard_map/ppermute | solution.py:65
  148.0 16.5 %collective-permute-done.22 = bf16[640,256]{0,1:T(8,128)(2,1)S(1)} collective-permute-done((bf16[640,256]{0,1:T(8,128)(2,1)S(1)}, bf16[640,256]{0,1:T(8,128)(2,1)S(1)}, u32[]{:S(2)}, u32[]{:S(2)}) %collective-permute-start.22) | collective-permute-done | bytes 327712 | tf_op jit(solution)/shard_map/ppermute | solution.py:65
  198.6 8.8 collective-permute-done.55
  283.4 18.4 %collective-permute-done.26 = bf16[2560,256]{1,0:T(8,128)(2,1)S(1)} collective-permute-done((bf16[2560,256]{1,0:T(8,128)(2,1)}, bf16[2560,256]{1,0:T(8,128)(2,1)S(1)}, u32[]{:S(2)}, u32[]{:S(2)}) %collective-permute-start.26) | collective-permute-done | bytes 1310752 | tf_op jit(solution)/shard_map/ppermute | solution.py:42
  306.9 51.0 %collective-permute-done.51 = bf16[2048,128]{1,0:T(8,128)(2,1)S(1)} collective-permute-done((bf16[2048,128]{1,0:T(8,128)(2,1)S(1)}, bf16[2048,128]{1,0:T(8,128)(2,1)S(1)}, u32[]{:S(2)}, u32[]{:S(2)}) %collective-permute-start.51) | collective-permute-done | bytes 524320 | tf_op jit(solution)/shard_map/ppermute | solution.py:42
  362.3 8.4 collective-permute-done.39
  374.5 6.0 collective-permute-done.29
  401.5 8.0 collective-permute-done.61
  455.0 6.1 convert_reduce_fusion
  487.3 13.9 %collective-permute-done.91 = bf16[2048,256]{0,1:T(8,128)(2,1)} collective-permute-done((bf16[2048,256]{0,1:T(8,128)(2,1)}, bf16[2048,256]{0,1:T(8,128)(2,1)}, u32[]{:S(2)}, u32[]{:S(2)}) %collective-permute-start.91) | collective-permute-done | bytes 1048608 | tf_op jit(solution)/shard_map/ppermute | solution.py:42
  506.8 15.2 %collective-permute-done.95 = bf16[2048,256]{0,1:T(8,128)(2,1)} collective-permute-done((bf16[2048,256]{0,1:T(8,128)(2,1)}, bf16[2048,256]{0,1:T(8,128)(2,1)}, u32[]{:S(2)}, u32[]{:S(2)}) %collective-permute-start.95) | collective-permute-done | bytes 1048608 | tf_op jit(solution)/shard_map/ppermute | solution.py:42
  541.3 6.6 convert_reduce_fusion.6
  547.9 8.6 multiply_reduce_fusion.1
  556.6 6.7 multiply_convert_fusion.1
  579.6 5.5 convolution_convert_fusion.28
  596.6 6.2 collective-permute-done.98
  605.9 10.7 %collective-permute-done.103 = bf16[1536,256]{0,1:T(8,128)(2,1)S(1)} collective-permute-done((bf16[1536,256]{0,1:T(8,128)(2,1)}, bf16[1536,256]{0,1:T(8,128)(2,1)S(1)}, u32[]{:S(2)}, u32[]{:S(2)}) %collective-permute-start.103) | collective-permute-done | bytes 786464 | tf_op jit(solution)/shard_map/ppermute | solution.py:42
  648.3 6.6 convert_reduce_fusion.1
  678.2 15.2 %collective-permute-done.68 = bf16[2048,256]{0,1:T(8,128)(2,1)} collective-permute-done((bf16[2048,256]{0,1:T(8,128)(2,1)}, bf16[2048,256]{0,1:T(8,128)(2,1)}, u32[]{:S(2)}, u32[]{:S(2)}) %collective-permute-start.68) | collective-permute-done | bytes 1048608 | tf_op jit(solution)/shard_map/ppermute | solution.py:42
  698.0 17.7 %collective-permute-done.72 = bf16[2048,256]{0,1:T(8,128)(2,1)S(1)} collective-permute-done((bf16[2048,256]{0,1:T(8,128)(2,1)}, bf16[2048,256]{0,1:T(8,128)(2,1)S(1)}, u32[]{:S(2)}, u32[]{:S(2)}) %collective-permute-start.72) | collective-permute-done | bytes 1048608 | tf_op jit(solution)/shard_map/ppermute | solution.py:42
  725.9 6.6 convert_reduce_fusion.7
  732.6 8.7 multiply_reduce_fusion
  741.4 6.3 multiply_convert_fusion
  811.9 6.2 convolution_convert_fusion.27
  829.8 7.5 collective-permute-done.111
  837.3 5.2 collective-permute-start.112
  850.5 7.6 collective-permute-done.85
  858.2 13.5 %collective-permute-start.86 = (bf16[512,256]{1,0:T(8,128)(2,1)S(1)}, bf16[512,256]{1,0:T(8,128)(2,1)S(1)}, u32[]{:S(2)}, u32[]{:S(2)}) collective-permute-start(bf16[512,256]{1,0:T(8,128)(2,1)S(1)} %get-tuple-element.173), channel_id=1, source_target_pairs={{0,1},{1,2},{2,3},{4,5},{5,6},{6,7},{8,9},{9,10},{10,11},{12,13},{... | collective-permute-start | bytes 786440 | tf_op jit(solution)/shard_map/ppermute | solution.py:84
  876.7 5.5 collective-permute-done.86
  (993 shorter events, 562.5 us)
Async XLA Ops:
  7.2 636.2 %all-gather.5.cloned.1.call-start = ((), (), s32[]{:S(2)}) async-start(), calls=%async_computation.4 | async-start | bytes 3276800 | tf_op jit(solution)/shard_map/all_gather | solution.py:319
  19.2 54.3 %collective-permute-start.45 = (bf16[512,256]{1,0:T(8,128)(2,1)}, bf16[512,256]{1,0:T(8,128)(2,1)}, u32[]{:S(2)}, u32[]{:S(2)}) collective-permute-start(bf16[512,256]{1,0:T(8,128)(2,1)} %pad_maximum_fusion.19), channel_id=1, source_target_pairs={{0,1},{1,2},{2,3},{4,5},{5,6},{6,7},{8,9},{9,10},{10,11},{12,13},{... | collective-permute-start | bytes 786440 | tf_op jit(solution)/shard_map/ppermute | solution.py:64
  23.4 50.8 %collective-permute-start.42 = (bf16[512,256]{1,0:T(8,128)(2,1)}, bf16[512,256]{1,0:T(8,128)(2,1)}, u32[]{:S(2)}, u32[]{:S(2)}) collective-permute-start(bf16[512,256]{1,0:T(8,128)(2,1)} %pad_maximum_fusion.19), channel_id=1, source_target_pairs={{1,0},{2,1},{3,2},{5,4},{6,5},{7,6},{9,8},{10,9},{11,10},{13,12},{... | collective-permute-start | bytes 786440 | tf_op jit(solution)/shard_map/ppermute | solution.py:65
  25.6 45.3 %collective-permute-start.7 = (bf16[384,256]{1,0:T(8,128)(2,1)}, bf16[384,256]{1,0:T(8,128)(2,1)}, u32[]{:S(2)}, u32[]{:S(2)}) collective-permute-start(bf16[384,256]{1,0:T(8,128)(2,1)} %bitcast.20), channel_id=1, source_target_pairs={{0,1},{1,2},{2,3},{4,5},{5,6},{6,7},{8,9},{9,10},{10,11},{12,13},{... | collective-permute-start | bytes 589832 | tf_op jit(solution)/shard_map/ppermute | solution.py:64
  67.1 46.7 %collective-permute-start.23 = (bf16[640,256]{0,1:T(8,128)(2,1)}, bf16[640,256]{0,1:T(8,128)(2,1)}, u32[]{:S(2)}, u32[]{:S(2)}) collective-permute-start(bf16[640,256]{0,1:T(8,128)(2,1)} %pad_maximum_fusion.18), channel_id=1, source_target_pairs={{0,1},{1,2},{2,3},{4,5},{5,6},{6,7},{8,9},{9,10},{10,11},{12,13},{... | collective-permute-start | bytes 983048 | tf_op jit(solution)/shard_map/ppermute | solution.py:64
  138.1 52.3 %collective-permute-start.57 = (bf16[1024,256]{0,1:T(8,128)(2,1)S(1)}, bf16[1024,256]{0,1:T(8,128)(2,1)}, u32[]{:S(2)}, u32[]{:S(2)}) collective-permute-start(bf16[1024,256]{0,1:T(8,128)(2,1)S(1)} %collective-permute-done.56), channel_id=1, source_target_pairs={{1,2},{2,3},{5,6},{6,7},{9,10},{10,11},{13,14},{14,15},{17,18},{18... | collective-permute-start | bytes 1572872 | tf_op jit(solution)/shard_map/ppermute | solution.py:64
  139.6 52.3 %collective-permute-start.54 = (bf16[1024,256]{0,1:T(8,128)(2,1)}, bf16[1024,256]{0,1:T(8,128)(2,1)}, u32[]{:S(2)}, u32[]{:S(2)}) collective-permute-start(bf16[1024,256]{0,1:T(8,128)(2,1)} %collective-permute-done.53), channel_id=1, source_target_pairs={{1,0},{2,1},{5,4},{6,5},{9,8},{10,9},{13,12},{14,13},{17,16},{18,1... | collective-permute-start | bytes 1572872 | tf_op jit(solution)/shard_map/ppermute | solution.py:65
  147.5 45.1 %collective-permute-start.11 = (bf16[1536,256]{1,0:T(8,128)(2,1)}, bf16[1536,256]{1,0:T(8,128)(2,1)}, u32[]{:S(2)}, u32[]{:S(2)}) collective-permute-start(bf16[1536,256]{1,0:T(8,128)(2,1)} %bitcast.26), channel_id=1, source_target_pairs={{0,16},{16,0},{8,24},{24,8},{1,17},{17,1},{9,25},{25,9},{2,18},{18... | collective-permute-start | bytes 2359304 | tf_op jit(solution)/shard_map/ppermute | solution.py:46
  175.7 103.6 %collective-permute-start.38 = (bf16[2048,256]{1,0:T(8,128)(2,1)}, bf16[2048,256]{1,0:T(8,128)(2,1)}, u32[]{:S(2)}, u32[]{:S(2)}) collective-permute-start(bf16[2048,256]{1,0:T(8,128)(2,1)} %bitcast.86), channel_id=1, source_target_pairs={{0,16},{16,0},{8,24},{24,8},{1,17},{17,1},{9,25},{25,9},{2,18},{18... | collective-permute-start | bytes 3145736 | tf_op jit(solution)/shard_map/ppermute | solution.py:46
  187.1 89.3 %collective-permute-start.37 = (bf16[2048,256]{1,0:T(8,128)(2,1)}, bf16[2048,256]{1,0:T(8,128)(2,1)}, u32[]{:S(2)}, u32[]{:S(2)}) collective-permute-start(bf16[2048,256]{1,0:T(8,128)(2,1)} %bitcast.86), channel_id=1, source_target_pairs={{0,8},{8,0},{16,24},{24,16},{1,9},{9,1},{17,25},{25,17},{2,10},{10... | collective-permute-start | bytes 3145736 | tf_op jit(solution)/shard_map/ppermute | solution.py:42
  190.4 79.4 %collective-permute-start.49 = (bf16[2048,256]{1,0:T(8,128)(2,1)}, bf16[2048,256]{1,0:T(8,128)(2,1)}, u32[]{:S(2)}, u32[]{:S(2)}) collective-permute-start(bf16[2048,256]{1,0:T(8,128)(2,1)} %bitcast.101), channel_id=1, source_target_pairs={{0,16},{16,0},{8,24},{24,8},{1,17},{17,1},{9,25},{25,9},{2,18},{18... | collective-permute-start | bytes 3145736 | tf_op jit(solution)/shard_map/ppermute | solution.py:46
  234.4 69.1 %collective-permute-start.27 = (bf16[2560,256]{1,0:T(8,128)(2,1)}, bf16[2560,256]{1,0:T(8,128)(2,1)}, u32[]{:S(2)}, u32[]{:S(2)}) collective-permute-start(bf16[2560,256]{1,0:T(8,128)(2,1)} %bitcast.56), channel_id=1, source_target_pairs={{0,16},{16,0},{8,24},{24,8},{1,17},{17,1},{9,25},{25,9},{2,18},{18... | collective-permute-start | bytes 3932168 | tf_op jit(solution)/shard_map/ppermute | solution.py:46
  271.8 111.4 %collective-permute-start.60 = (bf16[4096,256]{1,0:T(8,128)(2,1)S(1)}, bf16[4096,256]{1,0:T(8,128)(2,1)S(1)}, u32[]{:S(2)}, u32[]{:S(2)}) collective-permute-start(bf16[4096,256]{1,0:T(8,128)(2,1)S(1)} %bitcast.518), channel_id=1, source_target_pairs={{0,16},{16,0},{8,24},{24,8},{1,17},{17,1},{9,25},{25,9},{2,18},{18... | collective-permute-start | bytes 6291464 | tf_op jit(solution)/shard_map/ppermute | solution.py:46
  276.4 107.6 %collective-permute-start.59 = (bf16[4096,256]{1,0:T(8,128)(2,1)S(1)}, bf16[4096,256]{1,0:T(8,128)(2,1)S(1)}, u32[]{:S(2)}, u32[]{:S(2)}) collective-permute-start(bf16[4096,256]{1,0:T(8,128)(2,1)S(1)} %bitcast.519), channel_id=1, source_target_pairs={{0,8},{8,0},{16,24},{24,16},{1,9},{9,1},{17,25},{25,17},{2,10},{10... | collective-permute-start | bytes 6291464 | tf_op jit(solution)/shard_map/ppermute | solution.py:42
  279.3 78.6 %collective-permute-start.51 = (bf16[2048,128]{1,0:T(8,128)(2,1)S(1)}, bf16[2048,128]{1,0:T(8,128)(2,1)S(1)}, u32[]{:S(2)}, u32[]{:S(2)}) collective-permute-start(bf16[2048,128]{1,0:T(8,128)(2,1)S(1)} %get-tuple-element.191), channel_id=1, source_target_pairs={{0,8},{8,0},{16,24},{24,16},{1,9},{9,1},{17,25},{25,17},{2,10},{10... | collective-permute-start | bytes 1572872 | tf_op jit(solution)/shard_map/ppermute | solution.py:42
  301.7 57.7 %collective-permute-start.50 = (bf16[2048,128]{1,0:T(8,128)(2,1)S(1)}, bf16[2048,128]{1,0:T(8,128)(2,1)S(1)}, u32[]{:S(2)}, u32[]{:S(2)}) collective-permute-start(bf16[2048,128]{1,0:T(8,128)(2,1)S(1)} %get-tuple-element.193), channel_id=1, source_target_pairs={{0,16},{16,0},{8,24},{24,8},{1,17},{17,1},{9,25},{25,9},{2,18},{18... | collective-permute-start | bytes 1572872 | tf_op jit(solution)/shard_map/ppermute | solution.py:46
  303.4 69.6 %collective-permute-start.40 = (bf16[2048,128]{1,0:T(8,128)(2,1)S(1)}, bf16[2048,128]{1,0:T(8,128)(2,1)S(1)}, u32[]{:S(2)}, u32[]{:S(2)}) collective-permute-start(bf16[2048,128]{1,0:T(8,128)(2,1)S(1)} %get-tuple-element.195), channel_id=1, source_target_pairs={{0,8},{8,0},{16,24},{24,16},{1,9},{9,1},{17,25},{25,17},{2,10},{10... | collective-permute-start | bytes 1572872 | tf_op jit(solution)/shard_map/ppermute | solution.py:42
  480.3 44.8 %collective-permute-start.97 = (bf16[2048,256]{0,1:T(8,128)(2,1)}, bf16[2048,256]{0,1:T(8,128)(2,1)}, u32[]{:S(2)}, u32[]{:S(2)}) collective-permute-start(bf16[2048,256]{0,1:T(8,128)(2,1)} %convolution_convert_fusion.11), channel_id=1, source_target_pairs={{0,16},{16,0},{8,24},{24,8},{1,17},{17,1},{9,25},{25,9},{2,18},{18... | collective-permute-start | bytes 3145736 | tf_op jit(solution)/shard_map/ppermute | solution.py:46
  484.1 45.2 %collective-permute-start.63 = (bf16[592,1024]{1,0:T(8,128)(2,1)}, bf16[592,1024]{1,0:T(8,128)(2,1)}, u32[]{:S(2)}, u32[]{:S(2)}) collective-permute-start(bf16[592,1024]{1,0:T(8,128)(2,1)} %convolution_convert_fusion.21), channel_id=1, source_target_pairs={{0,4},{4,0},{1,5},{5,1},{2,6},{6,2},{3,7},{7,3},{8,12},{12,8},{9,1... | collective-permute-start | bytes 3637256 | tf_op jit(solution)/shard_map/ppermute | solution.py:50
  501.2 77.9 %collective-permute-start.65 = (bf16[592,1024]{1,0:T(8,128)(2,1)}, bf16[592,1024]{1,0:T(8,128)(2,1)}, u32[]{:S(2)}, u32[]{:S(2)}) collective-permute-start(bf16[592,1024]{1,0:T(8,128)(2,1)} %convolution_convert_fusion.20), channel_id=1, source_target_pairs={{0,4},{4,0},{1,5},{5,1},{2,6},{6,2},{3,7},{7,3},{8,12},{12,8},{9,1... | collective-permute-start | bytes 3637256 | tf_op jit(solution)/shard_map/ppermute | solution.py:50
  505.3 86.4 %collective-permute-start.92 = (bf16[2048,128]{0,1:T(8,128)(2,1)}, bf16[2048,128]{0,1:T(8,128)(2,1)}, u32[]{:S(2)}, u32[]{:S(2)}) collective-permute-start(bf16[2048,128]{0,1:T(8,128)(2,1)} %get-tuple-element.125), channel_id=1, source_target_pairs={{0,16},{16,0},{8,24},{24,8},{1,17},{17,1},{9,25},{25,9},{2,18},{18... | collective-permute-start | bytes 1572872 | tf_op jit(solution)/shard_map/ppermute | solution.py:46
  522.0 71.3 %collective-permute-start.94 = (bf16[2048,128]{0,1:T(8,128)(2,1)}, bf16[2048,128]{0,1:T(8,128)(2,1)}, u32[]{:S(2)}, u32[]{:S(2)}) collective-permute-start(bf16[2048,128]{0,1:T(8,128)(2,1)} %get-tuple-element.126), channel_id=1, source_target_pairs={{0,8},{8,0},{16,24},{24,16},{1,9},{9,1},{17,25},{25,17},{2,10},{10... | collective-permute-start | bytes 1572872 | tf_op jit(solution)/shard_map/ppermute | solution.py:42
  527.8 68.0 %collective-permute-start.96 = (bf16[2048,128]{0,1:T(8,128)(2,1)}, bf16[2048,128]{0,1:T(8,128)(2,1)}, u32[]{:S(2)}, u32[]{:S(2)}) collective-permute-start(bf16[2048,128]{0,1:T(8,128)(2,1)} %get-tuple-element.129), channel_id=1, source_target_pairs={{0,16},{16,0},{8,24},{24,8},{1,17},{17,1},{9,25},{25,9},{2,18},{18... | collective-permute-start | bytes 1572872 | tf_op jit(solution)/shard_map/ppermute | solution.py:46
  585.1 265.3 %reduce-scatter.5.cloned.1.call-start = ((), (), s32[]{:S(2)}) async-start(), calls=%async_computation.3 | async-start | bytes 3932160 | tf_op jit(solution)/shard_map/reduce_scatter | solution.py:336
  637.3 249.5 %reduce-scatter.3.cloned.1.call-start = ((), (), s32[]{:S(2)}) async-start(), calls=%async_computation.2 | async-start | bytes 2621440 | tf_op jit(solution)/shard_map/reduce_scatter | solution.py:338
  668.0 47.7 %collective-permute-start.72 = (bf16[2048,256]{0,1:T(8,128)(2,1)}, bf16[2048,256]{0,1:T(8,128)(2,1)S(1)}, u32[]{:S(2)}, u32[]{:S(2)}) collective-permute-start(bf16[2048,256]{0,1:T(8,128)(2,1)} %convolution_convert_fusion.16), channel_id=1, source_target_pairs={{0,8},{8,0},{16,24},{24,16},{1,9},{9,1},{17,25},{25,17},{2,10},{10... | collective-permute-start | bytes 3145736 | tf_op jit(solution)/shard_map/ppermute | solution.py:42
  668.9 47.9 %collective-permute-start.74 = (bf16[2048,256]{0,1:T(8,128)(2,1)}, bf16[2048,256]{0,1:T(8,128)(2,1)}, u32[]{:S(2)}, u32[]{:S(2)}) collective-permute-start(bf16[2048,256]{0,1:T(8,128)(2,1)} %convolution_convert_fusion.15), channel_id=1, source_target_pairs={{0,16},{16,0},{8,24},{24,8},{1,17},{17,1},{9,25},{25,9},{2,18},{18... | collective-permute-start | bytes 3145736 | tf_op jit(solution)/shard_map/ppermute | solution.py:46
  697.0 71.8 %collective-permute-start.69 = (bf16[2048,128]{0,1:T(8,128)(2,1)}, bf16[2048,128]{0,1:T(8,128)(2,1)}, u32[]{:S(2)}, u32[]{:S(2)}) collective-permute-start(bf16[2048,128]{0,1:T(8,128)(2,1)} %get-tuple-element.117), channel_id=1, source_target_pairs={{0,16},{16,0},{8,24},{24,8},{1,17},{17,1},{9,25},{25,9},{2,18},{18... | collective-permute-start | bytes 1572872 | tf_op jit(solution)/shard_map/ppermute | solution.py:46
  697.1 73.9 %collective-permute-start.71 = (bf16[2048,128]{0,1:T(8,128)(2,1)}, bf16[2048,128]{0,1:T(8,128)(2,1)}, u32[]{:S(2)}, u32[]{:S(2)}) collective-permute-start(bf16[2048,128]{0,1:T(8,128)(2,1)} %get-tuple-element.118), channel_id=1, source_target_pairs={{0,8},{8,0},{16,24},{24,16},{1,9},{9,1},{17,25},{25,17},{2,10},{10... | collective-permute-start | bytes 1572872 | tf_op jit(solution)/shard_map/ppermute | solution.py:42
  719.0 54.9 %collective-permute-start.73 = (bf16[2048,128]{0,1:T(8,128)(2,1)}, bf16[2048,128]{0,1:T(8,128)(2,1)}, u32[]{:S(2)}, u32[]{:S(2)}) collective-permute-start(bf16[2048,128]{0,1:T(8,128)(2,1)} %get-tuple-element.121), channel_id=1, source_target_pairs={{0,16},{16,0},{8,24},{24,8},{1,17},{17,1},{9,25},{25,9},{2,18},{18... | collective-permute-start | bytes 1572872 | tf_op jit(solution)/shard_map/ppermute | solution.py:46
  719.0 55.1 %collective-permute-start.75 = (bf16[2048,128]{0,1:T(8,128)(2,1)}, bf16[2048,128]{0,1:T(8,128)(2,1)}, u32[]{:S(2)}, u32[]{:S(2)}) collective-permute-start(bf16[2048,128]{0,1:T(8,128)(2,1)} %get-tuple-element.122), channel_id=1, source_target_pairs={{0,8},{8,0},{16,24},{24,16},{1,9},{9,1},{17,25},{25,17},{2,10},{10... | collective-permute-start | bytes 1572872 | tf_op jit(solution)/shard_map/ppermute | solution.py:42
  778.8 110.8 %all-gather.7.cloned.1.call-start = ((), (), s32[]{:S(2)}) async-start(), calls=%async_computation.5 | async-start | bytes 3276800 | tf_op jit(solution)/shard_map/all_gather | solution.py:319
  (251 other events, 4609.6 us)
Sparse Core Ops, SparseCore 0:
  585.2 52.7 all-gather.4
  640.3 59.0 reduce-scatter.4
  778.9 42.1 reduce-scatter.2
  823.2 65.7 all-gather.6

commit v3 on v2

--- a/solution.py
+++ b/solution.py
@@ -1,6 +1,8 @@
 import jax
 import jax.numpy as jnp
 from jax import lax
+from jax.experimental import pallas as pl
+from jax.experimental.pallas import tpu as pltpu
 from jax.sharding import PartitionSpec as P
 
 HD = 64
@@ -44,6 +46,10 @@
 
 def send_y(values):
     return lax.ppermute(values, "fsdp", Y_PAIRS)
+
+
+def after(values, *earlier):
+    return lax.optimization_barrier((values,) + earlier)[0]
 
 
 def swap(values):
@@ -86,16 +92,30 @@
     return (take(lane).astype(F32) + rising.astype(F32) + falling.astype(F32)).astype(BF)
 
 
-def gather_features(shard):
+def gather_features(along, previous):
     if not square():
-        return [lax.all_gather(shard, "fsdp", axis=1, tiled=True)]
-    half = shard.shape[1] // 2
-    from_x, from_y = send_x(shard), send_y(shard)
-    far_a, far_b = send_y(from_x[:, :half]), send_x(from_y[:, half:])
-    return [shard, from_x[:, half:], from_y[:, :half], from_x[:, :half], far_a, far_b, from_y[:, half:]]
-
-
-def gradient_rows(delta, values):
+        return [lax.all_gather(along, "fsdp", axis=along.ndim - 1, tiled=True)], ()
+    half = along.shape[-1] // 2
+    along = after(along, *previous)
+    from_x, from_y = send_x(along), send_y(along)
+    far_a, far_b = send_y(from_x[..., :half]), send_x(from_y[..., half:])
+    pieces = [along, from_x[..., half:], from_y[..., :half], from_x[..., :half], far_a, far_b, from_y[..., half:]]
+    return pieces, (from_x, from_y)
+
+
+def gather_group(along, heights, previous):
+    count = lax.axis_size("tp")
+    pieces, came = gather_features(along, previous)
+    pieces = [piece.reshape(count, -1, piece.shape[-1]) for piece in pieces]
+    result, start = [], 0
+    for height in heights:
+        cut = [piece[:, start : start + height].reshape(count * height, -1) for piece in pieces]
+        result.append(jnp.concatenate(cut, axis=1))
+        start += height
+    return result, came
+
+
+def gradient_start(delta, values):
     if not square():
         return lax.psum_scatter(mm_tn(delta, values).astype(BF), "fsdp", scatter_dimension=1, tiled=True)
     half = values.shape[1] // 8
@@ -103,36 +123,23 @@
     from_x = send_x(to_x)
     to_y = mm_tn(delta, values[:, 6 * half :]).astype(BF)
     from_y = send_y(to_y)
-    own_a, own_b, x_b, y_a = jnp.split(mm_tn(delta, values[:, : 4 * half]).astype(BF), 4, axis=1)
+    return mm_tn(delta, values[:, : 4 * half]).astype(BF), from_x, from_y
+
+
+def gradient_finish(begun, *earlier):
+    if not square():
+        return begun
+    kept, from_x, from_y = begun
+    half = from_x.shape[1] // 2
+    if earlier:
+        from_x, from_y = lax.optimization_barrier((from_x, from_y) + earlier)[:2]
+    own_a, own_b, x_b, y_a = jnp.split(kept, 4, axis=1)
     last_a = send_y(y_a + from_x[:, half:])
     last_b = send_x(x_b + from_y[:, :half])
     add = lambda *terms: sum(term.astype(F32) for term in terms).astype(BF)
     return jnp.concatenate([add(own_a, from_x[:, :half], last_a), add(own_b, from_y[:, half:], last_b)], axis=1)
 
 
-def gather_group(shards):
-    count = lax.axis_size("tp")
-    heights = [shard.shape[0] for shard in shards]
-    along = gather_line(jnp.concatenate(shards, axis=0))
-    pieces = gather_features(along.reshape(-1, along.shape[-1]))
-    pieces = [piece.reshape(count, -1, piece.shape[-1]) for piece in pieces]
-    result, start = [], 0
-    for height in heights:
-        cut = [piece[:, start : start + height].reshape(count * height, -1) for piece in pieces]
-        result.append(jnp.concatenate(cut, axis=1))
-        start += height
-    return result
-
-
-def heads_of(values):
-    return values.reshape(values.shape[0], -1, HD)
-
-
-def masked_scores(queries, keys, key_valid):
-    scores = jnp.einsum("qhd,khd->hqk", queries, keys, preferred_element_type=F32) * HD ** (-0.5)
-    return jnp.where(key_valid, scores, -1000000000.0)
-
-
 def mm(left, right):
     return jnp.dot(left, right, preferred_element_type=F32)
 
@@ -145,68 +152,126 @@
     return lax.dot_general(left, right, (((0,), (0,)), ((), ())), preferred_element_type=F32)
 
 
-def forward_layer(stream, weights, vectors, key_valid):
+def head_scores(project_ref, tile, head):
+    part = lambda k: project_ref[:, k * tile + head * HD : k * tile + (head + 1) * HD]
+    queries, keys, values = part(0), part(1), part(2)
+    scores = mm_nt(queries * BF(HD ** (-0.5)), keys)
+    valid = lax.broadcasted_iota(jnp.int32, (1, scores.shape[1]), 1) < SEQ
+    return queries, keys, values, jnp.where(valid, scores, -1000000000.0)
+
+
+def attend_kernel(project_ref, mixed_ref, total_ref):
+    tile = mixed_ref.shape[1]
+    mixed, totals = [], []
+    for head in range(tile // HD):
+        values, scores = head_scores(project_ref, tile, head)[2:]
+        highest = jnp.max(scores, axis=1, keepdims=True)
+        exponent = jnp.exp(scores - highest)
+        denominator = jnp.sum(exponent, axis=1, keepdims=True)
+        mixed.append(mm(exponent.astype(BF), values) / denominator)
+        totals.append(highest + jnp.log(denominator))
+    mixed_ref[...] = jnp.concatenate(mixed, axis=1).astype(BF)
+    total_ref[0] = jnp.concatenate(totals, axis=1)
+
+
+def attend_back_kernel(project_ref, mixed_ref, total_ref, delta_ref, out_ref):
+    tile = mixed_ref.shape[1]
+    scale = HD ** (-0.5)
+    parts = ([], [], [])
+    for head in range(tile // HD):
+        queries, keys, values, scores = head_scores(project_ref, tile, head)
+        here = slice(head * HD, (head + 1) * HD)
+        delta = delta_ref[:, here]
+        probs = jnp.exp(scores - total_ref[0, :, head : head + 1])
+        inner = jnp.sum(delta.astype(F32) * mixed_ref[:, here].astype(F32), axis=1, keepdims=True)
+        delta_scores = (probs * (mm_nt(delta, values) - inner)).astype(BF)
+        parts[0].append(mm(delta_scores, keys) * scale)
+        parts[1].append(mm_tn(delta_scores, queries) * scale)
+        parts[2].append(mm_tn(probs.astype(BF), delta))
+    out_ref[...] = jnp.concatenate(parts[0] + parts[1] + parts[2], axis=1).astype(BF)
+
+
+def attention_specs(rows, tile):
+    wide = pl.BlockSpec((rows, 3 * tile), lambda t: (0, t))
+    narrow = pl.BlockSpec((rows, tile), lambda t: (0, t))
+    totals = pl.BlockSpec((1, rows, tile // HD), lambda t: (t, 0, 0))
+    return wide, narrow, totals
+
+
+def attend(project, tile):
+    rows, count = project.shape[0], project.shape[1] // (3 * tile)
+    wide, narrow, totals = attention_specs(rows, tile)
+    work = rows * rows * tile * count
+    return pl.pallas_call(
+        attend_kernel,
+        grid=(count,),
+        in_specs=[wide],
+        out_specs=[narrow, totals],
+        out_shape=[
+            jax.ShapeDtypeStruct((rows, tile * count), BF),
+            jax.ShapeDtypeStruct((count, rows, tile // HD), F32),
+        ],
+        compiler_params=pltpu.CompilerParams(vmem_limit_bytes=32 * 1024 * 1024),
+        cost_estimate=pl.CostEstimate(flops=16 * work, bytes_accessed=8 * project.size // 3, transcendentals=work // HD),
+    )(project)
+
+
+def attend_back(project, mixed, totals, delta, tile):
+    rows, count = project.shape[0], project.shape[1] // (3 * tile)
+    wide, narrow, per_row = attention_specs(rows, tile)
+    work = rows * rows * tile * count
+    return pl.pallas_call(
+        attend_back_kernel,
+        grid=(count,),
+        in_specs=[wide, narrow, per_row, narrow],
+        out_specs=wide,
+        out_shape=jax.ShapeDtypeStruct(project.shape, BF),
+        compiler_params=pltpu.CompilerParams(vmem_limit_bytes=32 * 1024 * 1024),
+        cost_estimate=pl.CostEstimate(flops=40 * work, bytes_accessed=5 * project.size, transcendentals=work // HD),
+    )(project, mixed, totals, delta)
+
+
+def forward_layer(stream, weights, vectors, gates):
     qkv, out, up, down = weights
-    shift_q, shift_v, out_shift, up_shift, down_shift, gain_first, gain_second = vectors
+    qkv_shift, out_shift, up_shift, down_shift, gain_first, gain_second = vectors
     normed = layer_norm(stream, gain_first).astype(BF)
-    project = mm_nt(normed, qkv)
-    width = project.shape[1] // 3
-    tile = width // lax.axis_size("tp")
-    member = lambda k: jnp.concatenate(
-        [project[:, c : c + tile] for c in range(k * tile, 3 * width, 3 * tile)], axis=1
-    )
-    queries = heads_of((member(0) + shift_q).astype(BF))
-    keys = heads_of(member(1).astype(BF))
-    values = heads_of((member(2) + shift_v).astype(BF))
-    scores = masked_scores(queries, keys, key_valid)
-    highest = jnp.max(scores, axis=-1, keepdims=True)
-    exponent = jnp.exp(scores - highest)
-    denominator = jnp.sum(exponent, axis=-1, keepdims=True)
-    probs = (exponent / denominator).astype(BF)
-    log_total = highest + jnp.log(denominator)
-    mixed = jnp.einsum("hqk,khd->qhd", probs, values, preferred_element_type=F32).astype(BF)
-    mixed = mixed.reshape(stream.shape[0], width)
+    project = (mm_nt(normed, qkv) + qkv_shift).astype(BF)
+    tile = project.shape[1] // (3 * lax.axis_size("tp"))
+    mixed, totals = attend(after(project, *gates[0]), tile)
+    mixed = after(mixed, *gates[1])
     middle = stream + both_cores(mm(mixed, out)) + out_shift
     normed_b = layer_norm(middle, gain_second).astype(BF)
     hidden = mm_nt(normed_b, up) + up_shift
     active = gelu_exact(hidden).astype(BF)
     following = middle + both_cores(mm(active, down)) + down_shift
-    return following, (stream, normed, queries, keys, values, log_total, mixed, middle, normed_b, hidden, active)
-
-
-def backward_layer(gradient, saved, weights, vectors, key_valid, emit):
+    return following, (stream, normed, project, totals, mixed, middle, normed_b, hidden, active)
+
+
+def backward_layer(gradient, saved, weights, vectors, emit, gate):
     qkv, out, up, down = weights
-    gain_first, gain_second = vectors[5:]
-    stream, normed, queries, keys, values, log_total, mixed, middle, normed_b, hidden, active = saved
+    gain_first, gain_second = vectors[4:]
+    stream, normed, project, totals, mixed, middle, normed_b, hidden, active = saved
     total = lambda array: jnp.sum(array.astype(F32), axis=0)
     grad_low = gradient.astype(BF)
     emit("down", active, grad_low)
     delta_hidden = jax.vjp(gelu_exact, hidden)[1](mm_nt(grad_low, down))[0].astype(BF)
+    delta_hidden = gate("hidden", delta_hidden)
     emit("up", delta_hidden, normed_b)
     delta_normed_b = both_cores(mm(delta_hidden, up))
     back_middle, delta_gain_second = jax.vjp(layer_norm, middle, gain_second)[1](delta_normed_b)
     grad_middle = gradient + back_middle
     grad_attend = grad_middle.astype(BF)
+    grad_attend = gate("attend", grad_attend)
     emit("out", mixed, grad_attend)
-    delta_mixed = heads_of(mm_nt(grad_attend, out).astype(BF))
-    probs = jnp.exp(masked_scores(queries, keys, key_valid) - log_total)
-    delta_values = jnp.einsum("hqk,qhd->khd", probs.astype(BF), delta_mixed, preferred_element_type=F32).astype(BF)
-    delta_probs = jnp.einsum("qhd,khd->hqk", delta_mixed, values, preferred_element_type=F32)
-    inner = jnp.sum(probs * delta_probs, axis=-1, keepdims=True)
-    delta_scores = (probs * (delta_probs - inner)).astype(BF)
-    scale = HD ** (-0.5)
-    delta_queries = (jnp.einsum("hqk,khd->qhd", delta_scores, keys, preferred_element_type=F32) * scale).astype(BF)
-    delta_keys = (jnp.einsum("hqk,qhd->khd", delta_scores, queries, preferred_element_type=F32) * scale).astype(BF)
-    flat = [piece.reshape(stream.shape[0], -1) for piece in (delta_queries, delta_keys, delta_values)]
-    width = flat[0].shape[1]
-    tile = width // lax.axis_size("tp")
-    delta_project = jnp.concatenate([piece[:, c : c + tile] for c in range(0, width, tile) for piece in flat], axis=1)
+    delta_mixed = mm_nt(grad_attend, out).astype(BF)
+    tile = mixed.shape[1] // lax.axis_size("tp")
+    delta_project = attend_back(project, mixed, totals, delta_mixed, tile)
+    delta_project = gate("project", delta_project)
     emit("qkv", delta_project, normed)
     delta_normed = both_cores(mm(delta_project, qkv))
     back_stream, delta_gain_first = jax.vjp(layer_norm, stream, gain_first)[1](delta_normed)
     sums = (
-        total(flat[0]),
-        total(flat[2]),
+        total(delta_project),
         total(grad_attend),
         total(delta_hidden),
         total(grad_low),
@@ -241,7 +306,6 @@
     slot = jnp.minimum(lane, slots - 1)
     own_lengths = lax.dynamic_index_in_dim(lengths, slot, 0, keepdims=False)
     live = lane < jnp.minimum(image_count[0], slots)
-    key_valid = (jnp.arange(rows) < SEQ)[None, None, :]
     row_mask = ((jnp.arange(rows) < SEQ) & live).astype(F32)[:, None]
     halves = lambda array, axis: lax.dynamic_index_in_dim(
         array.reshape(array.shape[:axis] + (2, -1) + array.shape[axis + 1 :]), core, axis, keepdims=False
@@ -251,7 +315,19 @@
     for l in range(layers):
         qkv = jnp.transpose(halves(qkv_weight[l], 2), (1, 2, 0)).reshape(-1, qkv_weight.shape[1])
         cut.append((qkv, halves(out_weight[l], 0), halves(up_weight[l], 1).T, halves(down_weight[l], 0)))
-    first_qkv = gather_group([cut[0][0]])
+    heights = [piece.shape[0] for piece in cut[0]]
+    joined = lambda l, members: jnp.concatenate([cut[l][k] for k in members], axis=0)
+    groups = [[(0,), (1, 2), (3,)]] + [[(0, 1), (2,), (3,)]] * (layers - 1)
+    stages, along = [], ()
+    for l in range(layers):
+        for members in groups[l]:
+            shard = after(joined(l, members), *along)
+            if l == 0 and members == (0,):
+                along = (gather_line(shard).reshape(-1, shard.shape[1]),)
+            else:
+                along = (lax.all_gather(shard, "tp", axis=0, tiled=True),)
+            stages.append((l, members, along[0]))
+    first_along = stages[0][2]
 
     pieces = (qv_bias, up_bias, out_bias, down_bias, gain_one, gain_two)
     packed = jnp.concatenate([piece.reshape(1, -1) for piece in pieces], axis=1)
@@ -264,7 +340,7 @@
         spread = lax.all_gather(packed[0], "fsdp", axis=0)
     order = order_matrix(features)
     split = qv_bias.size + up_bias.size
-    across = gather_line(spread[:, :split])
+    across = gather_line(after(spread[:, :split], first_along))
 
     def by_core(array, count):
         array = array.reshape(n_tp, n_fsdp, layers, count, -1)
@@ -278,8 +354,10 @@
         by_feature = mm(by_feature, order)
     by_feature = by_feature.astype(F32).reshape(4, layers, features)
     out_all, down_all, one_all, two_all = by_feature[0], by_feature[1], by_feature[2], by_feature[3]
+    q_part, v_part = [qv_all[:, k].reshape(layers, n_tp, -1) for k in range(2)]
+    qkv_all = jnp.concatenate([q_part, jnp.zeros_like(q_part), v_part], axis=2).reshape(layers, -1).astype(F32)
     vectors = [
-        (qv_all[l, 0], qv_all[l, 1], out_all[l], up_all[l, 0], down_all[l], one_all[l], two_all[l])
+        (qkv_all[l], out_all[l], up_all[l, 0], down_all[l], one_all[l], two_all[l])
         for l in range(layers)
     ]
 
@@ -298,13 +376,16 @@
     stream = image[0].astype(F32)
     gradient = image[1].astype(F32) * row_mask
 
-    weights = [tuple(first_qkv + gather_group(cut[0][1:3]) + gather_group(cut[0][3:]))]
-    for l in range(1, layers):
-        weights.append(tuple(gather_group(cut[l][:2]) + gather_group(cut[l][2:])))
+    weights = [[] for l in range(layers)]
+    came, arrivals = (), []
+    for l, members, along in stages:
+        more, came = gather_group(along, [heights[k] for k in members], came)
+        weights[l] += more
+        arrivals.append(came)
 
     saved = []
     for l in range(layers):
-        stream, items = forward_layer(stream, weights[l], vectors[l], key_valid)
+        stream, items = forward_layer(stream, weights[l], vectors[l], arrivals[3 * l + 1 : 3 * l + 3])
         saved.append(items)
 
     place = jnp.arange(capacity)
@@ -316,31 +397,56 @@
         values = values.astype(BF)
         if order is not None:
             values = mm_nt(values, order).astype(BF)
-        return lax.all_gather(mm(pick_back, values).astype(BF), "tp", axis=0)[:slots]
+        return mm(pick_back, values).astype(BF)
+
+    def to_all(values):
+        return lax.all_gather(values, "tp", axis=0)[:slots]
 
     output = give_back(stream)
+    gradient, output = lax.optimization_barrier((gradient, output))
+    output = to_all(output)
     names = ("down", "up", "out", "qkv")
-    found = {}
+    begun, found = {}, {}
     sums = [None] * layers
     mine = [None] * layers
+
+    def reduced(layer, some):
+        joined = [found[layer, name].reshape(n_tp, -1, features // n_fsdp) for name in some]
+        return jnp.concatenate(joined, axis=1)
+
     for l in reversed(range(layers)):
 
-        def emit(name, delta, values):
-            found[name] = gradient_rows(delta, values).reshape(n_tp, -1, features // n_fsdp)
-
-        if l == layers - 2:
-            gradient, output = lax.optimization_barrier((gradient, output))
-        gradient, sums[l] = backward_layer(gradient, saved[l], weights[l], vectors[l], key_valid, emit)
-        together = lambda some: jnp.concatenate([found[name] for name in some], axis=1)
-        if l > 0:
-            mine[l] = lax.psum_scatter(together(names), "tp", scatter_dimension=0, tiled=False)
-        else:
-            early = lax.psum_scatter(together(names[:2]), "tp", scatter_dimension=0, tiled=False)
-            mine[l] = jnp.concatenate([early, scatter_line(together(names[2:]))], axis=0)
-    input_grad = give_back(gradient)
+        def emit(name, delta, values, l=l):
+            begun[l, name] = gradient_start(delta, values)
+
+        def first(name, layer):
+            found[layer, name] = gradient_finish(begun[layer, name])
+            return begun[layer, name][1:] if square() else ()
+
+        def gate(point, value, l=l):
+            held = ()
+            if point == "hidden" and l < layers - 1:
+                held = first("out", l + 1) + (found[l + 1, "down"],)
+            if point == "attend":
+                held = first("down", l)
+                if l < layers - 1:
+                    held += first("qkv", l + 1) + (found[l + 1, "up"], found[l + 1, "out"])
+            if point == "project":
+                held = first("up", l)
+                if l < layers - 1:
+                    mine[l + 1] = lax.psum_scatter(reduced(l + 1, names), "tp", scatter_dimension=0, tiled=False)
+                    held += (output, found[l, "down"])
+            return after(value, *held)
+
+        gradient, sums[l] = backward_layer(gradient, saved[l], weights[l], vectors[l], emit, gate)
+    found[0, "out"] = gradient_finish(begun[0, "out"])
+    early = lax.psum_scatter(reduced(0, names[:3]), "tp", scatter_dimension=0, tiled=False)
+    found[0, "qkv"] = gradient_finish(begun[0, "qkv"])
+    mine[0] = jnp.concatenate([early, scatter_line(reduced(0, names[3:]))], axis=0)
+    input_grad = to_all(give_back(gradient))
 
     grads = {name: [] for name in names}
-    heights = [2 * found[name].shape[1] // 2 for name in names]
+    heights = [found[0, name].shape[0] // n_tp for name in names]
     for l in range(layers):
         other = swap(mine[l])
         low = jnp.where(core == 0, mine[l], other)
@@ -366,14 +472,14 @@
 
     first = (core == 0).astype(F32)
     member = lambda k: jnp.stack([sums[l][k] for l in range(layers)])
-    by_feature = jnp.stack([member(k) for k in (2, 4, 5, 6)]).reshape(4 * layers, features) * first
+    by_feature = jnp.stack([member(k) for k in (1, 3, 4, 5)]).reshape(4 * layers, features) * first
     if order is not None:
         by_feature = lax.dot_general(
             by_feature, order.astype(F32), (((1,), (1,)), ((), ())), precision=lax.Precision.HIGHEST
         )
     joined = [
-        from_core(jnp.stack([member(0), member(1)], axis=1), 2),
-        from_core(member(3)[:, None], 1),
+        from_core(jnp.swapaxes(member(0).reshape(layers, n_tp, 3, -1)[:, :, ::2], 1, 2), 2),
+        from_core(member(2)[:, None], 1),
         by_feature.reshape(-1),
     ]
     summed = jnp.concatenate(joined).reshape(-1, 128)

time: 929 us -> 812 us (0.87)
  Pallas kernels: 0 us -> 55.3 us
  starting transfers between devices: 144 us -> 98.2 us
  other arithmetic: 125 us -> 85.7 us
  matrix products: 178 us -> 143 us
  waiting for transfers between devices: 285 us -> 259 us
  local copies, waits for them, and re-layouts: 162 us -> 145 us
    pallas_call x0 -> x4, Pallas kernels: none -> 55.3 us  [the longest x2 39.8 us: attend_back(): pl.pallas_call(attend_back_kernel, grid=(count,), in_specs=[wide, narrow,...]
    dot_general x12 -> x0, matrix products: 51.5 us -> none  [the longest x2 17.3 us: backward_layer(): jnp.einsum('qhd,khd->hqk', delta_mixed, values, preferred_element_type=F32)]
    ppermute x18 -> x6, waiting for transfers between devices: 63.7 us -> 23.3 us  [gather_line(): upper.append(lax.ppermute(upper[-1], 'tp', down_pairs[:count - 1 - step]))]
    ppermute x28 -> x30, waiting for transfers between devices: 156 us -> 127 us  [send_x(): return lax.ppermute(values, 'fsdp', X_PAIRS)]
    slice x40 -> x17, local copies, waits for them, and re-layouts: 51.2 us -> 24.1 us  [the longest x6 10.1 us: gather_features(): from_x[..., :half]]
    ppermute x18 -> x6, starting transfers between devices: 31.4 us -> 8.24 us  [gather_line(): lower.append(lax.ppermute(lower[-1], 'tp', up_pairs[step:]))]
    all_gather x2 -> x7, waiting for transfers between devices: 0.04 us -> 22.1 us  [the longest x2 14.6 us: to_all(): return lax.all_gather(values, 'tp', axis=0)[:slots]]
    ppermute x29 -> x31, waiting for transfers between devices: 39.3 us -> 56.2 us  [send_y(): return lax.ppermute(values, 'fsdp', Y_PAIRS)]
  transfers between devices with their start and end apart: 117 -> 102, of which waited for: 37 -> 43; matrix products, arithmetic and copies ran while one was open for 42% -> 38% of each run, Pallas kernels for 0% -> 7%
where the time goes in v3:
time: 812 us; the launch traced here: 804 us
  waiting for transfers between devices  259 us (32%)
  local copies, waits for them, and re-layouts  145 us (18%)
  matrix products  143 us (18%)
  starting transfers between devices  98.2 us (12%)
  other arithmetic  85.7 us (11%)
  Pallas kernels  55.3 us (7%)
  between operations  18.2 us (2%)
    ppermute x30, waiting for transfers between devices, send_x(): return lax.ppermute(values, 'fsdp', X_PAIRS)  127 us
    unnamed x280, local copies, waits for them, and re-layouts  60.7 us
    ppermute x31, waiting for transfers between devices, send_y(): return lax.ppermute(values, 'fsdp', Y_PAIRS)  56.2 us
    dot_general x14, matrix products, mm(): return jnp.dot(left, right, preferred_element_type=F32)  52 us
    dot_general x24, matrix products, mm_tn(): lax.dot_general(left, right, (((0,), (0,)), ((), ())), preferred_element_...  48.5 us
    dot_general x8, matrix products, mm_nt(): lax.dot_general(left, right, (((1,), (1,)), ((), ())), preferred_element_...  40.9 us
    pallas_call x2, Pallas kernels, attend_back(): pl.pallas_call(attend_back_kernel, grid=(count,), in_specs=[wide, narrow,...  39.8 us
    ppermute x31, starting transfers between devices, send_y(): return lax.ppermute(values, 'fsdp', Y_PAIRS)  34.8 us
  transfers between devices with their start and end apart: 102, of which 43 were waited for; matrix products, arithmetic and copies ran while one was open for 38% of the time, Pallas kernels for 7%

profile of v3, /device:TPU:0, one launch (start us, length us, event | category | flops | bytes accessed | tf_op | source)
XLA Modules:
  0.0 804.4 jit_solution(9483141877788503991)
XLA Ops:
  42.6 9.0 %collective-permute-done.5 = bf16[384,256]{1,0:T(8,128)(2,1)S(1)} collective-permute-done((bf16[384,256]{1,0:T(8,128)(2,1)}, bf16[384,256]{1,0:T(8,128)(2,1)S(1)}, u32[]{:S(2)}, u32[]{:S(2)}) %collective-permute-start.5) | collective-permute-done | bytes 196640 | tf_op jit(solution)/shard_map/ppermute | solution.py:71
  53.0 6.1 collective-permute-done.6
  99.5 7.5 all-gather.10.cloned.1.call-done
  123.4 14.3 %collective-permute-done.21 = bf16[2560,256]{0,1:T(8,128)(2,1)} collective-permute-done((bf16[2560,256]{0,1:T(8,128)(2,1)}, bf16[2560,256]{0,1:T(8,128)(2,1)}, u32[]{:S(2)}, u32[]{:S(2)}) %collective-permute-start.21) | collective-permute-done | bytes 1310752 | tf_op jit(solution)/shard_map/ppermute | solution.py:48
  162.9 7.7 shard_map.229
  186.5 10.5 %collective-permute-done.22 = bf16[2048,256]{1,0:T(8,128)(2,1)} collective-permute-done((bf16[2048,256]{1,0:T(8,128)(2,1)}, bf16[2048,256]{1,0:T(8,128)(2,1)}, u32[]{:S(2)}, u32[]{:S(2)}) %collective-permute-start.22) | collective-permute-done | bytes 1048608 | tf_op jit(solution)/shard_map/ppermute | solution.py:44
  223.9 7.4 multiply_convert_fusion.1
  246.9 8.3 %collective-permute-done.32 = bf16[2048,128]{1,0:T(8,128)(2,1)S(1)} collective-permute-done((bf16[2048,128]{1,0:T(8,128)(2,1)S(1)}, bf16[2048,128]{1,0:T(8,128)(2,1)S(1)}, u32[]{:S(2)}, u32[]{:S(2)}) %collective-permute-start.32) | collective-permute-done | bytes 524320 | tf_op jit(solution)/shard_map/ppermute | solution.py:48
  273.8 6.9 collective-permute-done.34
  293.9 7.8 shard_map.230
  306.0 11.5 %collective-permute-done.36 = bf16[2048,256]{1,0:T(8,128)(2,1)S(1)} collective-permute-done((bf16[2048,256]{1,0:T(8,128)(2,1)}, bf16[2048,256]{1,0:T(8,128)(2,1)S(1)}, u32[]{:S(2)}, u32[]{:S(2)}) %collective-permute-start.36) | collective-permute-done | bytes 1048608 | tf_op jit(solution)/shard_map/ppermute | solution.py:44
  317.7 6.4 collective-permute-done.37
  328.5 7.3 collective-permute-done.41
  338.7 7.5 multiply_convert_fusion
  357.3 5.5 convolution_convert_fusion.28
  364.8 7.6 add_convert_fusion.1
  372.4 6.8 convolution_convert_fusion.20
  400.9 10.7 %collective-permute-done.45 = bf16[2048,256]{1,0:T(8,128)(2,1)} collective-permute-done((bf16[2048,256]{1,0:T(8,128)(2,1)}, bf16[2048,256]{1,0:T(8,128)(2,1)}, u32[]{:S(2)}, u32[]{:S(2)}) %collective-permute-start.45) | collective-permute-done | bytes 1048608 | tf_op jit(solution)/shard_map/ppermute | solution.py:44
  418.1 15.9 %collective-permute-done.47 = bf16[2048,256]{1,0:T(8,128)(2,1)S(1)} collective-permute-done((bf16[2048,256]{1,0:T(8,128)(2,1)}, bf16[2048,256]{1,0:T(8,128)(2,1)S(1)}, u32[]{:S(2)}, u32[]{:S(2)}) %collective-permute-start.47) | collective-permute-done | bytes 1048608 | tf_op jit(solution)/shard_map/ppermute | solution.py:44
  451.5 25.2 %shard_map.231 = bf16[592,1536]{1,0:T(8,128)(2,1)S(1)} custom-call(bf16[592,1536]{1,0:T(8,128)(2,1)S(1)} %add_convert_fusion.2.project_ref, bf16[592,512]{1,0:T(8,128)(2,1)S(1)} %get-tuple-element.54.mixed_ref, f32[4,592,2]{2,1,0:T(8,128)S(1)} %copy-done.7, bf16[592,512]{1,0:T(8,128)(2,1)S(1)} %convolution_convert_fusion.30.delta_ref), custom_call_target="tpu_custom_call" | custom-call | flops 7177502720 | bytes 4546560 | tf_op jit(solution)/shard_map/pallas_call | solution.py:223
  487.0 5.7 collective-permute-done.50
  500.1 7.7 collective-permute-done.60
  510.1 14.4 %collective-permute-done.57 = bf16[1536,256]{1,0:T(8,128)(2,1)S(1)} collective-permute-done((bf16[1536,256]{1,0:T(8,128)(2,1)}, bf16[1536,256]{1,0:T(8,128)(2,1)S(1)}, u32[]{:S(2)}, u32[]{:S(2)}) %collective-permute-start.57) | collective-permute-done | bytes 786464 | tf_op jit(solution)/shard_map/ppermute | solution.py:44
  545.9 6.7 add_convert_fusion
  552.7 6.0 convolution_convert_fusion.19
  578.8 17.8 %collective-permute-done.55 = bf16[2048,256]{1,0:T(8,128)(2,1)} collective-permute-done((bf16[2048,256]{1,0:T(8,128)(2,1)}, bf16[2048,256]{1,0:T(8,128)(2,1)}, u32[]{:S(2)}, u32[]{:S(2)}) %collective-permute-start.55) | collective-permute-done | bytes 1048608 | tf_op jit(solution)/shard_map/ppermute | solution.py:44
  602.2 16.7 %collective-permute-done.63 = bf16[2048,256]{1,0:T(8,128)(2,1)S(1)} collective-permute-done((bf16[2048,256]{1,0:T(8,128)(2,1)}, bf16[2048,256]{1,0:T(8,128)(2,1)S(1)}, u32[]{:S(2)}, u32[]{:S(2)}) %collective-permute-start.63) | collective-permute-done | bytes 1048608 | tf_op jit(solution)/shard_map/ppermute | solution.py:44
  631.3 14.6 %shard_map.232 = bf16[592,1536]{1,0:T(8,128)(2,1)S(1)} custom-call(bf16[592,1536]{1,0:T(8,128)(2,1)S(1)} %copy-done.3, bf16[592,512]{1,0:T(8,128)(2,1)S(1)} %copy-done.1, f32[4,592,2]{2,1,0:T(8,128)S(1)} %copy-done.5, bf16[592,512]{1,0:T(8,128)(2,1)S(1)} %convolution_convert_fusion.29.delta_ref), custom_call_target="tpu_custom_call" | custom-call | flops 7177502720 | bytes 4546560 | tf_op jit(solution)/shard_map/pallas_call | solution.py:223
  725.4 11.9 %collective-permute-done.91 = f32[160,128]{1,0:T(8,128)S(1)} collective-permute-done((f32[160,128]{1,0:T(8,128)S(1)}, f32[160,128]{1,0:T(8,128)S(1)}, u32[]{:S(2)}, u32[]{:S(2)}) %collective-permute-start.91) | collective-permute-done | bytes 81952 | tf_op jit(solution)/shard_map/ppermute | solution.py:490
  743.2 8.9 %collective-permute-done.92 = f32[160,128]{1,0:T(8,128)S(1)} collective-permute-done((f32[160,128]{1,0:T(8,128)S(1)}, f32[160,128]{1,0:T(8,128)S(1)}, u32[]{:S(2)}, u32[]{:S(2)}) %collective-permute-start.92) | collective-permute-done | bytes 81952 | tf_op jit(solution)/shard_map/ppermute | solution.py:491
  755.9 6.0 collective-permute-done.83
  764.0 14.6 %all-gather.22.cloned.1.call-done = bf16[1280,1024]{1,0:T(8,128)(2,1)} async-done(((bf16[320,1024]{1,0:T(8,128)(2,1)}), bf16[1280,1024]{1,0:T(8,128)(2,1)}) %all-gather.22.cloned.1.call-update) | async-done | bytes 2621456 | tf_op jit(solution)/shard_map/all_gather | solution.py:403
  (780 shorter events, 465.3 us)
Async XLA Ops:
  7.2 99.8 %all-gather.10.cloned.1.call-start = ((), (), s32[]{:S(2)}) async-start(), calls=%async_computation.2 | async-start | bytes 1638400 | tf_op jit(solution)/shard_map/all_gather | solution.py:328
  26.3 52.7 %collective-permute-start = (bf16[320,2048]{1,0:T(8,128)(2,1)}, bf16[320,2048]{1,0:T(8,128)(2,1)}, u32[]{:S(2)}, u32[]{:S(2)}) collective-permute-start(bf16[320,2048]{1,0:T(8,128)(2,1)} %pad_maximum_fusion.2), channel_id=1, source_target_pairs={{0,4},{4,0},{1,5},{5,1},{2,6},{6,2},{3,7},{7,3},{8,12},{12,8},{9,1... | collective-permute-start | bytes 3932168 | tf_op jit(solution)/shard_map/ppermute | solution.py:56
  75.4 97.8 %all-gather.12.cloned.1.call-start = ((), (), s32[]{:S(2)}) async-start(), calls=%async_computation.3 | async-start | bytes 1310720 | tf_op jit(solution)/shard_map/all_gather | solution.py:328
  107.0 30.7 %collective-permute-start.21 = (bf16[2560,256]{0,1:T(8,128)(2,1)}, bf16[2560,256]{0,1:T(8,128)(2,1)}, u32[]{:S(2)}, u32[]{:S(2)}) collective-permute-start(bf16[2560,256]{0,1:T(8,128)(2,1)} %all-gather.10.cloned.1.call-done), channel_id=1, source_target_pairs={{0,16},{16,0},{8,24},{24,8},{1,17},{17,1},{9,25},{25,9},{2,18},{18... | collective-permute-start | bytes 3932168 | tf_op jit(solution)/shard_map/ppermute | solution.py:48
  109.4 37.4 %collective-permute-start.20 = (bf16[2560,256]{0,1:T(8,128)(2,1)}, bf16[2560,256]{0,1:T(8,128)(2,1)}, u32[]{:S(2)}, u32[]{:S(2)}) collective-permute-start(bf16[2560,256]{0,1:T(8,128)(2,1)} %all-gather.10.cloned.1.call-done), channel_id=1, source_target_pairs={{0,8},{8,0},{16,24},{24,16},{1,9},{9,1},{17,25},{25,17},{2,10},{10... | collective-permute-start | bytes 3932168 | tf_op jit(solution)/shard_map/ppermute | solution.py:44
  119.8 88.3 %all-gather.14.cloned.1.call-start = ((), (), s32[]{:S(2)}) async-start(), calls=%async_computation.4 | async-start | bytes 1310720 | tf_op jit(solution)/shard_map/all_gather | solution.py:328
  145.3 34.8 %collective-permute-start.25 = (bf16[2560,128]{0,1:T(8,128)(2,1)S(1)}, bf16[2560,128]{0,1:T(8,128)(2,1)}, u32[]{:S(2)}, u32[]{:S(2)}) collective-permute-start(bf16[2560,128]{0,1:T(8,128)(2,1)S(1)} %get-tuple-element.161), channel_id=1, source_target_pairs={{0,8},{8,0},{16,24},{24,16},{1,9},{9,1},{17,25},{25,17},{2,10},{10... | collective-permute-start | bytes 1966088 | tf_op jit(solution)/shard_map/ppermute | solution.py:44
  174.3 82.3 %all-gather.16.cloned.1.call-start = ((), (), s32[]{:S(2)}) async-start(), calls=%async_computation.5 | async-start | bytes 1310720 | tf_op jit(solution)/shard_map/all_gather | solution.py:328
  210.2 28.8 %collective-permute-start.31 = (bf16[2048,256]{1,0:T(8,128)(2,1)}, bf16[2048,256]{1,0:T(8,128)(2,1)}, u32[]{:S(2)}, u32[]{:S(2)}) collective-permute-start(bf16[2048,256]{1,0:T(8,128)(2,1)} %all-gather.14.cloned.1.call-done), channel_id=1, source_target_pairs={{0,16},{16,0},{8,24},{24,8},{1,17},{17,1},{9,25},{25,9},{2,18},{18... | collective-permute-start | bytes 3145736 | tf_op jit(solution)/shard_map/ppermute | solution.py:48
  212.3 75.5 %all-gather.18.cloned.1.call-start = ((), (), s32[]{:S(2)}) async-start(), calls=%async_computation.6 | async-start | bytes 1310720 | tf_op jit(solution)/shard_map/all_gather | solution.py:328
  235.0 34.7 %collective-permute-start.29 = (bf16[592,1024]{1,0:T(8,128)(2,1)}, bf16[592,1024]{1,0:T(8,128)(2,1)}, u32[]{:S(2)}, u32[]{:S(2)}) collective-permute-start(bf16[592,1024]{1,0:T(8,128)(2,1)} %convolution_convert_fusion.22), channel_id=1, source_target_pairs={{0,4},{4,0},{1,5},{5,1},{2,6},{6,2},{3,7},{7,3},{8,12},{12,8},{9,1... | collective-permute-start | bytes 3637256 | tf_op jit(solution)/shard_map/ppermute | solution.py:56
  258.6 404.3 %all-gather.20.cloned.1.call-start = ((), (), s32[]{:S(2)}) async-start(), calls=%async_computation.9 | async-start | bytes 3276800 | tf_op jit(solution)/shard_map/all_gather | solution.py:403
  287.8 29.7 %collective-permute-start.36 = (bf16[2048,256]{1,0:T(8,128)(2,1)}, bf16[2048,256]{1,0:T(8,128)(2,1)S(1)}, u32[]{:S(2)}, u32[]{:S(2)}) collective-permute-start(bf16[2048,256]{1,0:T(8,128)(2,1)} %all-gather.18.cloned.1.call-done), channel_id=1, source_target_pairs={{0,8},{8,0},{16,24},{24,16},{1,9},{9,1},{17,25},{25,17},{2,10},{10... | collective-permute-start | bytes 3145736 | tf_op jit(solution)/shard_map/ppermute | solution.py:44
  390.9 361.3 %reduce-scatter.5.cloned.1.call-start = ((), (), s32[]{:S(2)}) async-start(), calls=%async_computation.8 | async-start | bytes 3932160 | tf_op jit(solution)/shard_map/reduce_scatter | solution.py:437
  391.3 42.7 %collective-permute-start.47 = (bf16[2048,256]{1,0:T(8,128)(2,1)}, bf16[2048,256]{1,0:T(8,128)(2,1)S(1)}, u32[]{:S(2)}, u32[]{:S(2)}) collective-permute-start(bf16[2048,256]{1,0:T(8,128)(2,1)} %convolution_convert_fusion.12), channel_id=1, source_target_pairs={{0,8},{8,0},{16,24},{24,16},{1,9},{9,1},{17,25},{25,17},{2,10},{10... | collective-permute-start | bytes 3145736 | tf_op jit(solution)/shard_map/ppermute | solution.py:44
  391.7 44.2 %collective-permute-start.48 = (bf16[2048,256]{1,0:T(8,128)(2,1)}, bf16[2048,256]{1,0:T(8,128)(2,1)}, u32[]{:S(2)}, u32[]{:S(2)}) collective-permute-start(bf16[2048,256]{1,0:T(8,128)(2,1)} %convolution_convert_fusion.11), channel_id=1, source_target_pairs={{0,16},{16,0},{8,24},{24,8},{1,17},{17,1},{9,25},{25,9},{2,18},{18... | collective-permute-start | bytes 3145736 | tf_op jit(solution)/shard_map/ppermute | solution.py:48
  392.0 48.2 %collective-permute-start.44 = (bf16[592,1024]{1,0:T(8,128)(2,1)}, bf16[592,1024]{1,0:T(8,128)(2,1)}, u32[]{:S(2)}, u32[]{:S(2)}) collective-permute-start(bf16[592,1024]{1,0:T(8,128)(2,1)} %convolution_convert_fusion.20), channel_id=1, source_target_pairs={{0,4},{4,0},{1,5},{5,1},{2,6},{6,2},{3,7},{7,3},{8,12},{12,8},{9,1... | collective-permute-start | bytes 3637256 | tf_op jit(solution)/shard_map/ppermute | solution.py:56
  416.1 79.8 %collective-permute-start.52 = (bf16[2048,128]{1,0:T(8,128)(2,1)}, bf16[2048,128]{1,0:T(8,128)(2,1)}, u32[]{:S(2)}, u32[]{:S(2)}) collective-permute-start(bf16[2048,128]{1,0:T(8,128)(2,1)} %get-tuple-element.143), channel_id=1, source_target_pairs={{0,16},{16,0},{8,24},{24,8},{1,17},{17,1},{9,25},{25,9},{2,18},{18... | collective-permute-start | bytes 1572872 | tf_op jit(solution)/shard_map/ppermute | solution.py:48
  417.8 78.5 %collective-permute-start.53 = (bf16[2048,128]{1,0:T(8,128)(2,1)}, bf16[2048,128]{1,0:T(8,128)(2,1)}, u32[]{:S(2)}, u32[]{:S(2)}) collective-permute-start(bf16[2048,128]{1,0:T(8,128)(2,1)} %get-tuple-element.144), channel_id=1, source_target_pairs={{0,8},{8,0},{16,24},{24,16},{1,9},{9,1},{17,25},{25,17},{2,10},{10... | collective-permute-start | bytes 1572872 | tf_op jit(solution)/shard_map/ppermute | solution.py:44
  438.4 60.1 %collective-permute-start.59 = (bf16[2048,128]{1,0:T(8,128)(2,1)}, bf16[2048,128]{1,0:T(8,128)(2,1)}, u32[]{:S(2)}, u32[]{:S(2)}) collective-permute-start(bf16[2048,128]{1,0:T(8,128)(2,1)} %get-tuple-element.139), channel_id=1, source_target_pairs={{0,16},{16,0},{8,24},{24,8},{1,17},{17,1},{9,25},{25,9},{2,18},{18... | collective-permute-start | bytes 1572872 | tf_op jit(solution)/shard_map/ppermute | solution.py:48
  493.4 31.1 %collective-permute-start.57 = (bf16[1536,256]{1,0:T(8,128)(2,1)}, bf16[1536,256]{1,0:T(8,128)(2,1)S(1)}, u32[]{:S(2)}, u32[]{:S(2)}) collective-permute-start(bf16[1536,256]{1,0:T(8,128)(2,1)} %convolution_convert_fusion.18), channel_id=1, source_target_pairs={{0,8},{8,0},{16,24},{24,16},{1,9},{9,1},{17,25},{25,17},{2,10},{10... | collective-permute-start | bytes 2359304 | tf_op jit(solution)/shard_map/ppermute | solution.py:44
  495.9 28.6 %collective-permute-start.58 = (bf16[1536,256]{1,0:T(8,128)(2,1)}, bf16[1536,256]{1,0:T(8,128)(2,1)S(1)}, u32[]{:S(2)}, u32[]{:S(2)}) collective-permute-start(bf16[1536,256]{1,0:T(8,128)(2,1)} %convolution_convert_fusion.17), channel_id=1, source_target_pairs={{0,16},{16,0},{8,24},{24,8},{1,17},{17,1},{9,25},{25,9},{2,18},{18... | collective-permute-start | bytes 2359304 | tf_op jit(solution)/shard_map/ppermute | solution.py:48
  496.3 38.7 %collective-permute-start.49 = (bf16[592,1024]{1,0:T(8,128)(2,1)}, bf16[592,1024]{1,0:T(8,128)(2,1)}, u32[]{:S(2)}, u32[]{:S(2)}) collective-permute-start(bf16[592,1024]{1,0:T(8,128)(2,1)} %convolution_convert_fusion.26), channel_id=1, source_target_pairs={{0,4},{4,0},{1,5},{5,1},{2,6},{6,2},{3,7},{7,3},{8,12},{12,8},{9,1... | collective-permute-start | bytes 3637256 | tf_op jit(solution)/shard_map/ppermute | solution.py:56
  534.9 227.1 %reduce-scatter.3.cloned.1.call-start = ((), (), s32[]{:S(2)}) async-start(), calls=%async_computation.7 | async-start | bytes 2949120 | tf_op jit(solution)/shard_map/reduce_scatter | solution.py:443
  572.8 46.1 %collective-permute-start.63 = (bf16[2048,256]{1,0:T(8,128)(2,1)}, bf16[2048,256]{1,0:T(8,128)(2,1)S(1)}, u32[]{:S(2)}, u32[]{:S(2)}) collective-permute-start(bf16[2048,256]{1,0:T(8,128)(2,1)} %convolution_convert_fusion.8), channel_id=1, source_target_pairs={{0,8},{8,0},{16,24},{24,16},{1,9},{9,1},{17,25},{25,17},{2,10},{10... | collective-permute-start | bytes 3145736 | tf_op jit(solution)/shard_map/ppermute | solution.py:44
  574.1 45.8 %collective-permute-start.64 = (bf16[2048,256]{1,0:T(8,128)(2,1)}, bf16[2048,256]{1,0:T(8,128)(2,1)}, u32[]{:S(2)}, u32[]{:S(2)}) collective-permute-start(bf16[2048,256]{1,0:T(8,128)(2,1)} %convolution_convert_fusion.7), channel_id=1, source_target_pairs={{0,16},{16,0},{8,24},{24,8},{1,17},{17,1},{9,25},{25,9},{2,18},{18... | collective-permute-start | bytes 3145736 | tf_op jit(solution)/shard_map/ppermute | solution.py:48
  577.8 45.0 %collective-permute-start.54 = (bf16[592,1024]{1,0:T(8,128)(2,1)}, bf16[592,1024]{1,0:T(8,128)(2,1)S(1)}, u32[]{:S(2)}, u32[]{:S(2)}) collective-permute-start(bf16[592,1024]{1,0:T(8,128)(2,1)} %convolution_convert_fusion.19), channel_id=1, source_target_pairs={{0,4},{4,0},{1,5},{5,1},{2,6},{6,2},{3,7},{7,3},{8,12},{12,8},{9,1... | collective-permute-start | bytes 3637256 | tf_op jit(solution)/shard_map/ppermute | solution.py:56
  599.0 50.8 %collective-permute-start.65 = (bf16[2048,128]{1,0:T(8,128)(2,1)S(1)}, bf16[2048,128]{1,0:T(8,128)(2,1)S(1)}, u32[]{:S(2)}, u32[]{:S(2)}) collective-permute-start(bf16[2048,128]{1,0:T(8,128)(2,1)S(1)} %get-tuple-element.135), channel_id=1, source_target_pairs={{0,16},{16,0},{8,24},{24,8},{1,17},{17,1},{9,25},{25,9},{2,18},{18... | collective-permute-start | bytes 1572872 | tf_op jit(solution)/shard_map/ppermute | solution.py:48
  600.9 50.3 %collective-permute-start.66 = (bf16[2048,128]{1,0:T(8,128)(2,1)S(1)}, bf16[2048,128]{1,0:T(8,128)(2,1)S(1)}, u32[]{:S(2)}, u32[]{:S(2)}) collective-permute-start(bf16[2048,128]{1,0:T(8,128)(2,1)S(1)} %get-tuple-element.136), channel_id=1, source_target_pairs={{0,8},{8,0},{16,24},{24,16},{1,9},{9,1},{17,25},{25,17},{2,10},{10... | collective-permute-start | bytes 1572872 | tf_op jit(solution)/shard_map/ppermute | solution.py:44
  621.0 32.8 %collective-permute-start.68 = (bf16[2048,128]{1,0:T(8,128)(2,1)S(1)}, bf16[2048,128]{1,0:T(8,128)(2,1)S(1)}, u32[]{:S(2)}, u32[]{:S(2)}) collective-permute-start(bf16[2048,128]{1,0:T(8,128)(2,1)S(1)} %get-tuple-element.131), channel_id=1, source_target_pairs={{0,16},{16,0},{8,24},{24,8},{1,17},{17,1},{9,25},{25,9},{2,18},{18... | collective-permute-start | bytes 1572872 | tf_op jit(solution)/shard_map/ppermute | solution.py:48
  662.5 116.1 %all-gather.22.cloned.1.call-start = ((), (), s32[]{:S(2)}) async-start(), calls=%async_computation.10 | async-start | bytes 3276800 | tf_op jit(solution)/shard_map/all_gather | solution.py:403
  752.3 29.3 %collective-permute-start.87 = (bf16[1536,256]{1,0:T(8,128)(2,1)}, bf16[1536,256]{1,0:T(8,128)(2,1)S(1)}, u32[]{:S(2)}, u32[]{:S(2)}) collective-permute-start(bf16[1536,256]{1,0:T(8,128)(2,1)} %bitcast.434), channel_id=1, source_target_pairs={{0,4},{4,0},{1,5},{5,1},{2,6},{6,2},{3,7},{7,3},{8,12},{12,8},{9,1... | collective-permute-start | bytes 2359304 | tf_op jit(solution)/shard_map/ppermute | solution.py:56
  (181 other events, 2813.4 us)
Sparse Core Ops, SparseCore 0:
  75.5 31.4 all-gather.9
  119.9 25.5 all-gather.11
  174.4 27.6 all-gather.13
  212.5 27.1 all-gather.15
  258.7 27.1 all-gather.17
  391.0 52.4 all-gather.19
  535.0 59.2 reduce-scatter.4
  662.6 47.9 reduce-scatter.2
  712.8 65.8 all-gather.21

commit v4 on v3

--- a/solution.py
+++ b/solution.py
@@ -61,35 +61,35 @@
     return low.astype(F32) + swap(low).astype(F32)
 
 
-def gather_line(shard):
-    count, lane = lax.axis_size("tp"), lax.axis_index("tp")
-    up_pairs = [(j, j + 1) for j in range(count - 1)]
-    down_pairs = [(j + 1, j) for j in range(count - 1)]
-    lower, upper = [shard], [shard]
-    for step in range(count - 1):
-        lower.append(lax.ppermute(lower[-1], "tp", up_pairs[step:]))
-        upper.append(lax.ppermute(upper[-1], "tp", down_pairs[: count - 1 - step]))
-    placed = []
-    for owner in range(count):
-        piece = shard
-        for away in range(1, count):
-            piece = jnp.where(lane == owner + away, lower[away], piece)
-            piece = jnp.where(lane == owner - away, upper[away], piece)
-        placed.append(piece)
-    return jnp.stack(placed)
-
-
-def scatter_line(full):
-    count, lane = lax.axis_size("tp"), lax.axis_index("tp")
-    take = lambda k: lax.dynamic_index_in_dim(full, jnp.clip(k, 0, count - 1), 0, keepdims=False)
-    rising = falling = None
-    for step in range(count - 1):
-        to_up, to_down = take(lane + count - 1 - step), take(lane - (count - 1 - step))
-        if step:
-            to_up, to_down = to_up + rising, to_down + falling
-        rising = lax.ppermute(to_up, "tp", [(j, j + 1) for j in range(step + 1)])
-        falling = lax.ppermute(to_down, "tp", [(j + 1, j) for j in range(count - 2 - step, count - 1)])
-    return (take(lane).astype(F32) + rising.astype(F32) + falling.astype(F32)).astype(BF)
+def tp_bits():
+    count = lax.axis_size("tp")
+    bits = [1 << k for k in reversed(range(count.bit_length() - 1))]
+    assert 1 << len(bits) == count
+    return [(bit, axis) for axis, bit in enumerate(bits)]
+
+
+def tp_partner(values, bit):
+    return lax.ppermute(values, "tp", [(j, j ^ bit) for j in range(lax.axis_size("tp"))])
+
+
+def gather_pairs(shard):
+    lane, held = lax.axis_index("tp"), shard
+    for bit, axis in tp_bits():
+        other = tp_partner(held, bit)
+        upper = (lane & bit) != 0
+        held = jnp.stack([jnp.where(upper, other, held), jnp.where(upper, held, other)], axis=axis)
+    return held.reshape((-1,) + shard.shape)
+
+
+def scatter_pairs(full):
+    lane, bits = lax.axis_index("tp"), tp_bits()
+    held = full.reshape((2,) * len(bits) + full.shape[1:])
+    for bit, axis in reversed(bits):
+        mine = jnp.where((lane & bit) != 0, 1, 0)
+        take = lambda k: lax.dynamic_index_in_dim(held, k, axis, keepdims=False)
+        other = tp_partner(take(1 - mine), bit)
+        held = (take(mine).astype(F32) + other.astype(F32)).astype(BF)
+    return held
 
 
 def gather_features(along, previous):
@@ -126,18 +126,24 @@
     return mm_tn(delta, values[:, : 4 * half]).astype(BF), from_x, from_y
 
 
-def gradient_finish(begun, *earlier):
+def gradient_second(begun, marker):
     if not square():
         return begun
     kept, from_x, from_y = begun
     half = from_x.shape[1] // 2
-    if earlier:
-        from_x, from_y = lax.optimization_barrier((from_x, from_y) + earlier)[:2]
+    from_x, from_y = lax.optimization_barrier((from_x, from_y, marker))[:2]
     own_a, own_b, x_b, y_a = jnp.split(kept, 4, axis=1)
     last_a = send_y(y_a + from_x[:, half:])
     last_b = send_x(x_b + from_y[:, :half])
-    add = lambda *terms: sum(term.astype(F32) for term in terms).astype(BF)
-    return jnp.concatenate([add(own_a, from_x[:, :half], last_a), add(own_b, from_y[:, half:], last_b)], axis=1)
+    return (own_a, from_x[:, :half], last_a), (own_b, from_y[:, half:], last_b)
+
+
+def gradient_finish(terms, marker):
+    if not square():
+        return terms
+    last_a, last_b = lax.optimization_barrier((terms[0][2], terms[1][2], marker))[:2]
+    add = lambda own, near, last: (own.astype(F32) + near.astype(F32) + last.astype(F32)).astype(BF)
+    return jnp.concatenate([add(*terms[0][:2], last_a), add(*terms[1][:2], last_b)], axis=1)
 
 
 def mm(left, right):
@@ -263,12 +269,13 @@
     grad_attend = grad_middle.astype(BF)
     grad_attend = gate("attend", grad_attend)
     emit("out", mixed, grad_attend)
-    delta_mixed = mm_nt(grad_attend, out).astype(BF)
+    delta_mixed = gate("mixed", mm_nt(grad_attend, out).astype(BF))
     tile = mixed.shape[1] // lax.axis_size("tp")
     delta_project = attend_back(project, mixed, totals, delta_mixed, tile)
     delta_project = gate("project", delta_project)
-    emit("qkv", delta_project, normed)
-    delta_normed = both_cores(mm(delta_project, qkv))
+    low = mm(delta_project, qkv).astype(BF)
+    emit("qkv", after(delta_project, low), normed)
+    delta_normed = gate("normed", low.astype(F32) + swap(low).astype(F32))
     back_stream, delta_gain_first = jax.vjp(layer_norm, stream, gain_first)[1](delta_normed)
     sums = (
         total(delta_project),
@@ -317,16 +324,19 @@
         cut.append((qkv, halves(out_weight[l], 0), halves(up_weight[l], 1).T, halves(down_weight[l], 0)))
     heights = [piece.shape[0] for piece in cut[0]]
     joined = lambda l, members: jnp.concatenate([cut[l][k] for k in members], axis=0)
-    groups = [[(0,), (1, 2), (3,)]] + [[(0, 1), (2,), (3,)]] * (layers - 1)
-    stages, along = [], ()
-    for l in range(layers):
-        for members in groups[l]:
-            shard = after(joined(l, members), *along)
-            if l == 0 and members == (0,):
-                along = (gather_line(shard).reshape(-1, shard.shape[1]),)
-            else:
-                along = (lax.all_gather(shard, "tp", axis=0, tiled=True),)
-            stages.append((l, members, along[0]))
+    rows_of = lambda gathered, start, stop: gathered.reshape(n_tp, -1, gathered.shape[-1])[:, start:stop]
+    first_along = gather_pairs(joined(0, (0,)))
+    second_along = gather_pairs(after(joined(0, (1, 2)), first_along))
+    stages = [(0, (0,), first_along), (0, (1, 2), second_along)]
+    for l, members in [(0, (3,))] + [(l, some) for l in range(1, layers) for some in ((0, 1), (2, 3))]:
+        gathered = lax.all_gather(after(joined(l, members), first_along), "tp", axis=0, tiled=True)
+        first_along = gathered
+        if members == (2, 3):
+            stages.append((l, (2,), rows_of(gathered, 0, heights[2])))
+            stages.append((l, (3,), rows_of(gathered, heights[2], None)))
+        else:
+            stages.append((l, members, gathered))
+    stages = [(l, members, along.reshape(-1, along.shape[-1])) for l, members, along in stages]
     first_along = stages[0][2]
 
     pieces = (qv_bias, up_bias, out_bias, down_bias, gain_one, gain_two)
@@ -340,7 +350,7 @@
         spread = lax.all_gather(packed[0], "fsdp", axis=0)
     order = order_matrix(features)
     split = qv_bias.size + up_bias.size
-    across = gather_line(after(spread[:, :split], first_along))
+    across = gather_pairs(after(spread[:, :split], first_along))
 
     def by_core(array, count):
         array = array.reshape(n_tp, n_fsdp, layers, count, -1)
@@ -408,7 +418,22 @@
     names = ("down", "up", "out", "qkv")
     begun, found = {}, {}
     sums = [None] * layers
-    mine = [None] * layers
+
+    further, along = {}, {}
+
+    def second(layer, some, marker):
+        held = ()
+        for name in some:
+            further[layer, name] = gradient_second(begun[layer, name], marker)
+            held += begun[layer, name][1:] if square() else ()
+        return held
+
+    def finish(layer, some, marker):
+        for name in some:
+            found[layer, name] = gradient_finish(further[layer, name], marker)
+
+    def along_tp(layer, some):
+        return lax.psum_scatter(reduced(layer, some), "tp", scatter_dimension=0, tiled=False)
 
     def reduced(layer, some):
         joined = [found[layer, name].reshape(n_tp, -1, features // n_fsdp) for name in some]
@@ -419,31 +444,34 @@
         def emit(name, delta, values, l=l):
             begun[l, name] = gradient_start(delta, values)
 
-        def first(name, layer):
-            found[layer, name] = gradient_finish(begun[layer, name])
-            return begun[layer, name][1:] if square() else ()
-
         def gate(point, value, l=l):
             held = ()
-            if point == "hidden" and l < layers - 1:
-                held = first("out", l + 1) + (found[l + 1, "down"],)
-            if point == "attend":
-                held = first("down", l)
-                if l < layers - 1:
-                    held += first("qkv", l + 1) + (found[l + 1, "up"], found[l + 1, "out"])
-            if point == "project":
-                held = first("up", l)
-                if l < layers - 1:
-                    mine[l + 1] = lax.psum_scatter(reduced(l + 1, names), "tp", scatter_dimension=0, tiled=False)
-                    held += (output, found[l, "down"])
+            if l == layers - 1:
+                if point == "project":
+                    held = second(l, ("down", "up"), value)
+            elif point == "hidden":
+                held = second(l + 1, ("out", "qkv"), value)
+                finish(l + 1, ("down", "up"), value)
+                along[l + 1] = [along_tp(l + 1, names[:2])]
+            elif point == "attend":
+                finish(l + 1, ("out", "qkv"), value)
+                along[l + 1].append(along_tp(l + 1, names[2:]))
+            elif point == "project":
+                held = second(l, ("down", "up", "out"), value)
+                held += (output, along[l + 1][0], found[l + 1, "out"], found[l + 1, "qkv"])
+            elif point == "normed":
+                finish(l, ("down",), value)
             return after(value, *held)
 
         gradient, sums[l] = backward_layer(gradient, saved[l], weights[l], vectors[l], emit, gate)
-    found[0, "out"] = gradient_finish(begun[0, "out"])
-    early = lax.psum_scatter(reduced(0, names[:3]), "tp", scatter_dimension=0, tiled=False)
-    found[0, "qkv"] = gradient_finish(begun[0, "qkv"])
-    mine[0] = jnp.concatenate([early, scatter_line(reduced(0, names[3:]))], axis=0)
-    input_grad = to_all(give_back(gradient))
+    local_grad = give_back(gradient)
+    second(0, names[3:], local_grad)
+    finish(0, names[1:], local_grad)
+    pieces = [scatter_pairs(reduced(0, some)) for some in (names[:1], names[1:2], names[2:])]
+    mine = [jnp.concatenate(pieces, axis=0)] + [
+        after(jnp.concatenate(along[l], axis=0), local_grad) for l in range(1, layers)
+    ]
+    input_grad = to_all(after(local_grad, *along[1]))
 
     grads = {name: [] for name in names}
     heights = [found[0, name].shape[0] // n_tp for name in names]

time: 812 us -> 745 us (0.917)
  local copies, waits for them, and re-layouts: 145 us -> 118 us
  starting transfers between devices: 98.2 us -> 75.1 us
  matrix products: 143 us -> 131 us
  other arithmetic: 85.7 us -> 96.5 us
  Pallas kernels: 55.3 us -> 45.4 us
    ppermute x30, waiting for transfers between devices: 127 us -> 85.7 us  [send_x(): return lax.ppermute(values, 'fsdp', X_PAIRS)]
    ppermute x18 -> x12, waiting for transfers between devices: 31.5 us -> 62.1 us  [tp_partner(): lax.ppermute(values, 'tp', [(j, j ^ bit) for j in range(lax.axis_size('tp...]
    ppermute x18 -> x12, starting transfers between devices: 31 us -> 9.61 us  [tp_partner(): lax.ppermute(values, 'tp', [(j, j ^ bit) for j in range(lax.axis_size('tp...]
    ppermute x31, waiting for transfers between devices: 56.2 us -> 71.9 us  [send_y(): return lax.ppermute(values, 'fsdp', Y_PAIRS)]
    unnamed x280 -> x365, local copies, waits for them, and re-layouts: 60.7 us -> 45.4 us
    all_gather x2, waiting for transfers between devices: 14.6 us -> 0.01 us  [to_all(): return lax.all_gather(values, 'tp', axis=0)[:slots]]
    slice x34 -> x28, local copies, waits for them, and re-layouts: 15.8 us -> 2.78 us  [gather_group(): piece[:, start:start + height].reshape(count * height, -1)]
    pallas_call x2, Pallas kernels: 39.8 us -> 29.7 us  [attend_back(): pl.pallas_call(attend_back_kernel, grid=(count,), in_specs=[wide, narrow,...]
  transfers between devices with their start and end apart: 102 -> 94, of which waited for: 43 -> 36; matrix products, arithmetic and copies ran while one was open for 38% -> 38% of each run, Pallas kernels for 7% -> 6%
where the time goes in v4:
time: 745 us; the launch traced here: 738 us
  waiting for transfers between devices  253 us (34%)
  matrix products  131 us (18%)
  local copies, waits for them, and re-layouts  118 us (16%)
  other arithmetic  96.5 us (13%)
  starting transfers between devices  75.1 us (10%)
  Pallas kernels  45.4 us (6%)
  between operations  18.7 us (3%)
    ppermute x30, waiting for transfers between devices, send_x(): return lax.ppermute(values, 'fsdp', X_PAIRS)  85.7 us
    ppermute x31, waiting for transfers between devices, send_y(): return lax.ppermute(values, 'fsdp', Y_PAIRS)  71.9 us
    ppermute x12, waiting for transfers between devices, tp_partner(): lax.ppermute(values, 'tp', [(j, j ^ bit) for j in range(lax.axis_size('tp...  62.1 us
    dot_general x24, matrix products, mm_tn(): lax.dot_general(left, right, (((0,), (0,)), ((), ())), preferred_element_...  50.7 us
    dot_general x14, matrix products, mm(): return jnp.dot(left, right, preferred_element_type=F32)  46.7 us
    unnamed x365, local copies, waits for them, and re-layouts  45.4 us
    dot_general x8, matrix products, mm_nt(): lax.dot_general(left, right, (((1,), (1,)), ((), ())), preferred_element_...  31.4 us
    ppermute x31, starting transfers between devices, send_y(): return lax.ppermute(values, 'fsdp', Y_PAIRS)  31.2 us
  transfers between devices with their start and end apart: 94, of which 36 were waited for; matrix products, arithmetic and copies ran while one was open for 38% of the time, Pallas kernels for 6%

profile of v4, /device:TPU:0, one launch (start us, length us, event | category | flops | bytes accessed | tf_op | source)
XLA Modules:
  0.0 738.0 jit_solution(13628070636061167370)
XLA Ops:
  40.8 7.9 %collective-permute-done.5 = bf16[2,384,256]{2,1,0:T(8,128)(2,1)S(1)} collective-permute-done((bf16[2,384,256]{2,1,0:T(8,128)(2,1)S(1)}, bf16[2,384,256]{2,1,0:T(8,128)(2,1)S(1)}, u32[]{:S(2)}, u32[]{:S(2)}) %collective-permute-start.5) | collective-permute-done | bytes 393248 | tf_op jit(solution)/shard_map/ppermute | solution.py:72
  77.4 5.4 collective-permute-done.12
  95.1 7.0 collective-permute-done.13
  110.7 23.0 %collective-permute-done.14 = bf16[2560,256]{1,0:T(8,128)(2,1)} collective-permute-done((bf16[2560,256]{1,0:T(8,128)(2,1)S(1)}, bf16[2560,256]{1,0:T(8,128)(2,1)}, u32[]{:S(2)}, u32[]{:S(2)}) %collective-permute-start.14) | collective-permute-done | bytes 1310752 | tf_op jit(solution)/shard_map/ppermute | solution.py:44
  146.8 7.7 %shard_map.229 = (bf16[592,512]{1,0:T(8,128)(2,1)S(1)}, f32[4,592,2]{2,1,0:T(8,128)S(1)}) custom-call(bf16[592,1536]{1,0:T(8,128)(2,1)S(1)} %add_convert_fusion.3.project_ref), custom_call_target="tpu_custom_call" | custom-call | flops 2871001088 | bytes 2424832 | tf_op jit(solution)/shard_map/pallas_call | solution.py:211
  154.6 18.5 %collective-permute-done.18 = bf16[2560,128]{1,0:T(8,128)(2,1)S(1)} collective-permute-done((bf16[2560,128]{1,0:T(8,128)(2,1)S(1)}, bf16[2560,128]{1,0:T(8,128)(2,1)S(1)}, u32[]{:S(2)}, u32[]{:S(2)}) %collective-permute-start.18) | collective-permute-done | bytes 655392 | tf_op jit(solution)/shard_map/ppermute | solution.py:48
  190.8 22.1 %collective-permute-done.21 = bf16[2048,128]{1,0:T(8,128)(2,1)S(1)} collective-permute-done((bf16[2048,128]{1,0:T(8,128)(2,1)S(1)}, bf16[2048,128]{1,0:T(8,128)(2,1)S(1)}, u32[]{:S(2)}, u32[]{:S(2)}) %collective-permute-start.21) | collective-permute-done | bytes 524320 | tf_op jit(solution)/shard_map/ppermute | solution.py:48
  218.6 7.5 %multiply_convert_fusion.1 = (bf16[592,2048]{1,0:T(8,128)(2,1)S(1)}, f32[592,2048]{1,0:T(8,128)}) fusion(f32[2048]{0:T(1024)S(1)} %bitcast.509, bf16[592,1024]{1,0:T(8,128)(2,1)S(1)} %multiply_convert_fusion.4, bf16[2048,1024]{1,0:T(8,128)(2,1)} %constant_dynamic-update-slice_fusion.18), kind=kOutput, calls=%fused_computation.6 | convolution fusion | flops 2490302464 | bytes 12689408 | tf_op jit(solution)/shard_map/dot_general | solution.py:154
  232.4 4.9 reshape.569
  242.8 22.2 %collective-permute-done.28 = bf16[2048,256]{0,1:T(8,128)(2,1)S(1)} collective-permute-done((bf16[2048,256]{0,1:T(8,128)(2,1)S(1)}, bf16[2048,256]{0,1:T(8,128)(2,1)S(1)}, u32[]{:S(2)}, u32[]{:S(2)}) %collective-permute-start.28) | collective-permute-done | bytes 1048608 | tf_op jit(solution)/shard_map/ppermute | solution.py:44
  272.7 7.9 %shard_map.230 = (bf16[592,512]{1,0:T(8,128)(2,1)S(1)}, f32[4,592,2]{2,1,0:T(8,128)S(1)}) custom-call(bf16[592,1536]{1,0:T(8,128)(2,1)S(1)} %add_convert_fusion.2.project_ref), custom_call_target="tpu_custom_call" | custom-call | flops 2871001088 | bytes 2424832 | tf_op jit(solution)/shard_map/pallas_call | solution.py:211
  282.1 19.3 %collective-permute-done.34 = bf16[2048,128]{0,1:T(8,128)(2,1)S(1)} collective-permute-done((bf16[2048,128]{0,1:T(8,128)(2,1)S(1)}, bf16[2048,128]{0,1:T(8,128)(2,1)S(1)}, u32[]{:S(2)}, u32[]{:S(2)}) %collective-permute-start.34) | collective-permute-done | bytes 524320 | tf_op jit(solution)/shard_map/ppermute | solution.py:44
  305.1 8.9 %collective-permute-done.35 = bf16[2048,128]{0,1:T(8,128)(2,1)S(1)} collective-permute-done((bf16[2048,128]{0,1:T(8,128)(2,1)S(1)}, bf16[2048,128]{0,1:T(8,128)(2,1)S(1)}, u32[]{:S(2)}, u32[]{:S(2)}) %collective-permute-start.35) | collective-permute-done | bytes 524320 | tf_op jit(solution)/shard_map/ppermute | solution.py:48
  317.3 4.7 multiply_convert_fusion
  332.6 5.5 convolution_convert_fusion.28
  340.0 8.2 %add_convert_fusion.1 = bf16[592,2048]{1,0:T(8,128)(2,1)S(1)} fusion(f32[592,2048]{1,0:T(8,128)} %get-tuple-element.312, f32[2048]{0:T(1024)S(1)} %bitcast.512, bf16[592,1024]{1,0:T(8,128)(2,1)S(1)} %get-tuple-element.180, bf16[2048,1024]{0,1:T(8,128)(2,1)} %copy-done.87), kind=kOutput, calls=%fused_computation.3 | convolution fusion | flops 2500001792 | bytes 12689408 | tf_op jit(solution)/shard_map/dot_general | solution.py:154
  367.5 5.2 convolution_convert_fusion.6
  385.3 14.7 %shard_map.231 = bf16[592,1536]{1,0:T(8,128)(2,1)S(1)} custom-call(bf16[592,1536]{1,0:T(8,128)(2,1)S(1)} %add_convert_fusion.2.project_ref, bf16[592,512]{1,0:T(8,128)(2,1)S(1)} %get-tuple-element.86.mixed_ref, f32[4,592,2]{2,1,0:T(8,128)S(1)} %copy-done.7, bf16[592,512]{1,0:T(8,128)(2,1)S(1)} %convolution_convert_fusion.30.delta_ref), custom_call_target="tpu_custom_call" | custom-call | flops 7177502720 | bytes 4546560 | tf_op jit(solution)/shard_map/pallas_call | solution.py:229
  400.1 7.0 collective-permute-done.40
  439.6 5.2 add_convert_fusion
  451.3 5.9 convolution_convert_fusion.19
  464.4 5.2 collective-permute-done.57
  506.1 15.0 %shard_map.232 = bf16[592,1536]{1,0:T(8,128)(2,1)S(1)} custom-call(bf16[592,1536]{1,0:T(8,128)(2,1)S(1)} %copy-done.3, bf16[592,512]{1,0:T(8,128)(2,1)S(1)} %copy-done.1, f32[4,592,2]{2,1,0:T(8,128)S(1)} %copy-done.5, bf16[592,512]{1,0:T(8,128)(2,1)S(1)} %convolution_convert_fusion.29.delta_ref), custom_call_target="tpu_custom_call" | custom-call | flops 7177502720 | bytes 4546560 | tf_op jit(solution)/shard_map/pallas_call | solution.py:229
  526.9 4.8 collective-permute-done.62
  557.9 5.0 convolution_convert_fusion.25
  586.8 5.5 convolution_convert_fusion.27
  603.3 7.5 %collective-permute-done.74 = bf16[1536,256]{0,1:T(8,128)(2,1)S(1)} collective-permute-done((bf16[1536,256]{0,1:T(8,128)(2,1)}, bf16[1536,256]{0,1:T(8,128)(2,1)S(1)}, u32[]{:S(2)}, u32[]{:S(2)}) %collective-permute-start.74) | collective-permute-done | bytes 786464 | tf_op jit(solution)/shard_map/ppermute | solution.py:44
  626.8 19.6 %collective-permute-done.85 = f32[160,128]{1,0:T(8,128)S(1)} collective-permute-done((f32[160,128]{1,0:T(8,128)S(1)}, f32[160,128]{1,0:T(8,128)S(1)}, u32[]{:S(2)}, u32[]{:S(2)}) %collective-permute-start.85) | collective-permute-done | bytes 81952 | tf_op jit(solution)/shard_map/ppermute | solution.py:518
  652.4 5.5 collective-permute-done.86
  670.3 17.0 %collective-permute-done.67 = bf16[512,256]{1,0:T(8,128)(2,1)} collective-permute-done((bf16[512,256]{1,0:T(8,128)(2,1)S(1)}, bf16[512,256]{1,0:T(8,128)(2,1)}, u32[]{:S(2)}, u32[]{:S(2)}) %collective-permute-start.67) | collective-permute-done | bytes 262176 | tf_op jit(solution)/shard_map/ppermute | solution.py:72
  688.5 8.8 %collective-permute-done.78 = bf16[2,512,256]{2,1,0:T(8,128)(2,1)} collective-permute-done((bf16[2,512,256]{2,1,0:T(8,128)(2,1)}, bf16[2,512,256]{2,1,0:T(8,128)(2,1)}, u32[]{:S(2)}, u32[]{:S(2)}) %collective-permute-start.78) | collective-permute-done | bytes 524320 | tf_op jit(solution)/shard_map/ppermute | solution.py:72
  699.7 12.5 %collective-permute-done.79 = bf16[512,256]{1,0:T(8,128)(2,1)S(1)} collective-permute-done((bf16[512,256]{1,0:T(8,128)(2,1)S(1)}, bf16[512,256]{1,0:T(8,128)(2,1)S(1)}, u32[]{:S(2)}, u32[]{:S(2)}) %collective-permute-start.79) | collective-permute-done | bytes 262176 | tf_op jit(solution)/shard_map/ppermute | solution.py:72
  (853 shorter events, 394.0 us)
Async XLA Ops:
  7.2 103.4 %all-gather.8.cloned.1.call-start = ((), (), s32[]{:S(2)}) async-start(), calls=%async_computation.2 | async-start | bytes 1310720 | tf_op jit(solution)/shard_map/all_gather | solution.py:332
  23.2 59.8 %collective-permute-start = (bf16[320,2048]{1,0:T(8,128)(2,1)}, bf16[320,2048]{1,0:T(8,128)(2,1)}, u32[]{:S(2)}, u32[]{:S(2)}) collective-permute-start(bf16[320,2048]{1,0:T(8,128)(2,1)} %pad_maximum_fusion.1), channel_id=1, source_target_pairs={{0,4},{4,0},{1,5},{5,1},{2,6},{6,2},{3,7},{7,3},{8,12},{12,8},{9,1... | collective-permute-start | bytes 3932168 | tf_op jit(solution)/shard_map/ppermute | solution.py:56
  49.9 40.2 %collective-permute-start.6 = (bf16[1536,256]{1,0:T(8,128)(2,1)S(1)}, bf16[1536,256]{1,0:T(8,128)(2,1)}, u32[]{:S(2)}, u32[]{:S(2)}) collective-permute-start(bf16[1536,256]{1,0:T(8,128)(2,1)S(1)} %bitcast.380), channel_id=1, source_target_pairs={{0,8},{8,0},{16,24},{24,16},{1,9},{9,1},{17,25},{25,17},{2,10},{10... | collective-permute-start | bytes 2359304 | tf_op jit(solution)/shard_map/ppermute | solution.py:44
  50.5 41.5 %collective-permute-start.7 = (bf16[1536,256]{1,0:T(8,128)(2,1)S(1)}, bf16[1536,256]{1,0:T(8,128)(2,1)S(1)}, u32[]{:S(2)}, u32[]{:S(2)}) collective-permute-start(bf16[1536,256]{1,0:T(8,128)(2,1)S(1)} %bitcast.381), channel_id=1, source_target_pairs={{0,16},{16,0},{8,24},{24,8},{1,17},{17,1},{9,25},{25,9},{2,18},{18... | collective-permute-start | bytes 2359304 | tf_op jit(solution)/shard_map/ppermute | solution.py:48
  57.1 120.9 %all-gather.10.cloned.1.call-start = ((), (), s32[]{:S(2)}) async-start(), calls=%async_computation.3 | async-start | bytes 1310720 | tf_op jit(solution)/shard_map/all_gather | solution.py:332
  110.7 121.7 %all-gather.12.cloned.1.call-start = ((), (), s32[]{:S(2)}) async-start(), calls=%async_computation.4 | async-start | bytes 2621440 | tf_op jit(solution)/shard_map/all_gather | solution.py:332
  133.9 44.6 %collective-permute-start.16 = (bf16[2048,256]{1,0:T(8,128)(2,1)}, bf16[2048,256]{1,0:T(8,128)(2,1)}, u32[]{:S(2)}, u32[]{:S(2)}) collective-permute-start(bf16[2048,256]{1,0:T(8,128)(2,1)} %all-gather.8.cloned.1.call-done), channel_id=1, source_target_pairs={{0,8},{8,0},{16,24},{24,16},{1,9},{9,1},{17,25},{25,17},{2,10},{10... | collective-permute-start | bytes 3145736 | tf_op jit(solution)/shard_map/ppermute | solution.py:44
  135.4 43.0 %collective-permute-start.17 = (bf16[2048,256]{1,0:T(8,128)(2,1)}, bf16[2048,256]{1,0:T(8,128)(2,1)S(1)}, u32[]{:S(2)}, u32[]{:S(2)}) collective-permute-start(bf16[2048,256]{1,0:T(8,128)(2,1)} %all-gather.8.cloned.1.call-done), channel_id=1, source_target_pairs={{0,16},{16,0},{8,24},{24,8},{1,17},{17,1},{9,25},{25,9},{2,18},{18... | collective-permute-start | bytes 3145736 | tf_op jit(solution)/shard_map/ppermute | solution.py:48
  178.0 376.9 %all-gather.14.cloned.1.call-start = ((), (), s32[]{:S(2)}) async-start(), calls=%async_computation.7 | async-start | bytes 3276800 | tf_op jit(solution)/shard_map/all_gather | solution.py:413
  178.5 35.1 %collective-permute-start.24 = (bf16[2048,256]{1,0:T(8,128)(2,1)}, bf16[2048,256]{1,0:T(8,128)(2,1)S(1)}, u32[]{:S(2)}, u32[]{:S(2)}) collective-permute-start(bf16[2048,256]{1,0:T(8,128)(2,1)} %all-gather.10.cloned.1.call-done), channel_id=1, source_target_pairs={{0,8},{8,0},{16,24},{24,16},{1,9},{9,1},{17,25},{25,17},{2,10},{10... | collective-permute-start | bytes 3145736 | tf_op jit(solution)/shard_map/ppermute | solution.py:44
  179.1 34.5 %collective-permute-start.25 = (bf16[2048,256]{1,0:T(8,128)(2,1)}, bf16[2048,256]{1,0:T(8,128)(2,1)S(1)}, u32[]{:S(2)}, u32[]{:S(2)}) collective-permute-start(bf16[2048,256]{1,0:T(8,128)(2,1)} %all-gather.10.cloned.1.call-done), channel_id=1, source_target_pairs={{0,16},{16,0},{8,24},{24,8},{1,17},{17,1},{9,25},{25,9},{2,18},{18... | collective-permute-start | bytes 3145736 | tf_op jit(solution)/shard_map/ppermute | solution.py:48
  266.1 35.3 %collective-permute-start.30 = (bf16[2048,256]{0,1:T(8,128)(2,1)S(1)}, bf16[2048,256]{0,1:T(8,128)(2,1)S(1)}, u32[]{:S(2)}, u32[]{:S(2)}) collective-permute-start(bf16[2048,256]{0,1:T(8,128)(2,1)S(1)} %bitcast.369), channel_id=1, source_target_pairs={{0,8},{8,0},{16,24},{24,16},{1,9},{9,1},{17,25},{25,17},{2,10},{10... | collective-permute-start | bytes 3145736 | tf_op jit(solution)/shard_map/ppermute | solution.py:44
  358.8 41.3 %collective-permute-start.42 = (bf16[2048,256]{1,0:T(8,128)(2,1)}, bf16[2048,256]{1,0:T(8,128)(2,1)S(1)}, u32[]{:S(2)}, u32[]{:S(2)}) collective-permute-start(bf16[2048,256]{1,0:T(8,128)(2,1)} %convolution_convert_fusion.11), channel_id=1, source_target_pairs={{0,16},{16,0},{8,24},{24,8},{1,17},{17,1},{9,25},{25,9},{2,18},{18... | collective-permute-start | bytes 3145736 | tf_op jit(solution)/shard_map/ppermute | solution.py:48
  359.7 40.4 %collective-permute-start.41 = (bf16[2048,256]{1,0:T(8,128)(2,1)}, bf16[2048,256]{1,0:T(8,128)(2,1)}, u32[]{:S(2)}, u32[]{:S(2)}) collective-permute-start(bf16[2048,256]{1,0:T(8,128)(2,1)} %convolution_convert_fusion.12), channel_id=1, source_target_pairs={{0,8},{8,0},{16,24},{24,16},{1,9},{9,1},{17,25},{25,17},{2,10},{10... | collective-permute-start | bytes 3145736 | tf_op jit(solution)/shard_map/ppermute | solution.py:44
  361.0 46.1 %collective-permute-start.40 = (bf16[2048,256]{1,0:T(8,128)(2,1)}, bf16[2048,256]{1,0:T(8,128)(2,1)}, u32[]{:S(2)}, u32[]{:S(2)}) collective-permute-start(bf16[2048,256]{1,0:T(8,128)(2,1)} %convolution_convert_fusion.13), channel_id=1, source_target_pairs={{0,16},{16,0},{8,24},{24,8},{1,17},{17,1},{9,25},{25,9},{2,18},{18... | collective-permute-start | bytes 3145736 | tf_op jit(solution)/shard_map/ppermute | solution.py:48
  363.5 44.3 %collective-permute-start.39 = (bf16[2048,256]{1,0:T(8,128)(2,1)}, bf16[2048,256]{1,0:T(8,128)(2,1)}, u32[]{:S(2)}, u32[]{:S(2)}) collective-permute-start(bf16[2048,256]{1,0:T(8,128)(2,1)} %convolution_convert_fusion.14), channel_id=1, source_target_pairs={{0,8},{8,0},{16,24},{24,16},{1,9},{9,1},{17,25},{25,17},{2,10},{10... | collective-permute-start | bytes 3145736 | tf_op jit(solution)/shard_map/ppermute | solution.py:44
  364.9 193.0 %reduce-scatter.3.cloned.1.call-start = ((), (), s32[]{:S(2)}) async-start(), calls=%async_computation.5 | async-start | bytes 2621440 | tf_op jit(solution)/shard_map/reduce_scatter | solution.py:436
  450.3 70.8 %collective-permute-start.50 = (bf16[2048,256]{1,0:T(8,128)(2,1)}, bf16[2048,256]{1,0:T(8,128)(2,1)S(1)}, u32[]{:S(2)}, u32[]{:S(2)}) collective-permute-start(bf16[2048,256]{1,0:T(8,128)(2,1)} %convolution_convert_fusion.9), channel_id=1, source_target_pairs={{0,16},{16,0},{8,24},{24,8},{1,17},{17,1},{9,25},{25,9},{2,18},{18... | collective-permute-start | bytes 3145736 | tf_op jit(solution)/shard_map/ppermute | solution.py:48
  459.3 63.4 %collective-permute-start.49 = (bf16[2048,256]{1,0:T(8,128)(2,1)}, bf16[2048,256]{1,0:T(8,128)(2,1)}, u32[]{:S(2)}, u32[]{:S(2)}) collective-permute-start(bf16[2048,256]{1,0:T(8,128)(2,1)} %convolution_convert_fusion.10), channel_id=1, source_target_pairs={{0,8},{8,0},{16,24},{24,16},{1,9},{9,1},{17,25},{25,17},{2,10},{10... | collective-permute-start | bytes 3145736 | tf_op jit(solution)/shard_map/ppermute | solution.py:44
  469.6 53.9 %collective-permute-start.61 = (bf16[1536,128]{1,0:T(8,128)(2,1)}, bf16[1536,128]{1,0:T(8,128)(2,1)}, u32[]{:S(2)}, u32[]{:S(2)}) collective-permute-start(bf16[1536,128]{1,0:T(8,128)(2,1)} %get-tuple-element.224), channel_id=1, source_target_pairs={{0,16},{16,0},{8,24},{24,8},{1,17},{17,1},{9,25},{25,9},{2,18},{18... | collective-permute-start | bytes 1179656 | tf_op jit(solution)/shard_map/ppermute | solution.py:48
  476.6 62.3 %collective-permute-start.52 = (bf16[2048,256]{1,0:T(8,128)(2,1)}, bf16[2048,256]{1,0:T(8,128)(2,1)}, u32[]{:S(2)}, u32[]{:S(2)}) collective-permute-start(bf16[2048,256]{1,0:T(8,128)(2,1)} %convolution_convert_fusion.7), channel_id=1, source_target_pairs={{0,16},{16,0},{8,24},{24,8},{1,17},{17,1},{9,25},{25,9},{2,18},{18... | collective-permute-start | bytes 3145736 | tf_op jit(solution)/shard_map/ppermute | solution.py:48
  485.1 83.0 %reduce-scatter.5.cloned.1.call-start = ((), (), s32[]{:S(2)}) async-start(), calls=%async_computation.6 | async-start | bytes 1310720 | tf_op jit(solution)/shard_map/reduce_scatter | solution.py:436
  495.6 43.5 %collective-permute-start.51 = (bf16[2048,256]{1,0:T(8,128)(2,1)S(1)}, bf16[2048,256]{1,0:T(8,128)(2,1)S(1)}, u32[]{:S(2)}, u32[]{:S(2)}) collective-permute-start(bf16[2048,256]{1,0:T(8,128)(2,1)S(1)} %convolution_convert_fusion.8), channel_id=1, source_target_pairs={{0,8},{8,0},{16,24},{24,16},{1,9},{9,1},{17,25},{25,17},{2,10},{10... | collective-permute-start | bytes 3145736 | tf_op jit(solution)/shard_map/ppermute | solution.py:44
  531.6 49.8 %collective-permute-start.64 = (bf16[2048,128]{1,0:T(8,128)(2,1)}, bf16[2048,128]{1,0:T(8,128)(2,1)}, u32[]{:S(2)}, u32[]{:S(2)}) collective-permute-start(bf16[2048,128]{1,0:T(8,128)(2,1)} %get-tuple-element.198), channel_id=1, source_target_pairs={{0,16},{16,0},{8,24},{24,8},{1,17},{17,1},{9,25},{25,9},{2,18},{18... | collective-permute-start | bytes 1572872 | tf_op jit(solution)/shard_map/ppermute | solution.py:48
  533.7 49.2 %collective-permute-start.65 = (bf16[2048,128]{1,0:T(8,128)(2,1)}, bf16[2048,128]{1,0:T(8,128)(2,1)}, u32[]{:S(2)}, u32[]{:S(2)}) collective-permute-start(bf16[2048,128]{1,0:T(8,128)(2,1)} %get-tuple-element.197), channel_id=1, source_target_pairs={{0,8},{8,0},{16,24},{24,16},{1,9},{9,1},{17,25},{25,17},{2,10},{10... | collective-permute-start | bytes 1572872 | tf_op jit(solution)/shard_map/ppermute | solution.py:44
  543.3 184.6 %all-gather.16.cloned.1.call-start = ((), (), s32[]{:S(2)}) async-start(), calls=%async_computation.8 | async-start | bytes 3276800 | tf_op jit(solution)/shard_map/all_gather | solution.py:413
  546.4 45.9 %collective-permute-start.68 = (bf16[2048,128]{1,0:T(8,128)(2,1)}, bf16[2048,128]{1,0:T(8,128)(2,1)}, u32[]{:S(2)}, u32[]{:S(2)}) collective-permute-start(bf16[2048,128]{1,0:T(8,128)(2,1)} %get-tuple-element.202), channel_id=1, source_target_pairs={{0,16},{16,0},{8,24},{24,8},{1,17},{17,1},{9,25},{25,9},{2,18},{18... | collective-permute-start | bytes 1572872 | tf_op jit(solution)/shard_map/ppermute | solution.py:48
  549.5 43.3 %collective-permute-start.69 = (bf16[2048,128]{1,0:T(8,128)(2,1)}, bf16[2048,128]{1,0:T(8,128)(2,1)}, u32[]{:S(2)}, u32[]{:S(2)}) collective-permute-start(bf16[2048,128]{1,0:T(8,128)(2,1)} %get-tuple-element.201), channel_id=1, source_target_pairs={{0,8},{8,0},{16,24},{24,16},{1,9},{9,1},{17,25},{25,17},{2,10},{10... | collective-permute-start | bytes 1572872 | tf_op jit(solution)/shard_map/ppermute | solution.py:44
  577.8 36.3 %collective-permute-start.72 = (bf16[512,128]{1,0:T(8,128)(2,1)}, bf16[512,128]{1,0:T(8,128)(2,1)}, u32[]{:S(2)}, u32[]{:S(2)}) collective-permute-start(bf16[512,128]{1,0:T(8,128)(2,1)} %get-tuple-element.272), channel_id=1, source_target_pairs={{0,16},{16,0},{8,24},{24,8},{1,17},{17,1},{9,25},{25,9},{2,18},{18... | collective-permute-start | bytes 393224 | tf_op jit(solution)/shard_map/ppermute | solution.py:48
  603.3 58.3 %collective-permute-start.66 = (bf16[2,512,256]{2,1,0:T(8,128)(2,1)}, bf16[2,512,256]{2,1,0:T(8,128)(2,1)}, u32[]{:S(2)}, u32[]{:S(2)}) collective-permute-start(bf16[2,512,256]{2,1,0:T(8,128)(2,1)} %dynamic-slice_bitcast_fusion.3), channel_id=1, source_target_pairs={{0,1},{1,0},{2,3},{3,2},{4,5},{5,4},{6,7},{7,6},{8,9},{9,8},{10,11... | collective-permute-start | bytes 1572872 | tf_op jit(solution)/shard_map/ppermute | solution.py:72
  610.8 52.1 %collective-permute-start.70 = (bf16[2,512,256]{2,1,0:T(8,128)(2,1)}, bf16[2,512,256]{2,1,0:T(8,128)(2,1)}, u32[]{:S(2)}, u32[]{:S(2)}) collective-permute-start(bf16[2,512,256]{2,1,0:T(8,128)(2,1)} %dynamic-slice_bitcast_fusion.2), channel_id=1, source_target_pairs={{0,1},{1,0},{2,3},{3,2},{4,5},{5,4},{6,7},{7,6},{8,9},{9,8},{10,11... | collective-permute-start | bytes 1572872 | tf_op jit(solution)/shard_map/ppermute | solution.py:72
  652.4 44.9 %collective-permute-start.78 = (bf16[2,512,256]{2,1,0:T(8,128)(2,1)}, bf16[2,512,256]{2,1,0:T(8,128)(2,1)}, u32[]{:S(2)}, u32[]{:S(2)}) collective-permute-start(bf16[2,512,256]{2,1,0:T(8,128)(2,1)} %fusion.46), channel_id=1, source_target_pairs={{0,1},{1,0},{2,3},{3,2},{4,5},{5,4},{6,7},{7,6},{8,9},{9,8},{10,11... | collective-permute-start | bytes 1572872 | tf_op jit(solution)/shard_map/ppermute | solution.py:72
  (212 other events, 2549.4 us)
Sparse Core Ops, SparseCore 0:
  57.2 32.2 all-gather.7
  110.8 26.1 all-gather.9
  178.1 43.5 all-gather.11
  365.0 52.3 all-gather.13
  485.2 41.4 reduce-scatter.2
  543.4 24.6 reduce-scatter.4
  617.0 79.5 all-gather.15

commit v5 on v4

--- a/solution.py
+++ b/solution.py
@@ -49,7 +49,14 @@
 
 
 def after(values, *earlier):
-    return lax.optimization_barrier((values,) + earlier)[0]
+    for array in earlier:
+        one = lax.slice(array, (0,) * array.ndim, (1,) * array.ndim).reshape(())
+        values = values + jnp.minimum(jnp.abs(one.astype(F32)), 0.0).astype(values.dtype)
+    return values
+
+
+def beside(values, *others):
+    return lax.optimization_barrier((values,) + others)[0]
 
 
 def swap(values):
@@ -126,22 +133,22 @@
     return mm_tn(delta, values[:, : 4 * half]).astype(BF), from_x, from_y
 
 
-def gradient_second(begun, marker):
+def gradient_second(begun, marker, hold):
     if not square():
         return begun
     kept, from_x, from_y = begun
     half = from_x.shape[1] // 2
-    from_x, from_y = lax.optimization_barrier((from_x, from_y, marker))[:2]
+    from_x, from_y = hold(from_x, marker), hold(from_y, marker)
     own_a, own_b, x_b, y_a = jnp.split(kept, 4, axis=1)
     last_a = send_y(y_a + from_x[:, half:])
     last_b = send_x(x_b + from_y[:, :half])
     return (own_a, from_x[:, :half], last_a), (own_b, from_y[:, half:], last_b)
 
 
-def gradient_finish(terms, marker):
+def gradient_finish(terms, marker, hold):
     if not square():
         return terms
-    last_a, last_b = lax.optimization_barrier((terms[0][2], terms[1][2], marker))[:2]
+    last_a, last_b = hold(terms[0][2], marker), hold(terms[1][2], marker)
     add = lambda own, near, last: (own.astype(F32) + near.astype(F32) + last.astype(F32)).astype(BF)
     return jnp.concatenate([add(*terms[0][:2], last_a), add(*terms[1][:2], last_b)], axis=1)
 
@@ -324,19 +331,12 @@
         cut.append((qkv, halves(out_weight[l], 0), halves(up_weight[l], 1).T, halves(down_weight[l], 0)))
     heights = [piece.shape[0] for piece in cut[0]]
     joined = lambda l, members: jnp.concatenate([cut[l][k] for k in members], axis=0)
-    rows_of = lambda gathered, start, stop: gathered.reshape(n_tp, -1, gathered.shape[-1])[:, start:stop]
-    first_along = gather_pairs(joined(0, (0,)))
-    second_along = gather_pairs(after(joined(0, (1, 2)), first_along))
-    stages = [(0, (0,), first_along), (0, (1, 2), second_along)]
-    for l, members in [(0, (3,))] + [(l, some) for l in range(1, layers) for some in ((0, 1), (2, 3))]:
-        gathered = lax.all_gather(after(joined(l, members), first_along), "tp", axis=0, tiled=True)
-        first_along = gathered
-        if members == (2, 3):
-            stages.append((l, (2,), rows_of(gathered, 0, heights[2])))
-            stages.append((l, (3,), rows_of(gathered, heights[2], None)))
-        else:
-            stages.append((l, members, gathered))
-    stages = [(l, members, along.reshape(-1, along.shape[-1])) for l, members, along in stages]
+    stages, along = [], ()
+    for l in range(layers):
+        for members in ((0, 1), (2,), (3,)) if l else ((0,), (1, 2), (3,)):
+            gathered = gather_pairs(after(joined(l, members), *along))
+            along = (gathered,)
+            stages.append((l, members, gathered.reshape(-1, gathered.shape[-1])))
     first_along = stages[0][2]
 
     pieces = (qv_bias, up_bias, out_bias, down_bias, gain_one, gain_two)
@@ -393,9 +393,11 @@
         weights[l] += more
         arrivals.append(came)
 
+    arrivals = [came + (along,) for came, along in zip(arrivals, [stage[2] for stage in stages[1:]] + [()])]
+    arrivals = [tuple(jax.tree.leaves(came)) for came in arrivals] + [(), ()]
     saved = []
     for l in range(layers):
-        stream, items = forward_layer(stream, weights[l], vectors[l], arrivals[3 * l + 1 : 3 * l + 3])
+        stream, items = forward_layer(stream, weights[l], vectors[l], arrivals[3 * l + 1 : 3 * l + 4])
         saved.append(items)
 
     place = jnp.arange(capacity)
@@ -421,16 +423,16 @@
 
     further, along = {}, {}
 
-    def second(layer, some, marker):
+    def second(layer, some, marker, hold=beside):
         held = ()
         for name in some:
-            further[layer, name] = gradient_second(begun[layer, name], marker)
+            further[layer, name] = gradient_second(begun[layer, name], marker, hold)
             held += begun[layer, name][1:] if square() else ()
         return held
 
-    def finish(layer, some, marker):
+    def finish(layer, some, marker, hold=beside):
         for name in some:
-            found[layer, name] = gradient_finish(further[layer, name], marker)
+            found[layer, name] = gradient_finish(further[layer, name], marker, hold)
 
     def along_tp(layer, some):
         return lax.psum_scatter(reduced(layer, some), "tp", scatter_dimension=0, tiled=False)
@@ -461,17 +463,44 @@
                 held += (output, along[l + 1][0], found[l + 1, "out"], found[l + 1, "qkv"])
             elif point == "normed":
                 finish(l, ("down",), value)
-            return after(value, *held)
+            return beside(value, *held)
 
         gradient, sums[l] = backward_layer(gradient, saved[l], weights[l], vectors[l], emit, gate)
     local_grad = give_back(gradient)
-    second(0, names[3:], local_grad)
-    finish(0, names[1:], local_grad)
+    def from_core(array, count):
+        array = array.reshape(layers, count, n_tp, 1, -1)
+        mask = (jnp.arange(2) == core)[:, None]
+        return jnp.where(mask, array, 0.0).reshape(-1)
+
+    first = (core == 0).astype(F32)
+    member = lambda k: jnp.stack([sums[l][k] for l in range(layers)])
+    by_feature = jnp.stack([member(k) for k in (1, 3, 4, 5)]).reshape(4 * layers, features) * first
+    if order is not None:
+        by_feature = lax.dot_general(
+            by_feature, order.astype(F32), (((1,), (1,)), ((), ())), precision=lax.Precision.HIGHEST
+        )
+    joined = [
+        from_core(jnp.swapaxes(member(0).reshape(layers, n_tp, 3, -1)[:, :, ::2], 1, 2), 2),
+        from_core(member(2)[:, None], 1),
+        by_feature.reshape(-1),
+    ]
+    summed = after(jnp.concatenate(joined), local_grad).reshape(-1, 128)
+    if square():
+        for bit, _ in tp_bits():
+            summed = summed + tp_partner(summed, bit)
+        over_tp = summed
+        summed = summed + swap(summed)
+        summed = summed + send_x(summed)
+        summed = summed + send_y(summed)
+    else:
+        over_tp = summed = lax.psum(summed, ("fsdp", "ctx", "tp"))
+    second(0, names[3:], local_grad, after)
+    finish(0, names[1:], over_tp, after)
     pieces = [scatter_pairs(reduced(0, some)) for some in (names[:1], names[1:2], names[2:])]
     mine = [jnp.concatenate(pieces, axis=0)] + [
         after(jnp.concatenate(along[l], axis=0), local_grad) for l in range(1, layers)
     ]
-    input_grad = to_all(after(local_grad, *along[1]))
+    input_grad = to_all(local_grad)
 
     grads = {name: [] for name in names}
     heights = [found[0, name].shape[0] // n_tp for name in names]
@@ -493,32 +522,6 @@
         ]
     ).astype(F32)
 
-    def from_core(array, count):
-        array = array.reshape(layers, count, n_tp, 1, -1)
-        mask = (jnp.arange(2) == core)[:, None]
-        return jnp.where(mask, array, 0.0).reshape(-1)
-
-    first = (core == 0).astype(F32)
-    member = lambda k: jnp.stack([sums[l][k] for l in range(layers)])
-    by_feature = jnp.stack([member(k) for k in (1, 3, 4, 5)]).reshape(4 * layers, features) * first
-    if order is not None:
-        by_feature = lax.dot_general(
-            by_feature, order.astype(F32), (((1,), (1,)), ((), ())), precision=lax.Precision.HIGHEST
-        )
-    joined = [
-        from_core(jnp.swapaxes(member(0).reshape(layers, n_tp, 3, -1)[:, :, ::2], 1, 2), 2),
-        from_core(member(2)[:, None], 1),
-        by_feature.reshape(-1),
-    ]
-    summed = jnp.concatenate(joined).reshape(-1, 128)
-    if square() and n_tp == 4:
-        summed = summed + swap(summed)
-        summed = summed + send_x(summed)
-        summed = summed + send_y(summed)
-        summed = summed + lax.ppermute(summed, "tp", [(0, 1), (1, 0), (2, 3), (3, 2)])
-        summed = summed + lax.ppermute(summed, "tp", [(0, 2), (2, 0), (1, 3), (3, 1)])
-    else:
-        summed = lax.psum(summed, ("fsdp", "ctx", "tp"))
     summed = summed.reshape(-1)
     pick = lambda a, i, axis: lax.dynamic_index_in_dim(a, i, axis, keepdims=True)
     ends = (joined[0].size, joined[0].size + joined[1].size)

time: 745 us -> 739 us (level)
  waiting for transfers between devices: 253 us -> 206 us
  starting transfers between devices: 75.1 us -> 101 us
  between operations: 18.7 us -> 35.7 us
  other arithmetic: 96.5 us -> 105 us
    ppermute x30, waiting for transfers between devices: 85.7 us -> 23 us  [send_x(): return lax.ppermute(values, 'fsdp', X_PAIRS)]
    ppermute x2 -> x0, waiting for transfers between devices: 25.1 us -> none  [the longest x1 19.6 us: shards(): lax.ppermute(summed, 'tp', [(0, 1), (1, 0), (2, 3), (3, 2)])]
    ppermute x31, waiting for transfers between devices: 71.9 us -> 95.8 us  [send_y(): return lax.ppermute(values, 'fsdp', Y_PAIRS)]
    ppermute x12 -> x22, starting transfers between devices: 9.61 us -> 33.5 us  [tp_partner(): lax.ppermute(values, 'tp', [(j, j ^ bit) for j in range(lax.axis_size('tp...]
    ppermute x12 -> x22, waiting for transfers between devices: 62.1 us -> 85.5 us  [tp_partner(): lax.ppermute(values, 'tp', [(j, j ^ bit) for j in range(lax.axis_size('tp...]
    slice x1 -> x25, local copies, waits for them, and re-layouts: 2.26 us -> 15.9 us  [after(): one = lax.slice(array, (0,) * array.ndim, (1,) * array.ndim).reshape(())]
    unnamed x365 -> x362, local copies, waits for them, and re-layouts: 45.4 us -> 34.4 us
    add x10 -> x27, other arithmetic: 14.8 us -> 21.7 us  [the longest x8 15.8 us: gradient_second(): last_a = send_y(y_a + from_x[:, half:])]
  transfers between devices with their start and end apart: 94 -> 99, of which waited for: 36 -> 33; matrix products, arithmetic and copies ran while one was open for 38% -> 39% of each run, Pallas kernels for 6% -> 6%
where the time goes in v5:
time: 739 us; the launch traced here: 732 us
  waiting for transfers between devices  206 us (28%)
  matrix products  126 us (17%)
  local copies, waits for them, and re-layouts  113 us (15%)
  other arithmetic  105 us (14%)
  starting transfers between devices  101 us (14%)
  Pallas kernels  45.8 us (6%)
  between operations  35.7 us (5%)
    ppermute x31, waiting for transfers between devices, send_y(): return lax.ppermute(values, 'fsdp', Y_PAIRS)  95.8 us
    ppermute x22, waiting for transfers between devices, tp_partner(): lax.ppermute(values, 'tp', [(j, j ^ bit) for j in range(lax.axis_size('tp...  85.5 us
    dot_general x24, matrix products, mm_tn(): lax.dot_general(left, right, (((0,), (0,)), ((), ())), preferred_element_...  51 us
    dot_general x14, matrix products, mm(): return jnp.dot(left, right, preferred_element_type=F32)  42.3 us
    unnamed x362, local copies, waits for them, and re-layouts  34.4 us
    ppermute x30, starting transfers between devices, send_x(): return lax.ppermute(values, 'fsdp', X_PAIRS)  34 us
    ppermute x22, starting transfers between devices, tp_partner(): lax.ppermute(values, 'tp', [(j, j ^ bit) for j in range(lax.axis_size('tp...  33.5 us
    ppermute x31, starting transfers between devices, send_y(): return lax.ppermute(values, 'fsdp', Y_PAIRS)  31.6 us
  transfers between devices with their start and end apart: 99, of which 33 were waited for; matrix products, arithmetic and copies ran while one was open for 39% of the time, Pallas kernels for 6%

profile of v5, /device:TPU:0, one launch (start us, length us, event | category | flops | bytes accessed | tf_op | source)
XLA Modules:
  0.0 731.8 jit_solution(16302169630463561415)
XLA Ops:
  41.4 7.8 %collective-permute-done.5 = bf16[2,384,256]{2,1,0:T(8,128)(2,1)S(1)} collective-permute-done((bf16[2,384,256]{2,1,0:T(8,128)(2,1)S(1)}, bf16[2,384,256]{2,1,0:T(8,128)(2,1)S(1)}, u32[]{:S(2)}, u32[]{:S(2)}) %collective-permute-start.5) | collective-permute-done | bytes 393248 | tf_op jit(solution)/shard_map/ppermute | solution.py:79
  104.8 9.1 %collective-permute-done.16 = bf16[512,256]{1,0:T(8,128)(2,1)S(1)} collective-permute-done((bf16[512,256]{1,0:T(8,128)(2,1)S(1)}, bf16[512,256]{1,0:T(8,128)(2,1)S(1)}, u32[]{:S(2)}, u32[]{:S(2)}) %collective-permute-start.16) | collective-permute-done | bytes 262176 | tf_op jit(solution)/shard_map/ppermute | solution.py:79
  114.4 10.7 %collective-permute-done.17 = bf16[2,512,256]{2,1,0:T(8,128)(2,1)S(1)} collective-permute-done((bf16[2,512,256]{2,1,0:T(8,128)(2,1)S(1)}, bf16[2,512,256]{2,1,0:T(8,128)(2,1)S(1)}, u32[]{:S(2)}, u32[]{:S(2)}) %collective-permute-start.17) | collective-permute-done | bytes 524320 | tf_op jit(solution)/shard_map/ppermute | solution.py:79
  130.1 7.6 %collective-permute-done.20 = bf16[512,256]{1,0:T(8,128)(2,1)S(1)} collective-permute-done((bf16[512,256]{1,0:T(8,128)(2,1)S(1)}, bf16[512,256]{1,0:T(8,128)(2,1)S(1)}, u32[]{:S(2)}, u32[]{:S(2)}) %collective-permute-start.20) | collective-permute-done | bytes 262176 | tf_op jit(solution)/shard_map/ppermute | solution.py:79
  154.6 7.7 %shard_map.229 = (bf16[592,512]{1,0:T(8,128)(2,1)S(1)}, f32[4,592,2]{2,1,0:T(8,128)S(1)}) custom-call(bf16[592,1536]{1,0:T(8,128)(2,1)S(1)} %get-tuple-element.291.project_ref), custom_call_target="tpu_custom_call" | custom-call | flops 2871001088 | bytes 2424832 | tf_op jit(solution)/shard_map/pallas_call | solution.py:218
  165.5 14.4 %collective-permute-done.22 = bf16[2560,128]{1,0:T(8,128)(2,1)S(1)} collective-permute-done((bf16[2560,128]{1,0:T(8,128)(2,1)S(1)}, bf16[2560,128]{1,0:T(8,128)(2,1)S(1)}, u32[]{:S(2)}, u32[]{:S(2)}) %collective-permute-start.22) | collective-permute-done | bytes 655392 | tf_op jit(solution)/shard_map/ppermute | solution.py:48
  190.4 27.4 %collective-permute-done.25 = bf16[2048,128]{1,0:T(8,128)(2,1)S(1)} collective-permute-done((bf16[2048,128]{1,0:T(8,128)(2,1)S(1)}, bf16[2048,128]{1,0:T(8,128)(2,1)S(1)}, u32[]{:S(2)}, u32[]{:S(2)}) %collective-permute-start.25) | collective-permute-done | bytes 524320 | tf_op jit(solution)/shard_map/ppermute | solution.py:48
  233.1 4.9 multiply_convert_fusion.1
  240.9 14.2 %collective-permute-done.30 = bf16[2048,128]{1,0:T(8,128)(2,1)S(1)} collective-permute-done((bf16[2048,128]{1,0:T(8,128)(2,1)S(1)}, bf16[2048,128]{1,0:T(8,128)(2,1)S(1)}, u32[]{:S(2)}, u32[]{:S(2)}) %collective-permute-start.30) | collective-permute-done | bytes 524320 | tf_op jit(solution)/shard_map/ppermute | solution.py:48
  256.2 8.0 %collective-permute-done.37 = bf16[2,512,256]{2,1,0:T(8,128)(2,1)S(1)} collective-permute-done((bf16[2,512,256]{2,1,0:T(8,128)(2,1)S(1)}, bf16[2,512,256]{2,1,0:T(8,128)(2,1)S(1)}, u32[]{:S(2)}, u32[]{:S(2)}) %collective-permute-start.37) | collective-permute-done | bytes 524320 | tf_op jit(solution)/shard_map/ppermute | solution.py:79
  278.5 8.2 %shard_map.230 = (bf16[592,512]{1,0:T(8,128)(2,1)S(1)}, f32[4,592,2]{2,1,0:T(8,128)S(1)}) custom-call(bf16[592,1536]{1,0:T(8,128)(2,1)S(1)} %get-tuple-element.297.project_ref), custom_call_target="tpu_custom_call" | custom-call | flops 2871001088 | bytes 2424832 | tf_op jit(solution)/shard_map/pallas_call | solution.py:218
  286.6 16.0 %collective-permute-done.41 = bf16[2048,128]{1,0:T(8,128)(2,1)S(1)} collective-permute-done((bf16[2048,128]{1,0:T(8,128)(2,1)S(1)}, bf16[2048,128]{1,0:T(8,128)(2,1)S(1)}, u32[]{:S(2)}, u32[]{:S(2)}) %collective-permute-start.41) | collective-permute-done | bytes 524320 | tf_op jit(solution)/shard_map/ppermute | solution.py:48
  316.5 4.8 multiply_convert_fusion
  328.1 4.2 fusion.19
  332.4 5.5 convolution_convert_fusion.28
  340.4 7.4 %add_convert_fusion.1 = bf16[592,2048]{1,0:T(8,128)(2,1)S(1)} fusion(f32[592,2048]{1,0:T(8,128)} %get-tuple-element.300, f32[2048]{0:T(1024)S(1)} %bitcast.566, bf16[592,1024]{1,0:T(8,128)(2,1)S(1)} %get-tuple-element.140, bf16[2048,1024]{1,0:T(8,128)(2,1)} %copy-done.71), kind=kOutput, calls=%fused_computation.3 | convolution fusion | flops 2500001792 | bytes 12689408 | tf_op jit(solution)/shard_map/dot_general | solution.py:161
  366.5 5.1 convolution_convert_fusion.6
  383.7 15.0 %shard_map.231 = bf16[592,1536]{1,0:T(8,128)(2,1)S(1)} custom-call(bf16[592,1536]{1,0:T(8,128)(2,1)S(1)} %copy-done.5, bf16[592,512]{1,0:T(8,128)(2,1)S(1)} %add_add_fusion.19.mixed_ref, f32[4,592,2]{2,1,0:T(8,128)S(1)} %get-tuple-element.49.total_ref, bf16[592,512]{1,0:T(8,128)(2,1)S(1)} %convolution_convert_fusion.30.delta_ref), custom_call_target="tpu_custom_call" | custom-call | flops 7177502720 | bytes 4546560 | tf_op jit(solution)/shard_map/pallas_call | solution.py:236
  398.7 7.0 collective-permute-done.48
  439.8 5.2 add_convert_fusion
  454.4 4.0 collective-permute-done.64
  503.8 14.9 %shard_map.232 = bf16[592,1536]{1,0:T(8,128)(2,1)S(1)} custom-call(bf16[592,1536]{1,0:T(8,128)(2,1)S(1)} %copy-done.4, bf16[592,512]{1,0:T(8,128)(2,1)S(1)} %copy-done.1, f32[4,592,2]{2,1,0:T(8,128)S(1)} %copy-done.3, bf16[592,512]{1,0:T(8,128)(2,1)S(1)} %convolution_convert_fusion.29.delta_ref), custom_call_target="tpu_custom_call" | custom-call | flops 7177502720 | bytes 4546560 | tf_op jit(solution)/shard_map/pallas_call | solution.py:236
  555.1 5.1 convolution_convert_fusion.25
  580.4 5.3 convolution_convert_fusion.27
  587.0 5.7 collective-permute-done.86
  597.6 13.8 %collective-permute-done.84 = bf16[1536,256]{0,1:T(8,128)(2,1)S(1)} collective-permute-done((bf16[1536,256]{0,1:T(8,128)(2,1)}, bf16[1536,256]{0,1:T(8,128)(2,1)S(1)}, u32[]{:S(2)}, u32[]{:S(2)}) %collective-permute-start.84) | collective-permute-done | bytes 786464 | tf_op jit(solution)/shard_map/ppermute | solution.py:44
  612.3 4.0 collective-permute-start.77
  618.7 6.1 collective-permute-done.77
  627.5 10.3 %collective-permute-done.78 = f32[160,128]{1,0:T(8,128)} collective-permute-done((f32[160,128]{1,0:T(8,128)}, f32[160,128]{1,0:T(8,128)}, u32[]{:S(2)}, u32[]{:S(2)}) %collective-permute-start.78) | collective-permute-done | bytes 81952 | tf_op jit(solution)/shard_map/ppermute | solution.py:79
  670.8 4.7 collective-permute-start.75
  682.6 6.3 collective-permute-done.75
  695.9 11.2 %collective-permute-done.89 = bf16[512,256]{0,1:T(8,128)(2,1)S(1)} collective-permute-done((bf16[512,256]{0,1:T(8,128)(2,1)S(1)}, bf16[512,256]{0,1:T(8,128)(2,1)S(1)}, u32[]{:S(2)}, u32[]{:S(2)}) %collective-permute-start.89) | collective-permute-done | bytes 262176 | tf_op jit(solution)/shard_map/ppermute | solution.py:79
  (918 shorter events, 414.4 us)
Async XLA Ops:
  7.2 544.9 %all-gather.5.cloned.1.call-start = ((), (), s32[]{:S(2)}) async-start(), calls=%async_computation.4 | async-start | bytes 3276800 | tf_op jit(solution)/shard_map/all_gather | solution.py:415
  23.2 59.4 %collective-permute-start = (bf16[320,2048]{1,0:T(8,128)(2,1)}, bf16[320,2048]{1,0:T(8,128)(2,1)}, u32[]{:S(2)}, u32[]{:S(2)}) collective-permute-start(bf16[320,2048]{1,0:T(8,128)(2,1)} %pad_maximum_fusion.1), channel_id=1, source_target_pairs={{0,4},{4,0},{1,5},{5,1},{2,6},{6,2},{3,7},{7,3},{8,12},{12,8},{9,1... | collective-permute-start | bytes 3932168 | tf_op jit(solution)/shard_map/ppermute | solution.py:63
  49.4 39.5 %collective-permute-start.6 = (bf16[1536,256]{1,0:T(8,128)(2,1)S(1)}, bf16[1536,256]{1,0:T(8,128)(2,1)}, u32[]{:S(2)}, u32[]{:S(2)}) collective-permute-start(bf16[1536,256]{1,0:T(8,128)(2,1)S(1)} %bitcast.436), channel_id=1, source_target_pairs={{0,8},{8,0},{16,24},{24,16},{1,9},{9,1},{17,25},{25,17},{2,10},{10... | collective-permute-start | bytes 2359304 | tf_op jit(solution)/shard_map/ppermute | solution.py:44
  50.0 42.0 %collective-permute-start.7 = (bf16[1536,256]{1,0:T(8,128)(2,1)S(1)}, bf16[1536,256]{1,0:T(8,128)(2,1)}, u32[]{:S(2)}, u32[]{:S(2)}) collective-permute-start(bf16[1536,256]{1,0:T(8,128)(2,1)S(1)} %bitcast.437), channel_id=1, source_target_pairs={{0,16},{16,0},{8,24},{24,8},{1,17},{17,1},{9,25},{25,9},{2,18},{18... | collective-permute-start | bytes 2359304 | tf_op jit(solution)/shard_map/ppermute | solution.py:48
  100.5 37.5 %collective-permute-start.14 = (bf16[2560,256]{1,0:T(8,128)(2,1)S(1)}, bf16[2560,256]{1,0:T(8,128)(2,1)S(1)}, u32[]{:S(2)}, u32[]{:S(2)}) collective-permute-start(bf16[2560,256]{1,0:T(8,128)(2,1)S(1)} %bitcast.478), channel_id=1, source_target_pairs={{0,8},{8,0},{16,24},{24,16},{1,9},{9,1},{17,25},{25,17},{2,10},{10... | collective-permute-start | bytes 3932168 | tf_op jit(solution)/shard_map/ppermute | solution.py:44
  101.1 38.0 %collective-permute-start.15 = (bf16[2560,256]{1,0:T(8,128)(2,1)S(1)}, bf16[2560,256]{1,0:T(8,128)(2,1)S(1)}, u32[]{:S(2)}, u32[]{:S(2)}) collective-permute-start(bf16[2560,256]{1,0:T(8,128)(2,1)S(1)} %bitcast.479), channel_id=1, source_target_pairs={{0,16},{16,0},{8,24},{24,8},{1,17},{17,1},{9,25},{25,9},{2,18},{18... | collective-permute-start | bytes 3932168 | tf_op jit(solution)/shard_map/ppermute | solution.py:48
  140.8 40.1 %collective-permute-start.18 = (bf16[2048,256]{1,0:T(8,128)(2,1)S(1)}, bf16[2048,256]{1,0:T(8,128)(2,1)S(1)}, u32[]{:S(2)}, u32[]{:S(2)}) collective-permute-start(bf16[2048,256]{1,0:T(8,128)(2,1)S(1)} %get-tuple-element.296), channel_id=1, source_target_pairs={{0,8},{8,0},{16,24},{24,16},{1,9},{9,1},{17,25},{25,17},{2,10},{10... | collective-permute-start | bytes 3145736 | tf_op jit(solution)/shard_map/ppermute | solution.py:44
  142.3 39.9 %collective-permute-start.19 = (bf16[2048,256]{1,0:T(8,128)(2,1)S(1)}, bf16[2048,256]{1,0:T(8,128)(2,1)S(1)}, u32[]{:S(2)}, u32[]{:S(2)}) collective-permute-start(bf16[2048,256]{1,0:T(8,128)(2,1)S(1)} %get-tuple-element.296), channel_id=1, source_target_pairs={{0,16},{16,0},{8,24},{24,8},{1,17},{17,1},{9,25},{25,9},{2,18},{18... | collective-permute-start | bytes 3145736 | tf_op jit(solution)/shard_map/ppermute | solution.py:48
  142.7 37.3 %collective-permute-start.22 = (bf16[2560,128]{1,0:T(8,128)(2,1)S(1)}, bf16[2560,128]{1,0:T(8,128)(2,1)S(1)}, u32[]{:S(2)}, u32[]{:S(2)}) collective-permute-start(bf16[2560,128]{1,0:T(8,128)(2,1)S(1)} %get-tuple-element.185), channel_id=1, source_target_pairs={{0,16},{16,0},{8,24},{24,8},{1,17},{17,1},{9,25},{25,9},{2,18},{18... | collective-permute-start | bytes 1966088 | tf_op jit(solution)/shard_map/ppermute | solution.py:48
  184.2 35.5 %collective-permute-start.29 = (bf16[2048,256]{1,0:T(8,128)(2,1)S(1)}, bf16[2048,256]{1,0:T(8,128)(2,1)S(1)}, u32[]{:S(2)}, u32[]{:S(2)}) collective-permute-start(bf16[2048,256]{1,0:T(8,128)(2,1)S(1)} %add_add_fusion.16), channel_id=1, source_target_pairs={{0,16},{16,0},{8,24},{24,8},{1,17},{17,1},{9,25},{25,9},{2,18},{18... | collective-permute-start | bytes 3145736 | tf_op jit(solution)/shard_map/ppermute | solution.py:48
  190.0 37.8 %collective-permute-start.24 = (bf16[592,1024]{1,0:T(8,128)(2,1)S(1)}, bf16[592,1024]{1,0:T(8,128)(2,1)S(1)}, u32[]{:S(2)}, u32[]{:S(2)}) collective-permute-start(bf16[592,1024]{1,0:T(8,128)(2,1)S(1)} %convolution_convert_fusion.24), channel_id=1, source_target_pairs={{0,4},{4,0},{1,5},{5,1},{2,6},{6,2},{3,7},{7,3},{8,12},{12,8},{9,1... | collective-permute-start | bytes 3637256 | tf_op jit(solution)/shard_map/ppermute | solution.py:63
  221.2 44.6 %collective-permute-start.34 = (bf16[2048,256]{1,0:T(8,128)(2,1)S(1)}, bf16[2048,256]{1,0:T(8,128)(2,1)S(1)}, u32[]{:S(2)}, u32[]{:S(2)}) collective-permute-start(bf16[2048,256]{1,0:T(8,128)(2,1)S(1)} %bitcast.423), channel_id=1, source_target_pairs={{0,8},{8,0},{16,24},{24,16},{1,9},{9,1},{17,25},{25,17},{2,10},{10... | collective-permute-start | bytes 3145736 | tf_op jit(solution)/shard_map/ppermute | solution.py:44
  222.7 44.2 %collective-permute-start.35 = (bf16[2048,256]{1,0:T(8,128)(2,1)S(1)}, bf16[2048,256]{1,0:T(8,128)(2,1)S(1)}, u32[]{:S(2)}, u32[]{:S(2)}) collective-permute-start(bf16[2048,256]{1,0:T(8,128)(2,1)S(1)} %bitcast.424), channel_id=1, source_target_pairs={{0,16},{16,0},{8,24},{24,8},{1,17},{17,1},{9,25},{25,9},{2,18},{18... | collective-permute-start | bytes 3145736 | tf_op jit(solution)/shard_map/ppermute | solution.py:48
  357.3 41.4 %collective-permute-start.50 = (bf16[2048,256]{1,0:T(8,128)(2,1)}, bf16[2048,256]{1,0:T(8,128)(2,1)}, u32[]{:S(2)}, u32[]{:S(2)}) collective-permute-start(bf16[2048,256]{1,0:T(8,128)(2,1)} %convolution_convert_fusion.11), channel_id=1, source_target_pairs={{0,16},{16,0},{8,24},{24,8},{1,17},{17,1},{9,25},{25,9},{2,18},{18... | collective-permute-start | bytes 3145736 | tf_op jit(solution)/shard_map/ppermute | solution.py:48
  358.6 40.1 %collective-permute-start.49 = (bf16[2048,256]{1,0:T(8,128)(2,1)}, bf16[2048,256]{1,0:T(8,128)(2,1)}, u32[]{:S(2)}, u32[]{:S(2)}) collective-permute-start(bf16[2048,256]{1,0:T(8,128)(2,1)} %convolution_convert_fusion.12), channel_id=1, source_target_pairs={{0,8},{8,0},{16,24},{24,16},{1,9},{9,1},{17,25},{25,17},{2,10},{10... | collective-permute-start | bytes 3145736 | tf_op jit(solution)/shard_map/ppermute | solution.py:44
  360.0 45.7 %collective-permute-start.48 = (bf16[2048,256]{1,0:T(8,128)(2,1)}, bf16[2048,256]{1,0:T(8,128)(2,1)}, u32[]{:S(2)}, u32[]{:S(2)}) collective-permute-start(bf16[2048,256]{1,0:T(8,128)(2,1)} %convolution_convert_fusion.13), channel_id=1, source_target_pairs={{0,16},{16,0},{8,24},{24,8},{1,17},{17,1},{9,25},{25,9},{2,18},{18... | collective-permute-start | bytes 3145736 | tf_op jit(solution)/shard_map/ppermute | solution.py:48
  362.9 43.8 %collective-permute-start.47 = (bf16[2048,256]{1,0:T(8,128)(2,1)}, bf16[2048,256]{1,0:T(8,128)(2,1)}, u32[]{:S(2)}, u32[]{:S(2)}) collective-permute-start(bf16[2048,256]{1,0:T(8,128)(2,1)} %convolution_convert_fusion.14), channel_id=1, source_target_pairs={{0,8},{8,0},{16,24},{24,16},{1,9},{9,1},{17,25},{25,17},{2,10},{10... | collective-permute-start | bytes 3145736 | tf_op jit(solution)/shard_map/ppermute | solution.py:44
  363.5 191.6 %reduce-scatter.3.cloned.1.call-start = ((), (), s32[]{:S(2)}) async-start(), calls=%async_computation.2 | async-start | bytes 2621440 | tf_op jit(solution)/shard_map/reduce_scatter | solution.py:438
  449.8 68.9 %collective-permute-start.58 = (bf16[2048,256]{1,0:T(8,128)(2,1)}, bf16[2048,256]{1,0:T(8,128)(2,1)}, u32[]{:S(2)}, u32[]{:S(2)}) collective-permute-start(bf16[2048,256]{1,0:T(8,128)(2,1)} %convolution_convert_fusion.9), channel_id=1, source_target_pairs={{0,16},{16,0},{8,24},{24,8},{1,17},{17,1},{9,25},{25,9},{2,18},{18... | collective-permute-start | bytes 3145736 | tf_op jit(solution)/shard_map/ppermute | solution.py:48
  461.9 58.4 %collective-permute-start.57 = (bf16[2048,256]{1,0:T(8,128)(2,1)}, bf16[2048,256]{1,0:T(8,128)(2,1)}, u32[]{:S(2)}, u32[]{:S(2)}) collective-permute-start(bf16[2048,256]{1,0:T(8,128)(2,1)} %convolution_convert_fusion.10), channel_id=1, source_target_pairs={{0,8},{8,0},{16,24},{24,16},{1,9},{9,1},{17,25},{25,17},{2,10},{10... | collective-permute-start | bytes 3145736 | tf_op jit(solution)/shard_map/ppermute | solution.py:44
  469.7 51.8 %collective-permute-start.70 = (bf16[1536,128]{1,0:T(8,128)(2,1)}, bf16[1536,128]{1,0:T(8,128)(2,1)}, u32[]{:S(2)}, u32[]{:S(2)}) collective-permute-start(bf16[1536,128]{1,0:T(8,128)(2,1)} %get-tuple-element.182), channel_id=1, source_target_pairs={{0,8},{8,0},{16,24},{24,16},{1,9},{9,1},{17,25},{25,17},{2,10},{10... | collective-permute-start | bytes 1179656 | tf_op jit(solution)/shard_map/ppermute | solution.py:44
  480.5 52.9 %collective-permute-start.60 = (bf16[2048,256]{1,0:T(8,128)(2,1)}, bf16[2048,256]{1,0:T(8,128)(2,1)}, u32[]{:S(2)}, u32[]{:S(2)}) collective-permute-start(bf16[2048,256]{1,0:T(8,128)(2,1)} %convolution_convert_fusion.7), channel_id=1, source_target_pairs={{0,16},{16,0},{8,24},{24,8},{1,17},{17,1},{9,25},{25,9},{2,18},{18... | collective-permute-start | bytes 3145736 | tf_op jit(solution)/shard_map/ppermute | solution.py:48
  484.7 109.0 %reduce-scatter.5.cloned.1.call-start = ((), (), s32[]{:S(2)}) async-start(), calls=%async_computation.3 | async-start | bytes 1310720 | tf_op jit(solution)/shard_map/reduce_scatter | solution.py:438
  493.0 42.1 %collective-permute-start.59 = (bf16[2048,256]{1,0:T(8,128)(2,1)S(1)}, bf16[2048,256]{1,0:T(8,128)(2,1)S(1)}, u32[]{:S(2)}, u32[]{:S(2)}) collective-permute-start(bf16[2048,256]{1,0:T(8,128)(2,1)S(1)} %convolution_convert_fusion.8), channel_id=1, source_target_pairs={{0,8},{8,0},{16,24},{24,16},{1,9},{9,1},{17,25},{25,17},{2,10},{10... | collective-permute-start | bytes 3145736 | tf_op jit(solution)/shard_map/ppermute | solution.py:44
  527.8 43.9 %collective-permute-start.73 = (bf16[2048,128]{1,0:T(8,128)(2,1)}, bf16[2048,128]{1,0:T(8,128)(2,1)}, u32[]{:S(2)}, u32[]{:S(2)}) collective-permute-start(bf16[2048,128]{1,0:T(8,128)(2,1)} %get-tuple-element.158), channel_id=1, source_target_pairs={{0,8},{8,0},{16,24},{24,16},{1,9},{9,1},{17,25},{25,17},{2,10},{10... | collective-permute-start | bytes 1572872 | tf_op jit(solution)/shard_map/ppermute | solution.py:44
  533.4 39.7 %collective-permute-start.72 = (bf16[2048,128]{1,0:T(8,128)(2,1)}, bf16[2048,128]{1,0:T(8,128)(2,1)}, u32[]{:S(2)}, u32[]{:S(2)}) collective-permute-start(bf16[2048,128]{1,0:T(8,128)(2,1)} %get-tuple-element.157), channel_id=1, source_target_pairs={{0,16},{16,0},{8,24},{24,8},{1,17},{17,1},{9,25},{25,9},{2,18},{18... | collective-permute-start | bytes 1572872 | tf_op jit(solution)/shard_map/ppermute | solution.py:48
  537.7 103.6 %collective-permute-start.76 = (bf16[2048,128]{1,0:T(8,128)(2,1)}, bf16[2048,128]{1,0:T(8,128)(2,1)}, u32[]{:S(2)}, u32[]{:S(2)}) collective-permute-start(bf16[2048,128]{1,0:T(8,128)(2,1)} %get-tuple-element.161), channel_id=1, source_target_pairs={{0,16},{16,0},{8,24},{24,8},{1,17},{17,1},{9,25},{25,9},{2,18},{18... | collective-permute-start | bytes 1572872 | tf_op jit(solution)/shard_map/ppermute | solution.py:48
  546.8 175.2 %all-gather.7.cloned.1.call-start = ((), (), s32[]{:S(2)}) async-start(), calls=%async_computation.5 | async-start | bytes 3276800 | tf_op jit(solution)/shard_map/all_gather | solution.py:415
  548.6 92.8 %collective-permute-start.79 = (bf16[2048,128]{1,0:T(8,128)(2,1)}, bf16[2048,128]{1,0:T(8,128)(2,1)}, u32[]{:S(2)}, u32[]{:S(2)}) collective-permute-start(bf16[2048,128]{1,0:T(8,128)(2,1)} %get-tuple-element.162), channel_id=1, source_target_pairs={{0,8},{8,0},{16,24},{24,16},{1,9},{9,1},{17,25},{25,17},{2,10},{10... | collective-permute-start | bytes 1572872 | tf_op jit(solution)/shard_map/ppermute | solution.py:44
  568.8 75.6 %collective-permute-start.82 = (bf16[512,128]{1,0:T(8,128)(2,1)}, bf16[512,128]{1,0:T(8,128)(2,1)}, u32[]{:S(2)}, u32[]{:S(2)}) collective-permute-start(bf16[512,128]{1,0:T(8,128)(2,1)} %get-tuple-element.245), channel_id=1, source_target_pairs={{0,16},{16,0},{8,24},{24,8},{1,17},{17,1},{9,25},{25,9},{2,18},{18... | collective-permute-start | bytes 393224 | tf_op jit(solution)/shard_map/ppermute | solution.py:48
  571.8 72.7 %collective-permute-start.83 = (bf16[512,128]{1,0:T(8,128)(2,1)}, bf16[512,128]{1,0:T(8,128)(2,1)}, u32[]{:S(2)}, u32[]{:S(2)}) collective-permute-start(bf16[512,128]{1,0:T(8,128)(2,1)} %get-tuple-element.246), channel_id=1, source_target_pairs={{0,8},{8,0},{16,24},{24,16},{1,9},{9,1},{17,25},{25,17},{2,10},{10... | collective-permute-start | bytes 393224 | tf_op jit(solution)/shard_map/ppermute | solution.py:44
  644.4 36.6 %collective-permute-start.91 = (bf16[1536,256]{0,1:T(8,128)(2,1)S(1)}, bf16[1536,256]{0,1:T(8,128)(2,1)}, u32[]{:S(2)}, u32[]{:S(2)}) collective-permute-start(bf16[1536,256]{0,1:T(8,128)(2,1)S(1)} %maximum_add_fusion), channel_id=1, source_target_pairs={{0,4},{4,0},{1,5},{5,1},{2,6},{6,2},{3,7},{7,3},{8,12},{12,8},{9,1... | collective-permute-start | bytes 2359304 | tf_op jit(solution)/shard_map/ppermute | solution.py:63
  (219 other events, 2466.0 us)
Sparse Core Ops, SparseCore 0:
  363.6 57.0 all-gather.4
  484.8 46.1 reduce-scatter.2
  546.9 29.5 reduce-scatter.4
  587.1 63.3 all-gather.6

commit v6 on v5

--- a/solution.py
+++ b/solution.py
@@ -495,7 +495,8 @@
     else:
         over_tp = summed = lax.psum(summed, ("fsdp", "ctx", "tp"))
     second(0, names[3:], local_grad, after)
-    finish(0, names[1:], over_tp, after)
+    finish(0, names[1:2], local_grad, after)
+    finish(0, names[2:], over_tp, after)
     pieces = [scatter_pairs(reduced(0, some)) for some in (names[:1], names[1:2], names[2:])]
     mine = [jnp.concatenate(pieces, axis=0)] + [
         after(jnp.concatenate(along[l], axis=0), local_grad) for l in range(1, layers)

time: 739 us -> 741 us (level)
  waiting for transfers between devices: 206 us -> 193 us
  starting transfers between devices: 101 us -> 113 us
    ppermute x22, starting transfers between devices: 33.5 us -> 47.6 us  [tp_partner(): lax.ppermute(values, 'tp', [(j, j ^ bit) for j in range(lax.axis_size('tp...]
    ppermute x30, waiting for transfers between devices: 23 us -> 9.94 us  [send_x(): return lax.ppermute(values, 'fsdp', X_PAIRS)]
    unnamed x362 -> x368, local copies, waits for them, and re-layouts: 34.4 us -> 37 us
  transfers between devices with their start and end apart: 99 -> 99, of which waited for: 33 -> 32; matrix products, arithmetic and copies ran while one was open for 39% -> 39% of each run, Pallas kernels for 6% -> 6%
where the time goes in v6:
time: 741 us; the launch traced here: 735 us
  waiting for transfers between devices  193 us (26%)
  matrix products  127 us (17%)
  local copies, waits for them, and re-layouts  119 us (16%)
  starting transfers between devices  113 us (15%)
  other arithmetic  102 us (14%)
  Pallas kernels  45.8 us (6%)
  between operations  35.9 us (5%)
    ppermute x31, waiting for transfers between devices, send_y(): return lax.ppermute(values, 'fsdp', Y_PAIRS)  92.9 us
    ppermute x22, waiting for transfers between devices, tp_partner(): lax.ppermute(values, 'tp', [(j, j ^ bit) for j in range(lax.axis_size('tp...  88.8 us
    dot_general x24, matrix products, mm_tn(): lax.dot_general(left, right, (((0,), (0,)), ((), ())), preferred_element_...  50.9 us
    ppermute x22, starting transfers between devices, tp_partner(): lax.ppermute(values, 'tp', [(j, j ^ bit) for j in range(lax.axis_size('tp...  47.6 us
    dot_general x14, matrix products, mm(): return jnp.dot(left, right, preferred_element_type=F32)  42.4 us
    unnamed x368, local copies, waits for them, and re-layouts  37 us
    ppermute x30, starting transfers between devices, send_x(): return lax.ppermute(values, 'fsdp', X_PAIRS)  32.9 us
    ppermute x31, starting transfers between devices, send_y(): return lax.ppermute(values, 'fsdp', Y_PAIRS)  31.3 us
  transfers between devices with their start and end apart: 99, of which 32 were waited for; matrix products, arithmetic and copies ran while one was open for 39% of the time, Pallas kernels for 6%

profile of v6, /device:TPU:0, one launch (start us, length us, event | category | flops | bytes accessed | tf_op | source)
XLA Modules:
  0.0 734.7 jit_solution(12390397915772788523)
XLA Ops:
  41.4 7.8 %collective-permute-done.5 = bf16[2,384,256]{2,1,0:T(8,128)(2,1)S(1)} collective-permute-done((bf16[2,384,256]{2,1,0:T(8,128)(2,1)S(1)}, bf16[2,384,256]{2,1,0:T(8,128)(2,1)S(1)}, u32[]{:S(2)}, u32[]{:S(2)}) %collective-permute-start.5) | collective-permute-done | bytes 393248 | tf_op jit(solution)/shard_map/ppermute | solution.py:79
  104.8 9.1 %collective-permute-done.16 = bf16[512,256]{1,0:T(8,128)(2,1)S(1)} collective-permute-done((bf16[512,256]{1,0:T(8,128)(2,1)S(1)}, bf16[512,256]{1,0:T(8,128)(2,1)S(1)}, u32[]{:S(2)}, u32[]{:S(2)}) %collective-permute-start.16) | collective-permute-done | bytes 262176 | tf_op jit(solution)/shard_map/ppermute | solution.py:79
  114.4 10.7 %collective-permute-done.17 = bf16[2,512,256]{2,1,0:T(8,128)(2,1)S(1)} collective-permute-done((bf16[2,512,256]{2,1,0:T(8,128)(2,1)S(1)}, bf16[2,512,256]{2,1,0:T(8,128)(2,1)S(1)}, u32[]{:S(2)}, u32[]{:S(2)}) %collective-permute-start.17) | collective-permute-done | bytes 524320 | tf_op jit(solution)/shard_map/ppermute | solution.py:79
  130.1 7.6 %collective-permute-done.20 = bf16[512,256]{1,0:T(8,128)(2,1)S(1)} collective-permute-done((bf16[512,256]{1,0:T(8,128)(2,1)S(1)}, bf16[512,256]{1,0:T(8,128)(2,1)S(1)}, u32[]{:S(2)}, u32[]{:S(2)}) %collective-permute-start.20) | collective-permute-done | bytes 262176 | tf_op jit(solution)/shard_map/ppermute | solution.py:79
  154.5 7.7 %shard_map.229 = (bf16[592,512]{1,0:T(8,128)(2,1)S(1)}, f32[4,592,2]{2,1,0:T(8,128)S(1)}) custom-call(bf16[592,1536]{1,0:T(8,128)(2,1)S(1)} %get-tuple-element.291.project_ref), custom_call_target="tpu_custom_call" | custom-call | flops 2871001088 | bytes 2424832 | tf_op jit(solution)/shard_map/pallas_call | solution.py:218
  165.4 14.5 %collective-permute-done.22 = bf16[2560,128]{1,0:T(8,128)(2,1)S(1)} collective-permute-done((bf16[2560,128]{1,0:T(8,128)(2,1)S(1)}, bf16[2560,128]{1,0:T(8,128)(2,1)S(1)}, u32[]{:S(2)}, u32[]{:S(2)}) %collective-permute-start.22) | collective-permute-done | bytes 655392 | tf_op jit(solution)/shard_map/ppermute | solution.py:48
  190.3 27.4 %collective-permute-done.25 = bf16[2048,128]{1,0:T(8,128)(2,1)S(1)} collective-permute-done((bf16[2048,128]{1,0:T(8,128)(2,1)S(1)}, bf16[2048,128]{1,0:T(8,128)(2,1)S(1)}, u32[]{:S(2)}, u32[]{:S(2)}) %collective-permute-start.25) | collective-permute-done | bytes 524320 | tf_op jit(solution)/shard_map/ppermute | solution.py:48
  233.0 4.9 multiply_convert_fusion.1
  240.8 14.3 %collective-permute-done.30 = bf16[2048,128]{1,0:T(8,128)(2,1)S(1)} collective-permute-done((bf16[2048,128]{1,0:T(8,128)(2,1)S(1)}, bf16[2048,128]{1,0:T(8,128)(2,1)S(1)}, u32[]{:S(2)}, u32[]{:S(2)}) %collective-permute-start.30) | collective-permute-done | bytes 524320 | tf_op jit(solution)/shard_map/ppermute | solution.py:48
  256.1 8.1 %collective-permute-done.37 = bf16[2,512,256]{2,1,0:T(8,128)(2,1)S(1)} collective-permute-done((bf16[2,512,256]{2,1,0:T(8,128)(2,1)S(1)}, bf16[2,512,256]{2,1,0:T(8,128)(2,1)S(1)}, u32[]{:S(2)}, u32[]{:S(2)}) %collective-permute-start.37) | collective-permute-done | bytes 524320 | tf_op jit(solution)/shard_map/ppermute | solution.py:79
  278.4 8.2 %shard_map.230 = (bf16[592,512]{1,0:T(8,128)(2,1)S(1)}, f32[4,592,2]{2,1,0:T(8,128)S(1)}) custom-call(bf16[592,1536]{1,0:T(8,128)(2,1)S(1)} %get-tuple-element.297.project_ref), custom_call_target="tpu_custom_call" | custom-call | flops 2871001088 | bytes 2424832 | tf_op jit(solution)/shard_map/pallas_call | solution.py:218
  286.6 15.9 %collective-permute-done.41 = bf16[2048,128]{1,0:T(8,128)(2,1)S(1)} collective-permute-done((bf16[2048,128]{1,0:T(8,128)(2,1)S(1)}, bf16[2048,128]{1,0:T(8,128)(2,1)S(1)}, u32[]{:S(2)}, u32[]{:S(2)}) %collective-permute-start.41) | collective-permute-done | bytes 524320 | tf_op jit(solution)/shard_map/ppermute | solution.py:48
  316.4 4.8 multiply_convert_fusion
  328.1 4.2 fusion.19
  332.3 5.5 convolution_convert_fusion.28
  340.3 7.4 %add_convert_fusion.1 = bf16[592,2048]{1,0:T(8,128)(2,1)S(1)} fusion(f32[592,2048]{1,0:T(8,128)} %get-tuple-element.300, f32[2048]{0:T(1024)S(1)} %bitcast.564, bf16[592,1024]{1,0:T(8,128)(2,1)S(1)} %get-tuple-element.140, bf16[2048,1024]{1,0:T(8,128)(2,1)} %copy-done.76), kind=kOutput, calls=%fused_computation.3 | convolution fusion | flops 2500001792 | bytes 12689408 | tf_op jit(solution)/shard_map/dot_general | solution.py:161
  366.4 5.1 convolution_convert_fusion.6
  383.7 15.0 %shard_map.231 = bf16[592,1536]{1,0:T(8,128)(2,1)S(1)} custom-call(bf16[592,1536]{1,0:T(8,128)(2,1)S(1)} %copy-done.5, bf16[592,512]{1,0:T(8,128)(2,1)S(1)} %add_add_fusion.19.mixed_ref, f32[4,592,2]{2,1,0:T(8,128)S(1)} %get-tuple-element.49.total_ref, bf16[592,512]{1,0:T(8,128)(2,1)S(1)} %convolution_convert_fusion.30.delta_ref), custom_call_target="tpu_custom_call" | custom-call | flops 7177502720 | bytes 4546560 | tf_op jit(solution)/shard_map/pallas_call | solution.py:236
  398.7 6.9 collective-permute-done.48
  439.8 5.2 add_convert_fusion
  454.4 3.9 collective-permute-done.64
  476.7 3.9 convolution_convert_fusion.7
  503.8 14.9 %shard_map.232 = bf16[592,1536]{1,0:T(8,128)(2,1)S(1)} custom-call(bf16[592,1536]{1,0:T(8,128)(2,1)S(1)} %copy-done.4, bf16[592,512]{1,0:T(8,128)(2,1)S(1)} %copy-done.1, f32[4,592,2]{2,1,0:T(8,128)S(1)} %copy-done.3, bf16[592,512]{1,0:T(8,128)(2,1)S(1)} %convolution_convert_fusion.29.delta_ref), custom_call_target="tpu_custom_call" | custom-call | flops 7177502720 | bytes 4546560 | tf_op jit(solution)/shard_map/pallas_call | solution.py:236
  555.1 5.1 convolution_convert_fusion.25
  579.0 5.4 convolution_convert_fusion.27
  600.7 5.3 collective-permute-start.81
  610.0 10.0 %collective-permute-done.81 = f32[160,128]{1,0:T(8,128)} collective-permute-done((f32[160,128]{1,0:T(8,128)}, f32[160,128]{1,0:T(8,128)}, u32[]{:S(2)}, u32[]{:S(2)}) %collective-permute-start.81) | collective-permute-done | bytes 81952 | tf_op jit(solution)/shard_map/ppermute | solution.py:79
  621.6 8.7 %collective-permute-start.82 = (f32[160,128]{1,0:T(8,128)}, f32[160,128]{1,0:T(8,128)}, u32[]{:S(2)}, u32[]{:S(2)}) collective-permute-start(f32[160,128]{1,0:T(8,128)} %fusion.181), channel_id=1, source_target_pairs={{0,1},{1,0},{2,3},{3,2},{4,5},{5,4},{6,7},{7,6},{8,9},{9,8},{10,11... | collective-permute-start | bytes 245768 | tf_op jit(solution)/shard_map/ppermute | solution.py:79
  636.1 4.2 collective-permute-done.82
  661.8 13.5 %collective-permute-start.75 = (bf16[512,256]{0,1:T(8,128)(2,1)}, bf16[512,256]{0,1:T(8,128)(2,1)}, u32[]{:S(2)}, u32[]{:S(2)}) collective-permute-start(bf16[512,256]{0,1:T(8,128)(2,1)} %dynamic-slice_bitcast_fusion.4), channel_id=1, source_target_pairs={{0,2},{1,3},{2,0},{3,1},{4,6},{5,7},{6,4},{7,5},{8,10},{9,11},{10,... | collective-permute-start | bytes 786440 | tf_op jit(solution)/shard_map/ppermute | solution.py:79
  680.3 13.7 %collective-permute-done.75 = bf16[512,256]{0,1:T(8,128)(2,1)} collective-permute-done((bf16[512,256]{0,1:T(8,128)(2,1)}, bf16[512,256]{0,1:T(8,128)(2,1)}, u32[]{:S(2)}, u32[]{:S(2)}) %collective-permute-start.75) | collective-permute-done | bytes 262176 | tf_op jit(solution)/shard_map/ppermute | solution.py:79
  700.7 9.4 %collective-permute-done.89 = bf16[512,256]{0,1:T(8,128)(2,1)S(1)} collective-permute-done((bf16[512,256]{0,1:T(8,128)(2,1)S(1)}, bf16[512,256]{0,1:T(8,128)(2,1)S(1)}, u32[]{:S(2)}, u32[]{:S(2)}) %collective-permute-start.89) | collective-permute-done | bytes 262176 | tf_op jit(solution)/shard_map/ppermute | solution.py:79
  (924 shorter events, 410.5 us)
Async XLA Ops:
  7.2 545.0 %all-gather.5.cloned.1.call-start = ((), (), s32[]{:S(2)}) async-start(), calls=%async_computation.4 | async-start | bytes 3276800 | tf_op jit(solution)/shard_map/all_gather | solution.py:415
  23.2 59.4 %collective-permute-start = (bf16[320,2048]{1,0:T(8,128)(2,1)}, bf16[320,2048]{1,0:T(8,128)(2,1)}, u32[]{:S(2)}, u32[]{:S(2)}) collective-permute-start(bf16[320,2048]{1,0:T(8,128)(2,1)} %pad_maximum_fusion.1), channel_id=1, source_target_pairs={{0,4},{4,0},{1,5},{5,1},{2,6},{6,2},{3,7},{7,3},{8,12},{12,8},{9,1... | collective-permute-start | bytes 3932168 | tf_op jit(solution)/shard_map/ppermute | solution.py:63
  49.4 39.5 %collective-permute-start.6 = (bf16[1536,256]{1,0:T(8,128)(2,1)S(1)}, bf16[1536,256]{1,0:T(8,128)(2,1)}, u32[]{:S(2)}, u32[]{:S(2)}) collective-permute-start(bf16[1536,256]{1,0:T(8,128)(2,1)S(1)} %bitcast.436), channel_id=1, source_target_pairs={{0,8},{8,0},{16,24},{24,16},{1,9},{9,1},{17,25},{25,17},{2,10},{10... | collective-permute-start | bytes 2359304 | tf_op jit(solution)/shard_map/ppermute | solution.py:44
  50.0 41.9 %collective-permute-start.7 = (bf16[1536,256]{1,0:T(8,128)(2,1)S(1)}, bf16[1536,256]{1,0:T(8,128)(2,1)}, u32[]{:S(2)}, u32[]{:S(2)}) collective-permute-start(bf16[1536,256]{1,0:T(8,128)(2,1)S(1)} %bitcast.437), channel_id=1, source_target_pairs={{0,16},{16,0},{8,24},{24,8},{1,17},{17,1},{9,25},{25,9},{2,18},{18... | collective-permute-start | bytes 2359304 | tf_op jit(solution)/shard_map/ppermute | solution.py:48
  100.5 37.4 %collective-permute-start.14 = (bf16[2560,256]{1,0:T(8,128)(2,1)S(1)}, bf16[2560,256]{1,0:T(8,128)(2,1)S(1)}, u32[]{:S(2)}, u32[]{:S(2)}) collective-permute-start(bf16[2560,256]{1,0:T(8,128)(2,1)S(1)} %bitcast.478), channel_id=1, source_target_pairs={{0,8},{8,0},{16,24},{24,16},{1,9},{9,1},{17,25},{25,17},{2,10},{10... | collective-permute-start | bytes 3932168 | tf_op jit(solution)/shard_map/ppermute | solution.py:44
  101.1 38.0 %collective-permute-start.15 = (bf16[2560,256]{1,0:T(8,128)(2,1)S(1)}, bf16[2560,256]{1,0:T(8,128)(2,1)S(1)}, u32[]{:S(2)}, u32[]{:S(2)}) collective-permute-start(bf16[2560,256]{1,0:T(8,128)(2,1)S(1)} %bitcast.479), channel_id=1, source_target_pairs={{0,16},{16,0},{8,24},{24,8},{1,17},{17,1},{9,25},{25,9},{2,18},{18... | collective-permute-start | bytes 3932168 | tf_op jit(solution)/shard_map/ppermute | solution.py:48
  140.7 40.1 %collective-permute-start.18 = (bf16[2048,256]{1,0:T(8,128)(2,1)S(1)}, bf16[2048,256]{1,0:T(8,128)(2,1)S(1)}, u32[]{:S(2)}, u32[]{:S(2)}) collective-permute-start(bf16[2048,256]{1,0:T(8,128)(2,1)S(1)} %get-tuple-element.296), channel_id=1, source_target_pairs={{0,8},{8,0},{16,24},{24,16},{1,9},{9,1},{17,25},{25,17},{2,10},{10... | collective-permute-start | bytes 3145736 | tf_op jit(solution)/shard_map/ppermute | solution.py:44
  142.3 39.9 %collective-permute-start.19 = (bf16[2048,256]{1,0:T(8,128)(2,1)S(1)}, bf16[2048,256]{1,0:T(8,128)(2,1)S(1)}, u32[]{:S(2)}, u32[]{:S(2)}) collective-permute-start(bf16[2048,256]{1,0:T(8,128)(2,1)S(1)} %get-tuple-element.296), channel_id=1, source_target_pairs={{0,16},{16,0},{8,24},{24,8},{1,17},{17,1},{9,25},{25,9},{2,18},{18... | collective-permute-start | bytes 3145736 | tf_op jit(solution)/shard_map/ppermute | solution.py:48
  142.6 37.3 %collective-permute-start.22 = (bf16[2560,128]{1,0:T(8,128)(2,1)S(1)}, bf16[2560,128]{1,0:T(8,128)(2,1)S(1)}, u32[]{:S(2)}, u32[]{:S(2)}) collective-permute-start(bf16[2560,128]{1,0:T(8,128)(2,1)S(1)} %get-tuple-element.185), channel_id=1, source_target_pairs={{0,16},{16,0},{8,24},{24,8},{1,17},{17,1},{9,25},{25,9},{2,18},{18... | collective-permute-start | bytes 1966088 | tf_op jit(solution)/shard_map/ppermute | solution.py:48
  190.0 37.7 %collective-permute-start.24 = (bf16[592,1024]{1,0:T(8,128)(2,1)S(1)}, bf16[592,1024]{1,0:T(8,128)(2,1)S(1)}, u32[]{:S(2)}, u32[]{:S(2)}) collective-permute-start(bf16[592,1024]{1,0:T(8,128)(2,1)S(1)} %convolution_convert_fusion.24), channel_id=1, source_target_pairs={{0,4},{4,0},{1,5},{5,1},{2,6},{6,2},{3,7},{7,3},{8,12},{12,8},{9,1... | collective-permute-start | bytes 3637256 | tf_op jit(solution)/shard_map/ppermute | solution.py:63
  221.1 44.6 %collective-permute-start.34 = (bf16[2048,256]{1,0:T(8,128)(2,1)S(1)}, bf16[2048,256]{1,0:T(8,128)(2,1)S(1)}, u32[]{:S(2)}, u32[]{:S(2)}) collective-permute-start(bf16[2048,256]{1,0:T(8,128)(2,1)S(1)} %bitcast.423), channel_id=1, source_target_pairs={{0,8},{8,0},{16,24},{24,16},{1,9},{9,1},{17,25},{25,17},{2,10},{10... | collective-permute-start | bytes 3145736 | tf_op jit(solution)/shard_map/ppermute | solution.py:44
  222.6 44.2 %collective-permute-start.35 = (bf16[2048,256]{1,0:T(8,128)(2,1)S(1)}, bf16[2048,256]{1,0:T(8,128)(2,1)S(1)}, u32[]{:S(2)}, u32[]{:S(2)}) collective-permute-start(bf16[2048,256]{1,0:T(8,128)(2,1)S(1)} %bitcast.424), channel_id=1, source_target_pairs={{0,16},{16,0},{8,24},{24,8},{1,17},{17,1},{9,25},{25,9},{2,18},{18... | collective-permute-start | bytes 3145736 | tf_op jit(solution)/shard_map/ppermute | solution.py:48
  357.2 41.5 %collective-permute-start.50 = (bf16[2048,256]{1,0:T(8,128)(2,1)}, bf16[2048,256]{1,0:T(8,128)(2,1)}, u32[]{:S(2)}, u32[]{:S(2)}) collective-permute-start(bf16[2048,256]{1,0:T(8,128)(2,1)} %convolution_convert_fusion.11), channel_id=1, source_target_pairs={{0,16},{16,0},{8,24},{24,8},{1,17},{17,1},{9,25},{25,9},{2,18},{18... | collective-permute-start | bytes 3145736 | tf_op jit(solution)/shard_map/ppermute | solution.py:48
  358.5 40.2 %collective-permute-start.49 = (bf16[2048,256]{1,0:T(8,128)(2,1)}, bf16[2048,256]{1,0:T(8,128)(2,1)}, u32[]{:S(2)}, u32[]{:S(2)}) collective-permute-start(bf16[2048,256]{1,0:T(8,128)(2,1)} %convolution_convert_fusion.12), channel_id=1, source_target_pairs={{0,8},{8,0},{16,24},{24,16},{1,9},{9,1},{17,25},{25,17},{2,10},{10... | collective-permute-start | bytes 3145736 | tf_op jit(solution)/shard_map/ppermute | solution.py:44
  360.0 45.6 %collective-permute-start.48 = (bf16[2048,256]{1,0:T(8,128)(2,1)}, bf16[2048,256]{1,0:T(8,128)(2,1)}, u32[]{:S(2)}, u32[]{:S(2)}) collective-permute-start(bf16[2048,256]{1,0:T(8,128)(2,1)} %convolution_convert_fusion.13), channel_id=1, source_target_pairs={{0,16},{16,0},{8,24},{24,8},{1,17},{17,1},{9,25},{25,9},{2,18},{18... | collective-permute-start | bytes 3145736 | tf_op jit(solution)/shard_map/ppermute | solution.py:48
  362.9 43.7 %collective-permute-start.47 = (bf16[2048,256]{1,0:T(8,128)(2,1)}, bf16[2048,256]{1,0:T(8,128)(2,1)}, u32[]{:S(2)}, u32[]{:S(2)}) collective-permute-start(bf16[2048,256]{1,0:T(8,128)(2,1)} %convolution_convert_fusion.14), channel_id=1, source_target_pairs={{0,8},{8,0},{16,24},{24,16},{1,9},{9,1},{17,25},{25,17},{2,10},{10... | collective-permute-start | bytes 3145736 | tf_op jit(solution)/shard_map/ppermute | solution.py:44
  363.4 191.7 %reduce-scatter.3.cloned.1.call-start = ((), (), s32[]{:S(2)}) async-start(), calls=%async_computation.2 | async-start | bytes 2621440 | tf_op jit(solution)/shard_map/reduce_scatter | solution.py:438
  449.8 69.0 %collective-permute-start.58 = (bf16[2048,256]{1,0:T(8,128)(2,1)}, bf16[2048,256]{1,0:T(8,128)(2,1)}, u32[]{:S(2)}, u32[]{:S(2)}) collective-permute-start(bf16[2048,256]{1,0:T(8,128)(2,1)} %convolution_convert_fusion.9), channel_id=1, source_target_pairs={{0,16},{16,0},{8,24},{24,8},{1,17},{17,1},{9,25},{25,9},{2,18},{18... | collective-permute-start | bytes 3145736 | tf_op jit(solution)/shard_map/ppermute | solution.py:48
  461.9 58.4 %collective-permute-start.57 = (bf16[2048,256]{1,0:T(8,128)(2,1)}, bf16[2048,256]{1,0:T(8,128)(2,1)}, u32[]{:S(2)}, u32[]{:S(2)}) collective-permute-start(bf16[2048,256]{1,0:T(8,128)(2,1)} %convolution_convert_fusion.10), channel_id=1, source_target_pairs={{0,8},{8,0},{16,24},{24,16},{1,9},{9,1},{17,25},{25,17},{2,10},{10... | collective-permute-start | bytes 3145736 | tf_op jit(solution)/shard_map/ppermute | solution.py:44
  469.6 51.9 %collective-permute-start.70 = (bf16[1536,128]{1,0:T(8,128)(2,1)}, bf16[1536,128]{1,0:T(8,128)(2,1)}, u32[]{:S(2)}, u32[]{:S(2)}) collective-permute-start(bf16[1536,128]{1,0:T(8,128)(2,1)} %get-tuple-element.182), channel_id=1, source_target_pairs={{0,8},{8,0},{16,24},{24,16},{1,9},{9,1},{17,25},{25,17},{2,10},{10... | collective-permute-start | bytes 1179656 | tf_op jit(solution)/shard_map/ppermute | solution.py:44
  480.6 52.8 %collective-permute-start.60 = (bf16[2048,256]{1,0:T(8,128)(2,1)}, bf16[2048,256]{1,0:T(8,128)(2,1)}, u32[]{:S(2)}, u32[]{:S(2)}) collective-permute-start(bf16[2048,256]{1,0:T(8,128)(2,1)} %convolution_convert_fusion.7), channel_id=1, source_target_pairs={{0,16},{16,0},{8,24},{24,8},{1,17},{17,1},{9,25},{25,9},{2,18},{18... | collective-permute-start | bytes 3145736 | tf_op jit(solution)/shard_map/ppermute | solution.py:48
  484.8 106.2 %reduce-scatter.5.cloned.1.call-start = ((), (), s32[]{:S(2)}) async-start(), calls=%async_computation.3 | async-start | bytes 1310720 | tf_op jit(solution)/shard_map/reduce_scatter | solution.py:438
  493.1 42.1 %collective-permute-start.59 = (bf16[2048,256]{1,0:T(8,128)(2,1)S(1)}, bf16[2048,256]{1,0:T(8,128)(2,1)S(1)}, u32[]{:S(2)}, u32[]{:S(2)}) collective-permute-start(bf16[2048,256]{1,0:T(8,128)(2,1)S(1)} %convolution_convert_fusion.8), channel_id=1, source_target_pairs={{0,8},{8,0},{16,24},{24,16},{1,9},{9,1},{17,25},{25,17},{2,10},{10... | collective-permute-start | bytes 3145736 | tf_op jit(solution)/shard_map/ppermute | solution.py:44
  527.9 46.9 %collective-permute-start.73 = (bf16[2048,128]{1,0:T(8,128)(2,1)}, bf16[2048,128]{1,0:T(8,128)(2,1)}, u32[]{:S(2)}, u32[]{:S(2)}) collective-permute-start(bf16[2048,128]{1,0:T(8,128)(2,1)} %get-tuple-element.158), channel_id=1, source_target_pairs={{0,8},{8,0},{16,24},{24,16},{1,9},{9,1},{17,25},{25,17},{2,10},{10... | collective-permute-start | bytes 1572872 | tf_op jit(solution)/shard_map/ppermute | solution.py:44
  533.4 42.9 %collective-permute-start.72 = (bf16[2048,128]{1,0:T(8,128)(2,1)}, bf16[2048,128]{1,0:T(8,128)(2,1)}, u32[]{:S(2)}, u32[]{:S(2)}) collective-permute-start(bf16[2048,128]{1,0:T(8,128)(2,1)} %get-tuple-element.157), channel_id=1, source_target_pairs={{0,16},{16,0},{8,24},{24,8},{1,17},{17,1},{9,25},{25,9},{2,18},{18... | collective-permute-start | bytes 1572872 | tf_op jit(solution)/shard_map/ppermute | solution.py:48
  537.7 63.0 %collective-permute-start.76 = (bf16[2048,128]{1,0:T(8,128)(2,1)}, bf16[2048,128]{1,0:T(8,128)(2,1)}, u32[]{:S(2)}, u32[]{:S(2)}) collective-permute-start(bf16[2048,128]{1,0:T(8,128)(2,1)} %get-tuple-element.161), channel_id=1, source_target_pairs={{0,16},{16,0},{8,24},{24,8},{1,17},{17,1},{9,25},{25,9},{2,18},{18... | collective-permute-start | bytes 1572872 | tf_op jit(solution)/shard_map/ppermute | solution.py:48
  546.7 178.3 %all-gather.7.cloned.1.call-start = ((), (), s32[]{:S(2)}) async-start(), calls=%async_computation.5 | async-start | bytes 3276800 | tf_op jit(solution)/shard_map/all_gather | solution.py:415
  548.4 57.6 %collective-permute-start.77 = (bf16[2048,128]{1,0:T(8,128)(2,1)}, bf16[2048,128]{1,0:T(8,128)(2,1)}, u32[]{:S(2)}, u32[]{:S(2)}) collective-permute-start(bf16[2048,128]{1,0:T(8,128)(2,1)} %get-tuple-element.162), channel_id=1, source_target_pairs={{0,8},{8,0},{16,24},{24,16},{1,9},{9,1},{17,25},{25,17},{2,10},{10... | collective-permute-start | bytes 1572872 | tf_op jit(solution)/shard_map/ppermute | solution.py:44
  568.8 73.8 %collective-permute-start.80 = (bf16[512,128]{1,0:T(8,128)(2,1)}, bf16[512,128]{1,0:T(8,128)(2,1)}, u32[]{:S(2)}, u32[]{:S(2)}) collective-permute-start(bf16[512,128]{1,0:T(8,128)(2,1)} %get-tuple-element.245), channel_id=1, source_target_pairs={{0,16},{16,0},{8,24},{24,8},{1,17},{17,1},{9,25},{25,9},{2,18},{18... | collective-permute-start | bytes 393224 | tf_op jit(solution)/shard_map/ppermute | solution.py:48
  595.1 47.7 %collective-permute-start.83 = (bf16[512,128]{1,0:T(8,128)(2,1)}, bf16[512,128]{1,0:T(8,128)(2,1)}, u32[]{:S(2)}, u32[]{:S(2)}) collective-permute-start(bf16[512,128]{1,0:T(8,128)(2,1)} %get-tuple-element.246), channel_id=1, source_target_pairs={{0,8},{8,0},{16,24},{24,16},{1,9},{9,1},{17,25},{25,17},{2,10},{10... | collective-permute-start | bytes 393224 | tf_op jit(solution)/shard_map/ppermute | solution.py:44
  597.4 62.4 %collective-permute-start.74 = (bf16[2,512,256]{1,2,0:T(8,128)(2,1)}, bf16[2,512,256]{1,2,0:T(8,128)(2,1)}, u32[]{:S(2)}, u32[]{:S(2)}) collective-permute-start(bf16[2,512,256]{1,2,0:T(8,128)(2,1)} %bitcast.164), channel_id=1, source_target_pairs={{0,1},{1,0},{2,3},{3,2},{4,5},{5,4},{6,7},{7,6},{8,9},{9,8},{10,11... | collective-permute-start | bytes 1572872 | tf_op jit(solution)/shard_map/ppermute | solution.py:79
  653.7 41.5 %collective-permute-start.88 = (bf16[2,512,256]{1,2,0:T(8,128)(2,1)}, bf16[2,512,256]{1,2,0:T(8,128)(2,1)}, u32[]{:S(2)}, u32[]{:S(2)}) collective-permute-start(bf16[2,512,256]{1,2,0:T(8,128)(2,1)} %fusion.58), channel_id=1, source_target_pairs={{0,1},{1,0},{2,3},{3,2},{4,5},{5,4},{6,7},{7,6},{8,9},{9,8},{10,11... | collective-permute-start | bytes 1572872 | tf_op jit(solution)/shard_map/ppermute | solution.py:79
  (222 other events, 2559.7 us)
Sparse Core Ops, SparseCore 0:
  363.5 57.2 all-gather.4
  484.9 46.2 reduce-scatter.2
  546.8 29.8 reduce-scatter.4
  591.1 78.9 all-gather.6
